TPU v7x, 512 devices: a whole 4x4x16 slice. The times are simulated.
512 devices in a mesh: wide: 64 (over y_hi, z, core), narrow: 8 (over y_lo, x).
Axes of the slice: x: 4, y: 4 (y_hi: 2, y_lo: 2; y = y_hi * 2 + y_lo), z: 16, core: 2. Of those that a mesh axis runs over, the one named last changes fastest.
Arguments:
- descriptors: bfloat16 [1536, 2000], P('narrow'), may hold values from -6 to 6
- env_weights: bfloat16 [1536], P('narrow'), may hold values from 0.19921875 to 5
- sparse_points: bfloat16 [12288, 2000], P(('wide', 'narrow')), may hold values from -6 to 6
Outputs:
- normal: float32 [64, 33, 192, 192], P('wide', None, 'narrow')
All inputs are finite; a program needn't handle non-finite values.
Results may differ from a plain program's by a relative error of at most 0.0003.
Values may be sent and summed in bfloat16 or wider, within the bound.
No kernel may reach another device: no remote copies, remote signals or barrier semaphores. Data moves between devices by JAX's collectives and lax.ppermute only.
A program may use at most 64 MiB of HBM per device.

v0:
```python
import jax
import jax.numpy as jnp
from jax import lax
from jax.sharding import PartitionSpec as P


def from_behind(value, axis, by):
    length = lax.axis_size(axis)
    return lax.ppermute(value, axis, [(i, (i + by) % length) for i in range(length)])


def kernel_rows(points, gathered):
    products = lax.dot_general(
        points, gathered, (((1,), (1,)), ((), ())), preferred_element_type=jnp.float32
    )
    return products * products / gathered.shape[1]


def pair_blocks(columns, weighted):
    return lax.dot_general(
        columns,
        weighted,
        (((1,), (1,)), ((), ())),
        precision=lax.Precision.HIGHEST,
        preferred_element_type=jnp.float32,
    )


def step_loop(payload, block_terms, advance, totals, quarter):

    def turn_once(counter, status):
        rows, totals = status
        nearer = advance(rows)
        farther = advance(nearer)
        fresh_blocks = block_terms(jnp.concatenate([nearer, farther], axis=0))
        totals = lax.dynamic_update_slice_in_dim(totals, fresh_blocks, 2 * counter + 1, 0)
        return (farther, totals)

    _, totals = lax.fori_loop(0, quarter, turn_once, (payload, totals))
    return totals


def shards(descriptors, env_weights, sparse_points):
    gathered, all_weights = (
        lax.all_gather(descriptors, "narrow", axis=0, tiled=True),
        lax.all_gather(env_weights, "narrow", axis=0, tiled=True),
    )
    env_count = gathered.shape[0]
    piece_rows = sparse_points.shape[0]
    weighting = all_weights.astype(jnp.float32) / env_count
    local_kernel = kernel_rows(sparse_points, gathered)
    columns = lax.all_gather(local_kernel, "narrow", axis=0, tiled=True)
    weighted = columns * weighting[None, :]
    block_size = weighted.shape[0]
    axis_size = lax.axis_size("wide")
    half_axis = axis_size // 2
    quarter = half_axis // 2

    def terms_from_points(rows):
        return pair_blocks(kernel_rows(rows, gathered), weighted).reshape(
            -1, piece_rows, block_size
        )

    totals = jnp.zeros((half_axis + 1, piece_rows, block_size), jnp.float32)
    totals = totals.at[0].set(pair_blocks(local_kernel, weighted))
    totals = step_loop(
        sparse_points,
        terms_from_points,
        lambda rows: from_behind(rows, "wide", -1),
        totals,
        quarter,
    )
    return totals[None]


def solution(mesh):
    in_specs = (P("narrow", None), P("narrow"), P(("wide", "narrow"), None))
    out_specs = P("wide", None, "narrow", None)
    return jax.shard_map(shards, mesh=mesh, in_specs=in_specs, out_specs=out_specs, check_vma=False)
```

profile of v0, /device:TPU:1, one launch (start us, length us, event | category | flops | bytes accessed | tf_op | source)
XLA Modules:
  0.0 547.4 jit_solution(4962639259254469221)
XLA Ops:
  7.5 87.2 %all-gather.3.cloned.1.call-done = bf16[1536,2000]{1,0:T(8,128)(2,1)} async-done(((bf16[192,2000]{1,0:T(8,128)(2,1)}), bf16[1536,2000]{1,0:T(8,128)(2,1)}) %all-gather.3.cloned.1.call-update) | async-done | bytes 6144016 | tf_op jit(solution)/shard_map/all_gather | solution.py:45
  94.7 5.2 fusion.5
  102.1 13.0 %all-reduce.1 = bf16[1536]{0:T(1024)(128)(2,1)S(1)} all-reduce(bf16[1536]{0:T(1024)(128)(2,1)S(1)} %dynamic-update-slice.3), channel_id=1, replica_groups=mesh['wide'=64,'narrow'=8] {'narrow'}, use_global_device_ids=true, to_apply=%add.1 | all-reduce | flops 1536 | bytes 6144
  115.1 25.6 %all-gather.5.cloned.1.call-done = f32[192,1536]{1,0:T(8,128)} async-done(((f32[24,1536]{1,0:T(8,128)}), f32[192,1536]{1,0:T(8,128)}) %all-gather.5.cloned.1.call-update) | async-done | bytes 1179664 | tf_op jit(solution)/shard_map/all_gather | solution.py:52
  143.2 396.5 %while.18 = (s32[]{:T(128)}, bf16[24,2000]{1,0:T(8,128)(2,1)S(1)}, f32[33,24,192]{2,1,0:T(8,128)S(1)}, bf16[1536,2000]{1,0:T(8,128)(2,1)}, f32[192,1536]{1,0:T(8...) while((s32[]{:T(128)}, bf16[24,2000]{1,0:T(8,128)(2,1)S(1)}, f32[33,24,192]{2,1,0:T(8,128)S(1)}, ...), condition=%wide.region_1.0_spmd, body=%wide.region_0.0_spmd.sunk | while | flops 465312768 | bytes 9008875 | solution.py:39
  143.2 7.8 %collective-permute-start = (bf16[24,2000]{1,0:T(8,128)(2,1)S(1)}, bf16[24,2000]{1,0:T(8,128)(2,1)S(1)}, u32[]{:S(2)}, u32[]{:S(2)}) collective-permute-start(bf16[24,2000]{1,0:T(8,128)(2,1)S(1)} %get-tuple-element.201), channel_id=1, source_target_pairs={{0,504},{8,0},{16,8},{24,16},{32,24},{40,32},{48,40},{56,48},{64,5... | collective-permute-start | bytes 288008 | tf_op jit(solution)/shard_map/while/body/eval_jaxpr/ppermute | solution.py:9
  160.2 4.8 fusion.24
  166.3 5.2 collective-permute-start
  172.3 8.6 %collective-permute-start.1 = (bf16[24,2000]{1,0:T(8,128)(2,1)S(1)}, bf16[24,2000]{1,0:T(8,128)(2,1)S(1)}, u32[]{:S(2)}, u32[]{:S(2)}) collective-permute-start(bf16[24,2000]{1,0:T(8,128)(2,1)S(1)} %collective-permute-done), channel_id=1, source_target_pairs={{0,504},{8,0},{16,8},{24,16},{32,24},{40,32},{48,40},{56,48},{64,5... | collective-permute-start | bytes 288008 | tf_op jit(solution)/shard_map/while/body/eval_jaxpr/ppermute | solution.py:9
  181.9 4.8 fusion.24
  187.9 8.6 %collective-permute-start = (bf16[24,2000]{1,0:T(8,128)(2,1)S(1)}, bf16[24,2000]{1,0:T(8,128)(2,1)S(1)}, u32[]{:S(2)}, u32[]{:S(2)}) collective-permute-start(bf16[24,2000]{1,0:T(8,128)(2,1)S(1)} %get-tuple-element.201), channel_id=1, source_target_pairs={{0,504},{8,0},{16,8},{24,16},{32,24},{40,32},{48,40},{56,48},{64,5... | collective-permute-start | bytes 288008 | tf_op jit(solution)/shard_map/while/body/eval_jaxpr/ppermute | solution.py:9
  197.5 8.6 %collective-permute-start.1 = (bf16[24,2000]{1,0:T(8,128)(2,1)S(1)}, bf16[24,2000]{1,0:T(8,128)(2,1)S(1)}, u32[]{:S(2)}, u32[]{:S(2)}) collective-permute-start(bf16[24,2000]{1,0:T(8,128)(2,1)S(1)} %collective-permute-done), channel_id=1, source_target_pairs={{0,504},{8,0},{16,8},{24,16},{32,24},{40,32},{48,40},{56,48},{64,5... | collective-permute-start | bytes 288008 | tf_op jit(solution)/shard_map/while/body/eval_jaxpr/ppermute | solution.py:9
  207.0 4.8 fusion.24
  213.1 8.6 %collective-permute-start = (bf16[24,2000]{1,0:T(8,128)(2,1)S(1)}, bf16[24,2000]{1,0:T(8,128)(2,1)S(1)}, u32[]{:S(2)}, u32[]{:S(2)}) collective-permute-start(bf16[24,2000]{1,0:T(8,128)(2,1)S(1)} %get-tuple-element.201), channel_id=1, source_target_pairs={{0,504},{8,0},{16,8},{24,16},{32,24},{40,32},{48,40},{56,48},{64,5... | collective-permute-start | bytes 288008 | tf_op jit(solution)/shard_map/while/body/eval_jaxpr/ppermute | solution.py:9
  222.6 8.6 %collective-permute-start.1 = (bf16[24,2000]{1,0:T(8,128)(2,1)S(1)}, bf16[24,2000]{1,0:T(8,128)(2,1)S(1)}, u32[]{:S(2)}, u32[]{:S(2)}) collective-permute-start(bf16[24,2000]{1,0:T(8,128)(2,1)S(1)} %collective-permute-done), channel_id=1, source_target_pairs={{0,504},{8,0},{16,8},{24,16},{32,24},{40,32},{48,40},{56,48},{64,5... | collective-permute-start | bytes 288008 | tf_op jit(solution)/shard_map/while/body/eval_jaxpr/ppermute | solution.py:9
  232.1 4.8 fusion.24
  238.2 8.6 %collective-permute-start = (bf16[24,2000]{1,0:T(8,128)(2,1)S(1)}, bf16[24,2000]{1,0:T(8,128)(2,1)S(1)}, u32[]{:S(2)}, u32[]{:S(2)}) collective-permute-start(bf16[24,2000]{1,0:T(8,128)(2,1)S(1)} %get-tuple-element.201), channel_id=1, source_target_pairs={{0,504},{8,0},{16,8},{24,16},{32,24},{40,32},{48,40},{56,48},{64,5... | collective-permute-start | bytes 288008 | tf_op jit(solution)/shard_map/while/body/eval_jaxpr/ppermute | solution.py:9
  247.7 8.6 %collective-permute-start.1 = (bf16[24,2000]{1,0:T(8,128)(2,1)S(1)}, bf16[24,2000]{1,0:T(8,128)(2,1)S(1)}, u32[]{:S(2)}, u32[]{:S(2)}) collective-permute-start(bf16[24,2000]{1,0:T(8,128)(2,1)S(1)} %collective-permute-done), channel_id=1, source_target_pairs={{0,504},{8,0},{16,8},{24,16},{32,24},{40,32},{48,40},{56,48},{64,5... | collective-permute-start | bytes 288008 | tf_op jit(solution)/shard_map/while/body/eval_jaxpr/ppermute | solution.py:9
  257.3 4.8 fusion.24
  263.3 8.6 %collective-permute-start = (bf16[24,2000]{1,0:T(8,128)(2,1)S(1)}, bf16[24,2000]{1,0:T(8,128)(2,1)S(1)}, u32[]{:S(2)}, u32[]{:S(2)}) collective-permute-start(bf16[24,2000]{1,0:T(8,128)(2,1)S(1)} %get-tuple-element.201), channel_id=1, source_target_pairs={{0,504},{8,0},{16,8},{24,16},{32,24},{40,32},{48,40},{56,48},{64,5... | collective-permute-start | bytes 288008 | tf_op jit(solution)/shard_map/while/body/eval_jaxpr/ppermute | solution.py:9
  272.9 8.6 %collective-permute-start.1 = (bf16[24,2000]{1,0:T(8,128)(2,1)S(1)}, bf16[24,2000]{1,0:T(8,128)(2,1)S(1)}, u32[]{:S(2)}, u32[]{:S(2)}) collective-permute-start(bf16[24,2000]{1,0:T(8,128)(2,1)S(1)} %collective-permute-done), channel_id=1, source_target_pairs={{0,504},{8,0},{16,8},{24,16},{32,24},{40,32},{48,40},{56,48},{64,5... | collective-permute-start | bytes 288008 | tf_op jit(solution)/shard_map/while/body/eval_jaxpr/ppermute | solution.py:9
  282.4 4.8 fusion.24
  288.4 8.6 %collective-permute-start = (bf16[24,2000]{1,0:T(8,128)(2,1)S(1)}, bf16[24,2000]{1,0:T(8,128)(2,1)S(1)}, u32[]{:S(2)}, u32[]{:S(2)}) collective-permute-start(bf16[24,2000]{1,0:T(8,128)(2,1)S(1)} %get-tuple-element.201), channel_id=1, source_target_pairs={{0,504},{8,0},{16,8},{24,16},{32,24},{40,32},{48,40},{56,48},{64,5... | collective-permute-start | bytes 288008 | tf_op jit(solution)/shard_map/while/body/eval_jaxpr/ppermute | solution.py:9
  298.0 8.6 %collective-permute-start.1 = (bf16[24,2000]{1,0:T(8,128)(2,1)S(1)}, bf16[24,2000]{1,0:T(8,128)(2,1)S(1)}, u32[]{:S(2)}, u32[]{:S(2)}) collective-permute-start(bf16[24,2000]{1,0:T(8,128)(2,1)S(1)} %collective-permute-done), channel_id=1, source_target_pairs={{0,504},{8,0},{16,8},{24,16},{32,24},{40,32},{48,40},{56,48},{64,5... | collective-permute-start | bytes 288008 | tf_op jit(solution)/shard_map/while/body/eval_jaxpr/ppermute | solution.py:9
  307.5 4.8 fusion.24
  313.6 8.6 %collective-permute-start = (bf16[24,2000]{1,0:T(8,128)(2,1)S(1)}, bf16[24,2000]{1,0:T(8,128)(2,1)S(1)}, u32[]{:S(2)}, u32[]{:S(2)}) collective-permute-start(bf16[24,2000]{1,0:T(8,128)(2,1)S(1)} %get-tuple-element.201), channel_id=1, source_target_pairs={{0,504},{8,0},{16,8},{24,16},{32,24},{40,32},{48,40},{56,48},{64,5... | collective-permute-start | bytes 288008 | tf_op jit(solution)/shard_map/while/body/eval_jaxpr/ppermute | solution.py:9
  323.1 8.6 %collective-permute-start.1 = (bf16[24,2000]{1,0:T(8,128)(2,1)S(1)}, bf16[24,2000]{1,0:T(8,128)(2,1)S(1)}, u32[]{:S(2)}, u32[]{:S(2)}) collective-permute-start(bf16[24,2000]{1,0:T(8,128)(2,1)S(1)} %collective-permute-done), channel_id=1, source_target_pairs={{0,504},{8,0},{16,8},{24,16},{32,24},{40,32},{48,40},{56,48},{64,5... | collective-permute-start | bytes 288008 | tf_op jit(solution)/shard_map/while/body/eval_jaxpr/ppermute | solution.py:9
  332.7 4.8 fusion.24
  338.7 8.6 %collective-permute-start = (bf16[24,2000]{1,0:T(8,128)(2,1)S(1)}, bf16[24,2000]{1,0:T(8,128)(2,1)S(1)}, u32[]{:S(2)}, u32[]{:S(2)}) collective-permute-start(bf16[24,2000]{1,0:T(8,128)(2,1)S(1)} %get-tuple-element.201), channel_id=1, source_target_pairs={{0,504},{8,0},{16,8},{24,16},{32,24},{40,32},{48,40},{56,48},{64,5... | collective-permute-start | bytes 288008 | tf_op jit(solution)/shard_map/while/body/eval_jaxpr/ppermute | solution.py:9
  348.2 8.6 %collective-permute-start.1 = (bf16[24,2000]{1,0:T(8,128)(2,1)S(1)}, bf16[24,2000]{1,0:T(8,128)(2,1)S(1)}, u32[]{:S(2)}, u32[]{:S(2)}) collective-permute-start(bf16[24,2000]{1,0:T(8,128)(2,1)S(1)} %collective-permute-done), channel_id=1, source_target_pairs={{0,504},{8,0},{16,8},{24,16},{32,24},{40,32},{48,40},{56,48},{64,5... | collective-permute-start | bytes 288008 | tf_op jit(solution)/shard_map/while/body/eval_jaxpr/ppermute | solution.py:9
  357.8 4.8 fusion.24
  363.8 8.6 %collective-permute-start = (bf16[24,2000]{1,0:T(8,128)(2,1)S(1)}, bf16[24,2000]{1,0:T(8,128)(2,1)S(1)}, u32[]{:S(2)}, u32[]{:S(2)}) collective-permute-start(bf16[24,2000]{1,0:T(8,128)(2,1)S(1)} %get-tuple-element.201), channel_id=1, source_target_pairs={{0,504},{8,0},{16,8},{24,16},{32,24},{40,32},{48,40},{56,48},{64,5... | collective-permute-start | bytes 288008 | tf_op jit(solution)/shard_map/while/body/eval_jaxpr/ppermute | solution.py:9
  373.4 8.6 %collective-permute-start.1 = (bf16[24,2000]{1,0:T(8,128)(2,1)S(1)}, bf16[24,2000]{1,0:T(8,128)(2,1)S(1)}, u32[]{:S(2)}, u32[]{:S(2)}) collective-permute-start(bf16[24,2000]{1,0:T(8,128)(2,1)S(1)} %collective-permute-done), channel_id=1, source_target_pairs={{0,504},{8,0},{16,8},{24,16},{32,24},{40,32},{48,40},{56,48},{64,5... | collective-permute-start | bytes 288008 | tf_op jit(solution)/shard_map/while/body/eval_jaxpr/ppermute | solution.py:9
  382.9 4.8 fusion.24
  389.0 8.6 %collective-permute-start = (bf16[24,2000]{1,0:T(8,128)(2,1)S(1)}, bf16[24,2000]{1,0:T(8,128)(2,1)S(1)}, u32[]{:S(2)}, u32[]{:S(2)}) collective-permute-start(bf16[24,2000]{1,0:T(8,128)(2,1)S(1)} %get-tuple-element.201), channel_id=1, source_target_pairs={{0,504},{8,0},{16,8},{24,16},{32,24},{40,32},{48,40},{56,48},{64,5... | collective-permute-start | bytes 288008 | tf_op jit(solution)/shard_map/while/body/eval_jaxpr/ppermute | solution.py:9
  398.5 8.6 %collective-permute-start.1 = (bf16[24,2000]{1,0:T(8,128)(2,1)S(1)}, bf16[24,2000]{1,0:T(8,128)(2,1)S(1)}, u32[]{:S(2)}, u32[]{:S(2)}) collective-permute-start(bf16[24,2000]{1,0:T(8,128)(2,1)S(1)} %collective-permute-done), channel_id=1, source_target_pairs={{0,504},{8,0},{16,8},{24,16},{32,24},{40,32},{48,40},{56,48},{64,5... | collective-permute-start | bytes 288008 | tf_op jit(solution)/shard_map/while/body/eval_jaxpr/ppermute | solution.py:9
  408.0 4.8 fusion.24
  414.1 8.6 %collective-permute-start = (bf16[24,2000]{1,0:T(8,128)(2,1)S(1)}, bf16[24,2000]{1,0:T(8,128)(2,1)S(1)}, u32[]{:S(2)}, u32[]{:S(2)}) collective-permute-start(bf16[24,2000]{1,0:T(8,128)(2,1)S(1)} %get-tuple-element.201), channel_id=1, source_target_pairs={{0,504},{8,0},{16,8},{24,16},{32,24},{40,32},{48,40},{56,48},{64,5... | collective-permute-start | bytes 288008 | tf_op jit(solution)/shard_map/while/body/eval_jaxpr/ppermute | solution.py:9
  423.6 8.6 %collective-permute-start.1 = (bf16[24,2000]{1,0:T(8,128)(2,1)S(1)}, bf16[24,2000]{1,0:T(8,128)(2,1)S(1)}, u32[]{:S(2)}, u32[]{:S(2)}) collective-permute-start(bf16[24,2000]{1,0:T(8,128)(2,1)S(1)} %collective-permute-done), channel_id=1, source_target_pairs={{0,504},{8,0},{16,8},{24,16},{32,24},{40,32},{48,40},{56,48},{64,5... | collective-permute-start | bytes 288008 | tf_op jit(solution)/shard_map/while/body/eval_jaxpr/ppermute | solution.py:9
  439.2 8.6 %collective-permute-start = (bf16[24,2000]{1,0:T(8,128)(2,1)S(1)}, bf16[24,2000]{1,0:T(8,128)(2,1)S(1)}, u32[]{:S(2)}, u32[]{:S(2)}) collective-permute-start(bf16[24,2000]{1,0:T(8,128)(2,1)S(1)} %get-tuple-element.201), channel_id=1, source_target_pairs={{0,504},{8,0},{16,8},{24,16},{32,24},{40,32},{48,40},{56,48},{64,5... | collective-permute-start | bytes 288008 | tf_op jit(solution)/shard_map/while/body/eval_jaxpr/ppermute | solution.py:9
  448.8 8.6 %collective-permute-start.1 = (bf16[24,2000]{1,0:T(8,128)(2,1)S(1)}, bf16[24,2000]{1,0:T(8,128)(2,1)S(1)}, u32[]{:S(2)}, u32[]{:S(2)}) collective-permute-start(bf16[24,2000]{1,0:T(8,128)(2,1)S(1)} %collective-permute-done), channel_id=1, source_target_pairs={{0,504},{8,0},{16,8},{24,16},{32,24},{40,32},{48,40},{56,48},{64,5... | collective-permute-start | bytes 288008 | tf_op jit(solution)/shard_map/while/body/eval_jaxpr/ppermute | solution.py:9
  464.3 8.6 %collective-permute-start = (bf16[24,2000]{1,0:T(8,128)(2,1)S(1)}, bf16[24,2000]{1,0:T(8,128)(2,1)S(1)}, u32[]{:S(2)}, u32[]{:S(2)}) collective-permute-start(bf16[24,2000]{1,0:T(8,128)(2,1)S(1)} %get-tuple-element.201), channel_id=1, source_target_pairs={{0,504},{8,0},{16,8},{24,16},{32,24},{40,32},{48,40},{56,48},{64,5... | collective-permute-start | bytes 288008 | tf_op jit(solution)/shard_map/while/body/eval_jaxpr/ppermute | solution.py:9
  473.9 8.6 %collective-permute-start.1 = (bf16[24,2000]{1,0:T(8,128)(2,1)S(1)}, bf16[24,2000]{1,0:T(8,128)(2,1)S(1)}, u32[]{:S(2)}, u32[]{:S(2)}) collective-permute-start(bf16[24,2000]{1,0:T(8,128)(2,1)S(1)} %collective-permute-done), channel_id=1, source_target_pairs={{0,504},{8,0},{16,8},{24,16},{32,24},{40,32},{48,40},{56,48},{64,5... | collective-permute-start | bytes 288008 | tf_op jit(solution)/shard_map/while/body/eval_jaxpr/ppermute | solution.py:9
  489.5 8.6 %collective-permute-start = (bf16[24,2000]{1,0:T(8,128)(2,1)S(1)}, bf16[24,2000]{1,0:T(8,128)(2,1)S(1)}, u32[]{:S(2)}, u32[]{:S(2)}) collective-permute-start(bf16[24,2000]{1,0:T(8,128)(2,1)S(1)} %get-tuple-element.201), channel_id=1, source_target_pairs={{0,504},{8,0},{16,8},{24,16},{32,24},{40,32},{48,40},{56,48},{64,5... | collective-permute-start | bytes 288008 | tf_op jit(solution)/shard_map/while/body/eval_jaxpr/ppermute | solution.py:9
  499.0 8.6 %collective-permute-start.1 = (bf16[24,2000]{1,0:T(8,128)(2,1)S(1)}, bf16[24,2000]{1,0:T(8,128)(2,1)S(1)}, u32[]{:S(2)}, u32[]{:S(2)}) collective-permute-start(bf16[24,2000]{1,0:T(8,128)(2,1)S(1)} %collective-permute-done), channel_id=1, source_target_pairs={{0,504},{8,0},{16,8},{24,16},{32,24},{40,32},{48,40},{56,48},{64,5... | collective-permute-start | bytes 288008 | tf_op jit(solution)/shard_map/while/body/eval_jaxpr/ppermute | solution.py:9
  514.6 8.6 %collective-permute-start = (bf16[24,2000]{1,0:T(8,128)(2,1)S(1)}, bf16[24,2000]{1,0:T(8,128)(2,1)S(1)}, u32[]{:S(2)}, u32[]{:S(2)}) collective-permute-start(bf16[24,2000]{1,0:T(8,128)(2,1)S(1)} %get-tuple-element.201), channel_id=1, source_target_pairs={{0,504},{8,0},{16,8},{24,16},{32,24},{40,32},{48,40},{56,48},{64,5... | collective-permute-start | bytes 288008 | tf_op jit(solution)/shard_map/while/body/eval_jaxpr/ppermute | solution.py:9
  524.1 8.6 %collective-permute-start.1 = (bf16[24,2000]{1,0:T(8,128)(2,1)S(1)}, bf16[24,2000]{1,0:T(8,128)(2,1)S(1)}, u32[]{:S(2)}, u32[]{:S(2)}) collective-permute-start(bf16[24,2000]{1,0:T(8,128)(2,1)S(1)} %collective-permute-done), channel_id=1, source_target_pairs={{0,504},{8,0},{16,8},{24,16},{32,24},{40,32},{48,40},{56,48},{64,5... | collective-permute-start | bytes 288008 | tf_op jit(solution)/shard_map/while/body/eval_jaxpr/ppermute | solution.py:9
  533.7 4.8 fusion.24
  (87 shorter events, 81.5 us)
Async XLA Ops:
  6.5 88.1 %all-gather.3.cloned.1.call-start = ((), (), s32[]{:S(2)}) async-start(), calls=%async_computation | async-start | bytes 7077888 | tf_op jit(solution)/shard_map/all_gather | solution.py:45
  7.5 94.3 %copy-start.2 = (bf16[192]{0:T(256)(128)(2,1)S(1)}, bf16[192]{0:T(256)(128)(2,1)}, u32[]{:S(2)}) copy-start(bf16[192]{0:T(256)(128)(2,1)} %param.8) | copy-start | bytes 1156
  7.5 133.2 %all-gather.5.cloned.1.call-start = ((), (), s32[]{:S(2)}) async-start(), calls=%async_computation.1 | async-start | bytes 1327104 | tf_op jit(solution)/shard_map/all_gather | solution.py:52
  115.1 27.0 %copy-start = (f32[24,1536]{1,0:T(8,128)S(1)}, f32[24,1536]{1,0:T(8,128)}, u32[]{:S(2)}) copy-start(f32[24,1536]{1,0:T(8,128)} %fusion.5) | copy-start | bytes 442372
  143.2 11.1 %collective-permute-start = (bf16[24,2000]{1,0:T(8,128)(2,1)S(1)}, bf16[24,2000]{1,0:T(8,128)(2,1)S(1)}, u32[]{:S(2)}, u32[]{:S(2)}) collective-permute-start(bf16[24,2000]{1,0:T(8,128)(2,1)S(1)} %get-tuple-element.201), channel_id=1, source_target_pairs={{0,504},{8,0},{16,8},{24,16},{32,24},{40,32},{48,40},{56,48},{64,5... | collective-permute-start | bytes 288008 | tf_op jit(solution)/shard_map/while/body/eval_jaxpr/ppermute | solution.py:9
  154.3 5.9 %collective-permute-start.1 = (bf16[24,2000]{1,0:T(8,128)(2,1)S(1)}, bf16[24,2000]{1,0:T(8,128)(2,1)S(1)}, u32[]{:S(2)}, u32[]{:S(2)}) collective-permute-start(bf16[24,2000]{1,0:T(8,128)(2,1)S(1)} %collective-permute-done), channel_id=1, source_target_pairs={{0,504},{8,0},{16,8},{24,16},{32,24},{40,32},{48,40},{56,48},{64,5... | collective-permute-start | bytes 288008 | tf_op jit(solution)/shard_map/while/body/eval_jaxpr/ppermute | solution.py:9
  166.3 6.1 %collective-permute-start = (bf16[24,2000]{1,0:T(8,128)(2,1)S(1)}, bf16[24,2000]{1,0:T(8,128)(2,1)S(1)}, u32[]{:S(2)}, u32[]{:S(2)}) collective-permute-start(bf16[24,2000]{1,0:T(8,128)(2,1)S(1)} %get-tuple-element.201), channel_id=1, source_target_pairs={{0,504},{8,0},{16,8},{24,16},{32,24},{40,32},{48,40},{56,48},{64,5... | collective-permute-start | bytes 288008 | tf_op jit(solution)/shard_map/while/body/eval_jaxpr/ppermute | solution.py:9
  172.3 9.5 %collective-permute-start.1 = (bf16[24,2000]{1,0:T(8,128)(2,1)S(1)}, bf16[24,2000]{1,0:T(8,128)(2,1)S(1)}, u32[]{:S(2)}, u32[]{:S(2)}) collective-permute-start(bf16[24,2000]{1,0:T(8,128)(2,1)S(1)} %collective-permute-done), channel_id=1, source_target_pairs={{0,504},{8,0},{16,8},{24,16},{32,24},{40,32},{48,40},{56,48},{64,5... | collective-permute-start | bytes 288008 | tf_op jit(solution)/shard_map/while/body/eval_jaxpr/ppermute | solution.py:9
  187.9 9.6 %collective-permute-start = (bf16[24,2000]{1,0:T(8,128)(2,1)S(1)}, bf16[24,2000]{1,0:T(8,128)(2,1)S(1)}, u32[]{:S(2)}, u32[]{:S(2)}) collective-permute-start(bf16[24,2000]{1,0:T(8,128)(2,1)S(1)} %get-tuple-element.201), channel_id=1, source_target_pairs={{0,504},{8,0},{16,8},{24,16},{32,24},{40,32},{48,40},{56,48},{64,5... | collective-permute-start | bytes 288008 | tf_op jit(solution)/shard_map/while/body/eval_jaxpr/ppermute | solution.py:9
  197.5 9.5 %collective-permute-start.1 = (bf16[24,2000]{1,0:T(8,128)(2,1)S(1)}, bf16[24,2000]{1,0:T(8,128)(2,1)S(1)}, u32[]{:S(2)}, u32[]{:S(2)}) collective-permute-start(bf16[24,2000]{1,0:T(8,128)(2,1)S(1)} %collective-permute-done), channel_id=1, source_target_pairs={{0,504},{8,0},{16,8},{24,16},{32,24},{40,32},{48,40},{56,48},{64,5... | collective-permute-start | bytes 288008 | tf_op jit(solution)/shard_map/while/body/eval_jaxpr/ppermute | solution.py:9
  213.1 9.6 %collective-permute-start = (bf16[24,2000]{1,0:T(8,128)(2,1)S(1)}, bf16[24,2000]{1,0:T(8,128)(2,1)S(1)}, u32[]{:S(2)}, u32[]{:S(2)}) collective-permute-start(bf16[24,2000]{1,0:T(8,128)(2,1)S(1)} %get-tuple-element.201), channel_id=1, source_target_pairs={{0,504},{8,0},{16,8},{24,16},{32,24},{40,32},{48,40},{56,48},{64,5... | collective-permute-start | bytes 288008 | tf_op jit(solution)/shard_map/while/body/eval_jaxpr/ppermute | solution.py:9
  222.6 9.5 %collective-permute-start.1 = (bf16[24,2000]{1,0:T(8,128)(2,1)S(1)}, bf16[24,2000]{1,0:T(8,128)(2,1)S(1)}, u32[]{:S(2)}, u32[]{:S(2)}) collective-permute-start(bf16[24,2000]{1,0:T(8,128)(2,1)S(1)} %collective-permute-done), channel_id=1, source_target_pairs={{0,504},{8,0},{16,8},{24,16},{32,24},{40,32},{48,40},{56,48},{64,5... | collective-permute-start | bytes 288008 | tf_op jit(solution)/shard_map/while/body/eval_jaxpr/ppermute | solution.py:9
  238.2 9.6 %collective-permute-start = (bf16[24,2000]{1,0:T(8,128)(2,1)S(1)}, bf16[24,2000]{1,0:T(8,128)(2,1)S(1)}, u32[]{:S(2)}, u32[]{:S(2)}) collective-permute-start(bf16[24,2000]{1,0:T(8,128)(2,1)S(1)} %get-tuple-element.201), channel_id=1, source_target_pairs={{0,504},{8,0},{16,8},{24,16},{32,24},{40,32},{48,40},{56,48},{64,5... | collective-permute-start | bytes 288008 | tf_op jit(solution)/shard_map/while/body/eval_jaxpr/ppermute | solution.py:9
  247.7 9.5 %collective-permute-start.1 = (bf16[24,2000]{1,0:T(8,128)(2,1)S(1)}, bf16[24,2000]{1,0:T(8,128)(2,1)S(1)}, u32[]{:S(2)}, u32[]{:S(2)}) collective-permute-start(bf16[24,2000]{1,0:T(8,128)(2,1)S(1)} %collective-permute-done), channel_id=1, source_target_pairs={{0,504},{8,0},{16,8},{24,16},{32,24},{40,32},{48,40},{56,48},{64,5... | collective-permute-start | bytes 288008 | tf_op jit(solution)/shard_map/while/body/eval_jaxpr/ppermute | solution.py:9
  263.3 9.6 %collective-permute-start = (bf16[24,2000]{1,0:T(8,128)(2,1)S(1)}, bf16[24,2000]{1,0:T(8,128)(2,1)S(1)}, u32[]{:S(2)}, u32[]{:S(2)}) collective-permute-start(bf16[24,2000]{1,0:T(8,128)(2,1)S(1)} %get-tuple-element.201), channel_id=1, source_target_pairs={{0,504},{8,0},{16,8},{24,16},{32,24},{40,32},{48,40},{56,48},{64,5... | collective-permute-start | bytes 288008 | tf_op jit(solution)/shard_map/while/body/eval_jaxpr/ppermute | solution.py:9
  272.9 9.5 %collective-permute-start.1 = (bf16[24,2000]{1,0:T(8,128)(2,1)S(1)}, bf16[24,2000]{1,0:T(8,128)(2,1)S(1)}, u32[]{:S(2)}, u32[]{:S(2)}) collective-permute-start(bf16[24,2000]{1,0:T(8,128)(2,1)S(1)} %collective-permute-done), channel_id=1, source_target_pairs={{0,504},{8,0},{16,8},{24,16},{32,24},{40,32},{48,40},{56,48},{64,5... | collective-permute-start | bytes 288008 | tf_op jit(solution)/shard_map/while/body/eval_jaxpr/ppermute | solution.py:9
  288.4 9.6 %collective-permute-start = (bf16[24,2000]{1,0:T(8,128)(2,1)S(1)}, bf16[24,2000]{1,0:T(8,128)(2,1)S(1)}, u32[]{:S(2)}, u32[]{:S(2)}) collective-permute-start(bf16[24,2000]{1,0:T(8,128)(2,1)S(1)} %get-tuple-element.201), channel_id=1, source_target_pairs={{0,504},{8,0},{16,8},{24,16},{32,24},{40,32},{48,40},{56,48},{64,5... | collective-permute-start | bytes 288008 | tf_op jit(solution)/shard_map/while/body/eval_jaxpr/ppermute | solution.py:9
  298.0 9.5 %collective-permute-start.1 = (bf16[24,2000]{1,0:T(8,128)(2,1)S(1)}, bf16[24,2000]{1,0:T(8,128)(2,1)S(1)}, u32[]{:S(2)}, u32[]{:S(2)}) collective-permute-start(bf16[24,2000]{1,0:T(8,128)(2,1)S(1)} %collective-permute-done), channel_id=1, source_target_pairs={{0,504},{8,0},{16,8},{24,16},{32,24},{40,32},{48,40},{56,48},{64,5... | collective-permute-start | bytes 288008 | tf_op jit(solution)/shard_map/while/body/eval_jaxpr/ppermute | solution.py:9
  313.6 9.6 %collective-permute-start = (bf16[24,2000]{1,0:T(8,128)(2,1)S(1)}, bf16[24,2000]{1,0:T(8,128)(2,1)S(1)}, u32[]{:S(2)}, u32[]{:S(2)}) collective-permute-start(bf16[24,2000]{1,0:T(8,128)(2,1)S(1)} %get-tuple-element.201), channel_id=1, source_target_pairs={{0,504},{8,0},{16,8},{24,16},{32,24},{40,32},{48,40},{56,48},{64,5... | collective-permute-start | bytes 288008 | tf_op jit(solution)/shard_map/while/body/eval_jaxpr/ppermute | solution.py:9
  323.1 9.5 %collective-permute-start.1 = (bf16[24,2000]{1,0:T(8,128)(2,1)S(1)}, bf16[24,2000]{1,0:T(8,128)(2,1)S(1)}, u32[]{:S(2)}, u32[]{:S(2)}) collective-permute-start(bf16[24,2000]{1,0:T(8,128)(2,1)S(1)} %collective-permute-done), channel_id=1, source_target_pairs={{0,504},{8,0},{16,8},{24,16},{32,24},{40,32},{48,40},{56,48},{64,5... | collective-permute-start | bytes 288008 | tf_op jit(solution)/shard_map/while/body/eval_jaxpr/ppermute | solution.py:9
  338.7 9.6 %collective-permute-start = (bf16[24,2000]{1,0:T(8,128)(2,1)S(1)}, bf16[24,2000]{1,0:T(8,128)(2,1)S(1)}, u32[]{:S(2)}, u32[]{:S(2)}) collective-permute-start(bf16[24,2000]{1,0:T(8,128)(2,1)S(1)} %get-tuple-element.201), channel_id=1, source_target_pairs={{0,504},{8,0},{16,8},{24,16},{32,24},{40,32},{48,40},{56,48},{64,5... | collective-permute-start | bytes 288008 | tf_op jit(solution)/shard_map/while/body/eval_jaxpr/ppermute | solution.py:9
  348.2 9.5 %collective-permute-start.1 = (bf16[24,2000]{1,0:T(8,128)(2,1)S(1)}, bf16[24,2000]{1,0:T(8,128)(2,1)S(1)}, u32[]{:S(2)}, u32[]{:S(2)}) collective-permute-start(bf16[24,2000]{1,0:T(8,128)(2,1)S(1)} %collective-permute-done), channel_id=1, source_target_pairs={{0,504},{8,0},{16,8},{24,16},{32,24},{40,32},{48,40},{56,48},{64,5... | collective-permute-start | bytes 288008 | tf_op jit(solution)/shard_map/while/body/eval_jaxpr/ppermute | solution.py:9
  363.8 9.6 %collective-permute-start = (bf16[24,2000]{1,0:T(8,128)(2,1)S(1)}, bf16[24,2000]{1,0:T(8,128)(2,1)S(1)}, u32[]{:S(2)}, u32[]{:S(2)}) collective-permute-start(bf16[24,2000]{1,0:T(8,128)(2,1)S(1)} %get-tuple-element.201), channel_id=1, source_target_pairs={{0,504},{8,0},{16,8},{24,16},{32,24},{40,32},{48,40},{56,48},{64,5... | collective-permute-start | bytes 288008 | tf_op jit(solution)/shard_map/while/body/eval_jaxpr/ppermute | solution.py:9
  373.4 9.5 %collective-permute-start.1 = (bf16[24,2000]{1,0:T(8,128)(2,1)S(1)}, bf16[24,2000]{1,0:T(8,128)(2,1)S(1)}, u32[]{:S(2)}, u32[]{:S(2)}) collective-permute-start(bf16[24,2000]{1,0:T(8,128)(2,1)S(1)} %collective-permute-done), channel_id=1, source_target_pairs={{0,504},{8,0},{16,8},{24,16},{32,24},{40,32},{48,40},{56,48},{64,5... | collective-permute-start | bytes 288008 | tf_op jit(solution)/shard_map/while/body/eval_jaxpr/ppermute | solution.py:9
  389.0 9.6 %collective-permute-start = (bf16[24,2000]{1,0:T(8,128)(2,1)S(1)}, bf16[24,2000]{1,0:T(8,128)(2,1)S(1)}, u32[]{:S(2)}, u32[]{:S(2)}) collective-permute-start(bf16[24,2000]{1,0:T(8,128)(2,1)S(1)} %get-tuple-element.201), channel_id=1, source_target_pairs={{0,504},{8,0},{16,8},{24,16},{32,24},{40,32},{48,40},{56,48},{64,5... | collective-permute-start | bytes 288008 | tf_op jit(solution)/shard_map/while/body/eval_jaxpr/ppermute | solution.py:9
  398.5 9.5 %collective-permute-start.1 = (bf16[24,2000]{1,0:T(8,128)(2,1)S(1)}, bf16[24,2000]{1,0:T(8,128)(2,1)S(1)}, u32[]{:S(2)}, u32[]{:S(2)}) collective-permute-start(bf16[24,2000]{1,0:T(8,128)(2,1)S(1)} %collective-permute-done), channel_id=1, source_target_pairs={{0,504},{8,0},{16,8},{24,16},{32,24},{40,32},{48,40},{56,48},{64,5... | collective-permute-start | bytes 288008 | tf_op jit(solution)/shard_map/while/body/eval_jaxpr/ppermute | solution.py:9
  414.1 9.6 %collective-permute-start = (bf16[24,2000]{1,0:T(8,128)(2,1)S(1)}, bf16[24,2000]{1,0:T(8,128)(2,1)S(1)}, u32[]{:S(2)}, u32[]{:S(2)}) collective-permute-start(bf16[24,2000]{1,0:T(8,128)(2,1)S(1)} %get-tuple-element.201), channel_id=1, source_target_pairs={{0,504},{8,0},{16,8},{24,16},{32,24},{40,32},{48,40},{56,48},{64,5... | collective-permute-start | bytes 288008 | tf_op jit(solution)/shard_map/while/body/eval_jaxpr/ppermute | solution.py:9
  423.6 9.5 %collective-permute-start.1 = (bf16[24,2000]{1,0:T(8,128)(2,1)S(1)}, bf16[24,2000]{1,0:T(8,128)(2,1)S(1)}, u32[]{:S(2)}, u32[]{:S(2)}) collective-permute-start(bf16[24,2000]{1,0:T(8,128)(2,1)S(1)} %collective-permute-done), channel_id=1, source_target_pairs={{0,504},{8,0},{16,8},{24,16},{32,24},{40,32},{48,40},{56,48},{64,5... | collective-permute-start | bytes 288008 | tf_op jit(solution)/shard_map/while/body/eval_jaxpr/ppermute | solution.py:9
  439.2 9.6 %collective-permute-start = (bf16[24,2000]{1,0:T(8,128)(2,1)S(1)}, bf16[24,2000]{1,0:T(8,128)(2,1)S(1)}, u32[]{:S(2)}, u32[]{:S(2)}) collective-permute-start(bf16[24,2000]{1,0:T(8,128)(2,1)S(1)} %get-tuple-element.201), channel_id=1, source_target_pairs={{0,504},{8,0},{16,8},{24,16},{32,24},{40,32},{48,40},{56,48},{64,5... | collective-permute-start | bytes 288008 | tf_op jit(solution)/shard_map/while/body/eval_jaxpr/ppermute | solution.py:9
  448.8 9.5 %collective-permute-start.1 = (bf16[24,2000]{1,0:T(8,128)(2,1)S(1)}, bf16[24,2000]{1,0:T(8,128)(2,1)S(1)}, u32[]{:S(2)}, u32[]{:S(2)}) collective-permute-start(bf16[24,2000]{1,0:T(8,128)(2,1)S(1)} %collective-permute-done), channel_id=1, source_target_pairs={{0,504},{8,0},{16,8},{24,16},{32,24},{40,32},{48,40},{56,48},{64,5... | collective-permute-start | bytes 288008 | tf_op jit(solution)/shard_map/while/body/eval_jaxpr/ppermute | solution.py:9
  464.3 9.6 %collective-permute-start = (bf16[24,2000]{1,0:T(8,128)(2,1)S(1)}, bf16[24,2000]{1,0:T(8,128)(2,1)S(1)}, u32[]{:S(2)}, u32[]{:S(2)}) collective-permute-start(bf16[24,2000]{1,0:T(8,128)(2,1)S(1)} %get-tuple-element.201), channel_id=1, source_target_pairs={{0,504},{8,0},{16,8},{24,16},{32,24},{40,32},{48,40},{56,48},{64,5... | collective-permute-start | bytes 288008 | tf_op jit(solution)/shard_map/while/body/eval_jaxpr/ppermute | solution.py:9
  473.9 9.5 %collective-permute-start.1 = (bf16[24,2000]{1,0:T(8,128)(2,1)S(1)}, bf16[24,2000]{1,0:T(8,128)(2,1)S(1)}, u32[]{:S(2)}, u32[]{:S(2)}) collective-permute-start(bf16[24,2000]{1,0:T(8,128)(2,1)S(1)} %collective-permute-done), channel_id=1, source_target_pairs={{0,504},{8,0},{16,8},{24,16},{32,24},{40,32},{48,40},{56,48},{64,5... | collective-permute-start | bytes 288008 | tf_op jit(solution)/shard_map/while/body/eval_jaxpr/ppermute | solution.py:9
  489.5 9.6 %collective-permute-start = (bf16[24,2000]{1,0:T(8,128)(2,1)S(1)}, bf16[24,2000]{1,0:T(8,128)(2,1)S(1)}, u32[]{:S(2)}, u32[]{:S(2)}) collective-permute-start(bf16[24,2000]{1,0:T(8,128)(2,1)S(1)} %get-tuple-element.201), channel_id=1, source_target_pairs={{0,504},{8,0},{16,8},{24,16},{32,24},{40,32},{48,40},{56,48},{64,5... | collective-permute-start | bytes 288008 | tf_op jit(solution)/shard_map/while/body/eval_jaxpr/ppermute | solution.py:9
  499.0 9.5 %collective-permute-start.1 = (bf16[24,2000]{1,0:T(8,128)(2,1)S(1)}, bf16[24,2000]{1,0:T(8,128)(2,1)S(1)}, u32[]{:S(2)}, u32[]{:S(2)}) collective-permute-start(bf16[24,2000]{1,0:T(8,128)(2,1)S(1)} %collective-permute-done), channel_id=1, source_target_pairs={{0,504},{8,0},{16,8},{24,16},{32,24},{40,32},{48,40},{56,48},{64,5... | collective-permute-start | bytes 288008 | tf_op jit(solution)/shard_map/while/body/eval_jaxpr/ppermute | solution.py:9
  514.6 9.6 %collective-permute-start = (bf16[24,2000]{1,0:T(8,128)(2,1)S(1)}, bf16[24,2000]{1,0:T(8,128)(2,1)S(1)}, u32[]{:S(2)}, u32[]{:S(2)}) collective-permute-start(bf16[24,2000]{1,0:T(8,128)(2,1)S(1)} %get-tuple-element.201), channel_id=1, source_target_pairs={{0,504},{8,0},{16,8},{24,16},{32,24},{40,32},{48,40},{56,48},{64,5... | collective-permute-start | bytes 288008 | tf_op jit(solution)/shard_map/while/body/eval_jaxpr/ppermute | solution.py:9
  524.1 9.5 %collective-permute-start.1 = (bf16[24,2000]{1,0:T(8,128)(2,1)S(1)}, bf16[24,2000]{1,0:T(8,128)(2,1)S(1)}, u32[]{:S(2)}, u32[]{:S(2)}) collective-permute-start(bf16[24,2000]{1,0:T(8,128)(2,1)S(1)} %collective-permute-done), channel_id=1, source_target_pairs={{0,504},{8,0},{16,8},{24,16},{32,24},{40,32},{48,40},{56,48},{64,5... | collective-permute-start | bytes 288008 | tf_op jit(solution)/shard_map/while/body/eval_jaxpr/ppermute | solution.py:9
  539.7 0.9 copy-start.1
Sparse Core Ops, SparseCore 0:
  9.4 85.1 all-gather.2
  100.0 40.6 all-gather.4
where the time goes:
time: 554 us; the launch traced here: 547 us
  starting transfers between devices  265 us (48%)
  waiting for transfers between devices  148 us (27%)
  matrix products  102 us (18%)
  between operations  14.1 us (3%)
  blocking collectives  13 us (2%)
    ppermute x32, starting transfers between devices, from_behind(): lax.ppermute(value, axis, [(i, (i + by) % length) for i in range(length)])  265 us
    all_gather x1, waiting for transfers between devices, shards(): lax.all_gather(descriptors, 'narrow', axis=0, tiled=True)  87.2 us
    dot_general x17, matrix products, kernel_rows(): lax.dot_general(points, gathered, (((1,), (1,)), ((), ())), preferred_ele...  81.3 us
    ppermute x32, waiting for transfers between devices, from_behind(): lax.ppermute(value, axis, [(i, (i + by) % length) for i in range(length)])  34.8 us
    all_gather x1, waiting for transfers between devices, shards(): columns = lax.all_gather(local_kernel, 'narrow', axis=0, tiled=True)  25.6 us
    dot_general x17, matrix products, pair_blocks(): lax.dot_general(columns, weighted, (((1,), (1,)), ((), ())), precision=la...  20.7 us
    unnamed x1, blocking collectives  13 us
  transfers between devices with their start and end apart: 34, of which 34 were waited for; matrix products, arithmetic and copies ran while one was open for 0% of the time, Pallas kernels for 0%

commit v1 on v0

v1 whole, which is shorter than its diff:
```python
import jax
import jax.numpy as jnp
from jax import lax
from jax.sharding import PartitionSpec as P


def from_ahead(value, chips):
    size = lax.axis_size("wide")
    return lax.ppermute(value, "wide", [(i, (i - 2 * chips) % size) for i in range(size)])


def from_partner(value):
    size = lax.axis_size("wide")
    return lax.ppermute(value, "wide", [(i, i ^ 1) for i in range(size)])


def squared_dots(left, right, width):
    dots = lax.dot_general(left, right, (((1,), (1,)), ((), ())), preferred_element_type=jnp.float32)
    return dots * dots / width


def pair_blocks(rows, columns):
    return lax.dot_general(
        rows,
        columns,
        (((1,), (0,)), ((), ())),
        precision=lax.Precision.HIGH,
        preferred_element_type=jnp.float32,
    )


def shards(descriptors, env_weights, sparse_points):
    core = lax.axis_index("wide") % 2
    narrow = lax.axis_size("narrow")
    width = descriptors.shape[1]
    half = descriptors.shape[0] // 2
    env_count = descriptors.shape[0] * narrow
    piece = sparse_points.shape[0]
    block = piece * narrow

    points = jnp.pad(sparse_points, ((0, 0), (0, 1)))
    weighted_half = lax.dynamic_slice_in_dim(
        jnp.concatenate([descriptors, env_weights[:, None]], axis=1), core * half, half, 0
    )
    payload, points = lax.optimization_barrier(
        (jnp.concatenate([weighted_half, points], axis=0), points)
    )
    gathered = lax.all_gather(payload, "narrow", axis=0, tiled=False)
    envs = gathered[:, :half].reshape(narrow * half, width + 1)
    block_own = gathered[:, half:].reshape(block, width + 1)
    block_other = from_partner(block_own)

    strided = {0: points}
    for chips in (4, 12, 16, 8):
        strided[chips] = from_ahead(points, chips)

    def bundle(*chips):
        return jnp.concatenate([strided[c] for c in chips], axis=0)

    two_up = from_ahead(bundle(0, 4), 2)
    two_down = from_ahead(bundle(12, 16), -2)
    one_up = from_ahead(bundle(0, 4, 8, 12), 1)
    one_down = from_ahead(bundle(4, 8, 12, 16), -1)
    stride_own = bundle(0, 4, 8, 12, 16)
    twos_own = jnp.concatenate([two_up, two_down], axis=0)

    def in_order(stride, twos, ups, downs):
        cut = lambda rows, j: rows[j * piece : (j + 1) * piece]
        parts = []
        for j in range(17):
            source, index = ((stride, j // 4), (ups, j // 4), (twos, j // 4), (downs, j // 4))[j % 4]
            parts.append(cut(source, index))
        return jnp.concatenate(parts, axis=0)

    own = in_order(stride_own, twos_own, one_up, one_down)
    other = in_order(*(from_partner(v) for v in (stride_own, twos_own, one_up, one_down)))

    kernel_own = squared_dots(own, envs, width)
    kernel_other = squared_dots(other, envs, width)
    scale = envs[:, width:].astype(jnp.float32) / env_count
    columns_own = squared_dots(envs, block_own, width) * scale
    columns_other = squared_dots(envs, block_other, width) * scale

    odd = 16 * piece
    rows_other = jnp.concatenate(
        [kernel_other, lax.dynamic_slice_in_dim(kernel_own, (1 - core) * piece, odd, 0)], axis=0
    )
    arrived = from_partner(pair_blocks(rows_other, columns_other))
    rows_own = jnp.concatenate(
        [kernel_own, lax.dynamic_slice_in_dim(kernel_other, core * piece, odd, 0)], axis=0
    )
    total = (pair_blocks(rows_own, columns_own) + arrived).reshape(33, piece, block)
    even, odds = total[:17], total[17:]
    mixed = jnp.stack([even[:16], odds], axis=1).reshape(32, piece, block)
    return jnp.concatenate([mixed, even[16:]], axis=0)[None]


def solution(mesh):
    in_specs = (P("narrow", None), P("narrow"), P(("wide", "narrow"), None))
    out_specs = P("wide", None, "narrow", None)
    return jax.shard_map(shards, mesh=mesh, in_specs=in_specs, out_specs=out_specs, check_vma=False)
```

time: 554 us -> 171 us (0.31); the launches traced: 547 us -> 170 us
  starting transfers between devices: 265 us -> 64.1 us
  waiting for transfers between devices: 148 us -> 56.6 us
  matrix products: 102 us -> 13.6 us
  local copies, waits for them, and re-layouts: 3.58 us -> 18.5 us
  blocking collectives: 13 us -> 0 us
    ppermute x32 -> x14, starting transfers between devices: 265 us -> 64.1 us  [the longest x8 47.8 us: from_ahead(): lax.ppermute(value, 'wide', [(i, (i - 2 * chips) % size) for i in range(s...]
    dot_general x34 -> x6, matrix products: 102 us -> 13.6 us  [the longest x4 8.75 us: squared_dots(): lax.dot_general(left, right, (((1,), (1,)), ((), ())), preferred_element_...]
    all_gather x2 -> x1, waiting for transfers between devices: 113 us -> 34.3 us  [shards(): gathered = lax.all_gather(payload, 'narrow', axis=0, tiled=False)]
    unnamed x1 -> x0, blocking collectives: 13 us -> none
    ppermute x32 -> x14, waiting for transfers between devices: 34.8 us -> 22.2 us  [the longest x8 21.2 us: from_ahead(): lax.ppermute(value, 'wide', [(i, (i - 2 * chips) % size) for i in range(s...]
    unnamed x10 -> x38, local copies, waits for them, and re-layouts: 3.31 us -> 11.7 us
  transfers between devices with their start and end apart: 34 -> 15, of which waited for: 34 -> 6; matrix products, arithmetic and copies ran while one was open for 0% -> 11% of each run, Pallas kernels for 0% -> 0%
where the time goes in v1:
time: 171 us; the launch traced here: 170 us
  starting transfers between devices  64.1 us (37%)
  waiting for transfers between devices  56.6 us (33%)
  local copies, waits for them, and re-layouts  18.5 us (11%)
  between operations  13.9 us (8%)
  matrix products  13.6 us (8%)
  other arithmetic  3.3 us (2%)
    ppermute x8, starting transfers between devices, from_ahead(): lax.ppermute(value, 'wide', [(i, (i - 2 * chips) % size) for i in range(s...  47.8 us
    all_gather x1, waiting for transfers between devices, shards(): gathered = lax.all_gather(payload, 'narrow', axis=0, tiled=False)  34.3 us
    ppermute x8, waiting for transfers between devices, from_ahead(): lax.ppermute(value, 'wide', [(i, (i - 2 * chips) % size) for i in range(s...  21.2 us
    ppermute x6, starting transfers between devices, from_partner(): return lax.ppermute(value, 'wide', [(i, i ^ 1) for i in range(size)])  16.4 us
    unnamed x38, local copies, waits for them, and re-layouts  11.7 us
    dot_general x4, matrix products, squared_dots(): lax.dot_general(left, right, (((1,), (1,)), ((), ())), preferred_element_...  8.75 us
    dot_general x2, matrix products, pair_blocks(): lax.dot_general(rows, columns, (((1,), (0,)), ((), ())), precision=lax.Pr...  4.88 us
  transfers between devices with their start and end apart: 15, of which 6 were waited for; matrix products, arithmetic and copies ran while one was open for 11% of the time, Pallas kernels for 0%

profile of v1, /device:TPU:1, one launch (start us, length us, event | category | flops | bytes accessed | tf_op | source)
XLA Modules:
  0.0 170.0 jit_solution(15216498642575922461)
XLA Ops:
  6.5 0.7 broadcast_in_dim.8
  7.3 0.9 pad.4
  8.2 1.1 fusion.15
  9.3 0.8 pad_maximum_fusion.1
  10.1 5.6 %collective-permute-start.5 = (bf16[24,2001]{1,0:T(8,128)(2,1)S(1)}, bf16[24,2001]{1,0:T(8,128)(2,1)S(1)}, u32[]{:S(2)}, u32[]{:S(2)}) collective-permute-start(bf16[24,2001]{1,0:T(8,128)(2,1)S(1)} %pad.4), channel_id=1, source_target_pairs={{0,256},{8,264},{16,272},{24,280},{32,288},{40,296},{48,304},{56,3... | collective-permute-start | bytes 288152 | tf_op jit(solution)/shard_map/ppermute | solution.py:9
  15.8 8.6 %collective-permute-start.2 = (bf16[24,2001]{1,0:T(8,128)(2,1)S(1)}, bf16[24,2001]{1,0:T(8,128)(2,1)S(1)}, u32[]{:S(2)}, u32[]{:S(2)}) collective-permute-start(bf16[24,2001]{1,0:T(8,128)(2,1)S(1)} %pad.4), channel_id=1, source_target_pairs={{0,320},{8,328},{16,336},{24,344},{32,352},{40,360},{48,368},{56,3... | collective-permute-start | bytes 288152 | tf_op jit(solution)/shard_map/ppermute | solution.py:9
  24.4 13.3 %collective-permute-start.1 = (bf16[24,2001]{1,0:T(8,128)(2,1)S(1)}, bf16[24,2001]{1,0:T(8,128)(2,1)S(1)}, u32[]{:S(2)}, u32[]{:S(2)}) collective-permute-start(bf16[24,2001]{1,0:T(8,128)(2,1)S(1)} %pad.4), channel_id=1, source_target_pairs={{0,384},{8,392},{16,400},{24,408},{32,416},{40,424},{48,432},{56,4... | collective-permute-start | bytes 288152 | tf_op jit(solution)/shard_map/ppermute | solution.py:9
  37.6 5.2 %collective-permute-start = (bf16[24,2001]{1,0:T(8,128)(2,1)S(1)}, bf16[24,2001]{1,0:T(8,128)(2,1)S(1)}, u32[]{:S(2)}, u32[]{:S(2)}) collective-permute-start(bf16[24,2001]{1,0:T(8,128)(2,1)S(1)} %pad.4), channel_id=1, source_target_pairs={{0,448},{8,456},{16,464},{24,472},{32,480},{40,488},{48,496},{56,5... | collective-permute-start | bytes 288152 | tf_op jit(solution)/shard_map/ppermute | solution.py:9
  42.9 3.0 %collective-permute-done.1 = bf16[24,2001]{1,0:T(8,128)(2,1)S(1)} collective-permute-done((bf16[24,2001]{1,0:T(8,128)(2,1)S(1)}, bf16[24,2001]{1,0:T(8,128)(2,1)S(1)}, u32[]{:S(2)}, u32[]{:S(2)}) %collective-permute-start.1) | collective-permute-done | bytes 96080 | tf_op jit(solution)/shard_map/ppermute | solution.py:9
  45.9 6.8 %collective-permute-done = bf16[24,2001]{1,0:T(8,128)(2,1)S(1)} collective-permute-done((bf16[24,2001]{1,0:T(8,128)(2,1)S(1)}, bf16[24,2001]{1,0:T(8,128)(2,1)S(1)}, u32[]{:S(2)}, u32[]{:S(2)}) %collective-permute-start) | collective-permute-done | bytes 96080 | tf_op jit(solution)/shard_map/ppermute | solution.py:9
  52.8 2.9 %collective-permute-start.3 = (bf16[96,2001]{1,0:T(8,128)(2,1)S(1)}, bf16[96,2001]{1,0:T(8,128)(2,1)S(1)}, u32[]{:S(2)}, u32[]{:S(2)}) collective-permute-start(bf16[96,2001]{1,0:T(8,128)(2,1)S(1)} %get-tuple-element.12), channel_id=1, source_target_pairs={{0,496},{8,504},{16,0},{24,8},{32,16},{40,24},{48,32},{56,40},{64,... | collective-permute-start | bytes 1152584 | tf_op jit(solution)/shard_map/ppermute | solution.py:9
  55.8 2.3 %collective-permute-start.7 = (bf16[48,2001]{1,0:T(8,128)(2,1)S(1)}, bf16[48,2001]{1,0:T(8,128)(2,1)S(1)}, u32[]{:S(2)}, u32[]{:S(2)}) collective-permute-start(bf16[48,2001]{1,0:T(8,128)(2,1)S(1)} %pad_maximum_fusion.6), channel_id=1, source_target_pairs={{0,32},{8,40},{16,48},{24,56},{32,64},{40,72},{48,80},{56,88},{64,... | collective-permute-start | bytes 576296 | tf_op jit(solution)/shard_map/ppermute | solution.py:9
  58.1 7.9 %collective-permute-start.4 = (bf16[48,2001]{1,0:T(8,128)(2,1)S(1)}, bf16[48,2001]{1,0:T(8,128)(2,1)S(1)}, u32[]{:S(2)}, u32[]{:S(2)}) collective-permute-start(bf16[48,2001]{1,0:T(8,128)(2,1)S(1)} %pad_maximum_fusion.5), channel_id=1, source_target_pairs={{0,480},{8,488},{16,496},{24,504},{32,0},{40,8},{48,16},{56,24},{6... | collective-permute-start | bytes 576296 | tf_op jit(solution)/shard_map/ppermute | solution.py:9
  66.0 1.9 %collective-permute-start.6 = (bf16[96,2001]{1,0:T(8,128)(2,1)S(1)}, bf16[96,2001]{1,0:T(8,128)(2,1)S(1)}, u32[]{:S(2)}, u32[]{:S(2)}) collective-permute-start(bf16[96,2001]{1,0:T(8,128)(2,1)S(1)} %get-tuple-element.11), channel_id=1, source_target_pairs={{0,16},{8,24},{16,32},{24,40},{32,48},{40,56},{48,64},{56,72},{64,... | collective-permute-start | bytes 1152584 | tf_op jit(solution)/shard_map/ppermute | solution.py:9
  68.0 3.8 %collective-permute-done.4 = bf16[48,2001]{1,0:T(8,128)(2,1)S(1)} collective-permute-done((bf16[48,2001]{1,0:T(8,128)(2,1)S(1)}, bf16[48,2001]{1,0:T(8,128)(2,1)S(1)}, u32[]{:S(2)}, u32[]{:S(2)}) %collective-permute-start.4) | collective-permute-done | bytes 192128 | tf_op jit(solution)/shard_map/ppermute | solution.py:9
  71.9 7.5 %collective-permute-done.6 = bf16[96,2001]{1,0:T(8,128)(2,1)S(1)} collective-permute-done((bf16[96,2001]{1,0:T(8,128)(2,1)S(1)}, bf16[96,2001]{1,0:T(8,128)(2,1)S(1)}, u32[]{:S(2)}, u32[]{:S(2)}) %collective-permute-start.6) | collective-permute-done | bytes 384224 | tf_op jit(solution)/shard_map/ppermute | solution.py:9
  79.6 1.2 copy-done.1
  80.8 5.6 %collective-permute-start.8 = (bf16[120,2001]{1,0:T(8,128)(2,1)S(1)}, bf16[120,2001]{1,0:T(8,128)(2,1)S(1)}, u32[]{:S(2)}, u32[]{:S(2)}) collective-permute-start(bf16[120,2001]{1,0:T(8,128)(2,1)S(1)} %get-tuple-element.13), channel_id=1, source_target_pairs={{0,8},{8,0},{16,24},{24,16},{32,40},{40,32},{48,56},{56,48},{64,72... | collective-permute-start | bytes 1440728 | tf_op jit(solution)/shard_map/ppermute | solution.py:14
  86.5 1.9 %collective-permute-start.10 = (bf16[96,2001]{1,0:T(8,128)(2,1)S(1)}, bf16[96,2001]{1,0:T(8,128)(2,1)S(1)}, u32[]{:S(2)}, u32[]{:S(2)}) collective-permute-start(bf16[96,2001]{1,0:T(8,128)(2,1)S(1)} %pad_maximum_fusion.4), channel_id=1, source_target_pairs={{0,8},{8,0},{16,24},{24,16},{32,40},{40,32},{48,56},{56,48},{64,72... | collective-permute-start | bytes 1152584 | tf_op jit(solution)/shard_map/ppermute | solution.py:14
  88.5 2.4 %collective-permute-start.11 = (bf16[96,2001]{1,0:T(8,128)(2,1)S(1)}, bf16[96,2001]{1,0:T(8,128)(2,1)S(1)}, u32[]{:S(2)}, u32[]{:S(2)}) collective-permute-start(bf16[96,2001]{1,0:T(8,128)(2,1)S(1)} %collective-permute-done.6), channel_id=1, source_target_pairs={{0,8},{8,0},{16,24},{24,16},{32,40},{40,32},{48,56},{56,48},{64,72... | collective-permute-start | bytes 1152584 | tf_op jit(solution)/shard_map/ppermute | solution.py:14
  90.9 1.9 %collective-permute-start.9 = (bf16[96,2001]{1,0:T(8,128)(2,1)S(1)}, bf16[96,2001]{1,0:T(8,128)(2,1)S(1)}, u32[]{:S(2)}, u32[]{:S(2)}) collective-permute-start(bf16[96,2001]{1,0:T(8,128)(2,1)S(1)} %collective-permute-done.3), channel_id=1, source_target_pairs={{0,8},{8,0},{16,24},{24,16},{32,40},{40,32},{48,56},{56,48},{64,72... | collective-permute-start | bytes 1152584 | tf_op jit(solution)/shard_map/ppermute | solution.py:14
  92.8 0.6 slice_dynamic-update-slice_fusion.16
  93.5 1.0 collective-permute-done.9
  94.5 0.6 slice_dynamic-update-slice_fusion.15
  95.1 0.6 slice_dynamic-update-slice_fusion.14
  96.4 0.6 slice_dynamic-update-slice_fusion.12
  97.1 0.6 slice_dynamic-update-slice_fusion.11
  97.7 0.6 slice_dynamic-update-slice_fusion.10
  98.4 0.6 slice_dynamic-update-slice_fusion.9
  99.0 0.6 slice_dynamic-update-slice_fusion.8
  99.7 0.7 slice_dynamic-update-slice_fusion.7
  100.3 0.6 slice_dynamic-update-slice_fusion.6
  101.6 0.7 slice_dynamic-update-slice_fusion.4
  102.3 0.6 slice_dynamic-update-slice_fusion.3
  102.9 0.6 slice_dynamic-update-slice_fusion.2
  104.2 0.7 slice_dynamic-update-slice_fusion
  104.9 34.3 %all-gather.3.cloned.1.call-done = bf16[960,2001]{1,0:T(8,128)(2,1)} async-done(((bf16[120,2001]{1,0:T(8,128)(2,1)}), bf16[960,2001]{1,0:T(8,128)(2,1)}) %all-gather.3.cloned.1.call-update) | async-done | bytes 3841936 | tf_op jit(solution)/shard_map/all_gather | solution.py:48
  139.2 1.2 slice.180
  140.4 2.4 %slice.162 = bf16[8,96,2001]{2,1,0:T(8,128)(2,1)S(1)} slice(bf16[8,120,2001]{2,1,0:T(8,128)(2,1)} %bitcast.21), slice={[0:8], [0:96], [0:2001]} | slice | bytes 6147072 | tf_op jit(solution)/shard_map/slice | solution.py:49
  142.8 2.6 %collective-permute-start.12 = (bf16[192,2001]{1,0:T(8,128)(2,1)S(1)}, bf16[192,2001]{1,0:T(8,128)(2,1)S(1)}, u32[]{:S(2)}, u32[]{:S(2)}) collective-permute-start(bf16[192,2001]{1,0:T(8,128)(2,1)S(1)} %bitcast.30), channel_id=1, source_target_pairs={{0,8},{8,0},{16,24},{24,16},{32,40},{40,32},{48,56},{56,48},{64,72... | collective-permute-start | bytes 2305160 | tf_op jit(solution)/shard_map/ppermute | solution.py:14
  145.4 1.5 fusion.8
  147.3 2.9 %fusion.9 = f32[408,768]{1,0:T(8,128)S(1)} fusion(bf16[408,2001]{1,0:T(8,128)(2,1)} %slice_dynamic-update-slice_fusion, bf16[768,2001]{1,0:T(8,128)(2,1)S(1)} %bitcast.24), kind=kOutput, calls=%fused_computation.11 | convolution fusion | flops 1254629376 | bytes 5959728 | tf_op jit(solution)/shard_map/dot_general | solution.py:18
  150.2 1.2 fusion.14
  151.5 2.3 %fusion.4 = f32[792,192]{0,1:T(8,128)} fusion(f32[768,192]{0,1:T(8,128)S(1)} %fusion.14, f32[384,768]{1,0:T(8,128)S(1)} %constant_dynamic-slice_fusion, f32[408,768]{1,0:T(8,128)S(1)} %fusion.9), kind=kOutput, calls=%fused_computation.4 | convolution fusion | flops 701319168 | bytes 3631104 | tf_op jit(solution)/shard_map/dot_general | solution.py:23
  153.8 1.9 %collective-permute-start.13 = (f32[792,192]{0,1:T(8,128)}, f32[792,192]{0,1:T(8,128)}, u32[]{:S(2)}, u32[]{:S(2)}) collective-permute-start(f32[792,192]{0,1:T(8,128)} %fusion.4), channel_id=1, source_target_pairs={{0,8},{8,0},{16,24},{24,16},{32,40},{40,32},{48,56},{56,48},{64,72... | collective-permute-start | bytes 1824776 | tf_op jit(solution)/shard_map/ppermute | solution.py:14
  155.8 3.1 %fusion.13 = f32[768,192]{0,1:T(8,128)S(1)} fusion(bf16[768,2001]{1,0:T(8,128)(2,1)} %bitcast.26, bf16[192,2001]{1,0:T(8,128)(2,1)S(1)} %bitcast.31, f32[768]{0:T(1024)S(1)} %multiply_reduce_fusion), kind=kOutput, calls=%fused_computation.15 | convolution fusion | flops 590413824 | bytes 4434816 | tf_op jit(solution)/shard_map/dot_general | solution.py:18
  158.9 2.6 %fusion.10 = f32[792,192]{0,1:T(8,128)S(1)} fusion(f32[792,192]{0,1:T(8,128)} %collective-permute-done.13, f32[768,192]{0,1:T(8,128)S(1)} %fusion.13, f32[384,768]{1,0:T(8,128)S(1)} %constant_dynamic-slice_fusion.1, f32[408,768]{1,0:T(8,128)S(1)} %fusion.8), kind=kOutput, calls=%fused_computation.14 | convolution fusion | flops 701471232 | bytes 4239360 | tf_op jit(solution)/shard_map/dot_general | solution.py:23
  162.2 0.9 maximum_bitcast_fusion
  (50 shorter events, 3.4 us)
Async XLA Ops:
  6.5 132.6 %all-gather.3.cloned.1.call-start = ((), (), s32[]{:S(2)}) async-start(), calls=%async_computation | async-start | bytes 4423680 | tf_op jit(solution)/shard_map/all_gather | solution.py:48
  10.1 32.7 %collective-permute-start.5 = (bf16[24,2001]{1,0:T(8,128)(2,1)S(1)}, bf16[24,2001]{1,0:T(8,128)(2,1)S(1)}, u32[]{:S(2)}, u32[]{:S(2)}) collective-permute-start(bf16[24,2001]{1,0:T(8,128)(2,1)S(1)} %pad.4), channel_id=1, source_target_pairs={{0,256},{8,264},{16,272},{24,280},{32,288},{40,296},{48,304},{56,3... | collective-permute-start | bytes 288152 | tf_op jit(solution)/shard_map/ppermute | solution.py:9
  15.8 27.1 %collective-permute-start.2 = (bf16[24,2001]{1,0:T(8,128)(2,1)S(1)}, bf16[24,2001]{1,0:T(8,128)(2,1)S(1)}, u32[]{:S(2)}, u32[]{:S(2)}) collective-permute-start(bf16[24,2001]{1,0:T(8,128)(2,1)S(1)} %pad.4), channel_id=1, source_target_pairs={{0,320},{8,328},{16,336},{24,344},{32,352},{40,360},{48,368},{56,3... | collective-permute-start | bytes 288152 | tf_op jit(solution)/shard_map/ppermute | solution.py:9
  24.4 21.6 %collective-permute-start.1 = (bf16[24,2001]{1,0:T(8,128)(2,1)S(1)}, bf16[24,2001]{1,0:T(8,128)(2,1)S(1)}, u32[]{:S(2)}, u32[]{:S(2)}) collective-permute-start(bf16[24,2001]{1,0:T(8,128)(2,1)S(1)} %pad.4), channel_id=1, source_target_pairs={{0,384},{8,392},{16,400},{24,408},{32,416},{40,424},{48,432},{56,4... | collective-permute-start | bytes 288152 | tf_op jit(solution)/shard_map/ppermute | solution.py:9
  37.6 15.1 %collective-permute-start = (bf16[24,2001]{1,0:T(8,128)(2,1)S(1)}, bf16[24,2001]{1,0:T(8,128)(2,1)S(1)}, u32[]{:S(2)}, u32[]{:S(2)}) collective-permute-start(bf16[24,2001]{1,0:T(8,128)(2,1)S(1)} %pad.4), channel_id=1, source_target_pairs={{0,448},{8,456},{16,464},{24,472},{32,480},{40,488},{48,496},{56,5... | collective-permute-start | bytes 288152 | tf_op jit(solution)/shard_map/ppermute | solution.py:9
  52.8 15.2 %collective-permute-start.3 = (bf16[96,2001]{1,0:T(8,128)(2,1)S(1)}, bf16[96,2001]{1,0:T(8,128)(2,1)S(1)}, u32[]{:S(2)}, u32[]{:S(2)}) collective-permute-start(bf16[96,2001]{1,0:T(8,128)(2,1)S(1)} %get-tuple-element.12), channel_id=1, source_target_pairs={{0,496},{8,504},{16,0},{24,8},{32,16},{40,24},{48,32},{56,40},{64,... | collective-permute-start | bytes 1152584 | tf_op jit(solution)/shard_map/ppermute | solution.py:9
  55.8 23.7 %collective-permute-start.7 = (bf16[48,2001]{1,0:T(8,128)(2,1)S(1)}, bf16[48,2001]{1,0:T(8,128)(2,1)S(1)}, u32[]{:S(2)}, u32[]{:S(2)}) collective-permute-start(bf16[48,2001]{1,0:T(8,128)(2,1)S(1)} %pad_maximum_fusion.6), channel_id=1, source_target_pairs={{0,32},{8,40},{16,48},{24,56},{32,64},{40,72},{48,80},{56,88},{64,... | collective-permute-start | bytes 576296 | tf_op jit(solution)/shard_map/ppermute | solution.py:9
  58.1 13.8 %collective-permute-start.4 = (bf16[48,2001]{1,0:T(8,128)(2,1)S(1)}, bf16[48,2001]{1,0:T(8,128)(2,1)S(1)}, u32[]{:S(2)}, u32[]{:S(2)}) collective-permute-start(bf16[48,2001]{1,0:T(8,128)(2,1)S(1)} %pad_maximum_fusion.5), channel_id=1, source_target_pairs={{0,480},{8,488},{16,496},{24,504},{32,0},{40,8},{48,16},{56,24},{6... | collective-permute-start | bytes 576296 | tf_op jit(solution)/shard_map/ppermute | solution.py:9
  66.0 13.3 %collective-permute-start.6 = (bf16[96,2001]{1,0:T(8,128)(2,1)S(1)}, bf16[96,2001]{1,0:T(8,128)(2,1)S(1)}, u32[]{:S(2)}, u32[]{:S(2)}) collective-permute-start(bf16[96,2001]{1,0:T(8,128)(2,1)S(1)} %get-tuple-element.11), channel_id=1, source_target_pairs={{0,16},{8,24},{16,32},{24,40},{32,48},{40,56},{48,64},{56,72},{64,... | collective-permute-start | bytes 1152584 | tf_op jit(solution)/shard_map/ppermute | solution.py:9
  79.6 1.2 copy-start.1
  80.8 12.0 %collective-permute-start.8 = (bf16[120,2001]{1,0:T(8,128)(2,1)S(1)}, bf16[120,2001]{1,0:T(8,128)(2,1)S(1)}, u32[]{:S(2)}, u32[]{:S(2)}) collective-permute-start(bf16[120,2001]{1,0:T(8,128)(2,1)S(1)} %get-tuple-element.13), channel_id=1, source_target_pairs={{0,8},{8,0},{16,24},{24,16},{32,40},{40,32},{48,56},{56,48},{64,72... | collective-permute-start | bytes 1440728 | tf_op jit(solution)/shard_map/ppermute | solution.py:14
  86.5 8.6 %collective-permute-start.10 = (bf16[96,2001]{1,0:T(8,128)(2,1)S(1)}, bf16[96,2001]{1,0:T(8,128)(2,1)S(1)}, u32[]{:S(2)}, u32[]{:S(2)}) collective-permute-start(bf16[96,2001]{1,0:T(8,128)(2,1)S(1)} %pad_maximum_fusion.4), channel_id=1, source_target_pairs={{0,8},{8,0},{16,24},{24,16},{32,40},{40,32},{48,56},{56,48},{64,72... | collective-permute-start | bytes 1152584 | tf_op jit(solution)/shard_map/ppermute | solution.py:14
  88.5 7.3 %collective-permute-start.11 = (bf16[96,2001]{1,0:T(8,128)(2,1)S(1)}, bf16[96,2001]{1,0:T(8,128)(2,1)S(1)}, u32[]{:S(2)}, u32[]{:S(2)}) collective-permute-start(bf16[96,2001]{1,0:T(8,128)(2,1)S(1)} %collective-permute-done.6), channel_id=1, source_target_pairs={{0,8},{8,0},{16,24},{24,16},{32,40},{40,32},{48,56},{56,48},{64,72... | collective-permute-start | bytes 1152584 | tf_op jit(solution)/shard_map/ppermute | solution.py:14
  90.9 3.6 %collective-permute-start.9 = (bf16[96,2001]{1,0:T(8,128)(2,1)S(1)}, bf16[96,2001]{1,0:T(8,128)(2,1)S(1)}, u32[]{:S(2)}, u32[]{:S(2)}) collective-permute-start(bf16[96,2001]{1,0:T(8,128)(2,1)S(1)} %collective-permute-done.3), channel_id=1, source_target_pairs={{0,8},{8,0},{16,24},{24,16},{32,40},{40,32},{48,56},{56,48},{64,72... | collective-permute-start | bytes 1152584 | tf_op jit(solution)/shard_map/ppermute | solution.py:14
  140.4 5.0 %copy-start.2 = (bf16[408,2001]{1,0:T(8,128)(2,1)S(1)}, bf16[408,2001]{1,0:T(8,128)(2,1)}, u32[]{:S(2)}) copy-start(bf16[408,2001]{1,0:T(8,128)(2,1)} %copy-done.1) | copy-start | bytes 4898452
  142.8 7.4 %copy-start = (bf16[8,96,2001]{2,1,0:T(8,128)(2,1)}, bf16[8,96,2001]{2,1,0:T(8,128)(2,1)S(1)}, u32[]{:S(2)}) copy-start(bf16[8,96,2001]{2,1,0:T(8,128)(2,1)S(1)} %slice.162) | copy-start | bytes 9220612
  142.8 7.4 %collective-permute-start.12 = (bf16[192,2001]{1,0:T(8,128)(2,1)S(1)}, bf16[192,2001]{1,0:T(8,128)(2,1)S(1)}, u32[]{:S(2)}, u32[]{:S(2)}) collective-permute-start(bf16[192,2001]{1,0:T(8,128)(2,1)S(1)} %bitcast.30), channel_id=1, source_target_pairs={{0,8},{8,0},{16,24},{24,16},{32,40},{40,32},{48,56},{56,48},{64,72... | collective-permute-start | bytes 2305160 | tf_op jit(solution)/shard_map/ppermute | solution.py:14
  153.8 5.1 %collective-permute-start.13 = (f32[792,192]{0,1:T(8,128)}, f32[792,192]{0,1:T(8,128)}, u32[]{:S(2)}, u32[]{:S(2)}) collective-permute-start(f32[792,192]{0,1:T(8,128)} %fusion.4), channel_id=1, source_target_pairs={{0,8},{8,0},{16,24},{24,16},{32,40},{40,32},{48,56},{56,48},{64,72... | collective-permute-start | bytes 1824776 | tf_op jit(solution)/shard_map/ppermute | solution.py:14
Sparse Core Ops, SparseCore 0:
  86.6 52.5 all-gather.2

commit v2 on v1

v2 whole, which is shorter than its diff:
```python
import functools

import jax
import jax.numpy as jnp
from jax import lax
from jax.experimental import pallas as pl
from jax.experimental.pallas import tpu as pltpu
from jax.sharding import PartitionSpec as P

LANES = 2048
UNITS = (
    (0, True), (4, True), (8, True), (12, False), (16, True),
    (1, True), (5, True), (9, True), (13, False),
    (15, False), (11, False), (7, False), (3, True),
    (2, True), (6, True), (14, False), (10, False),
)


def permuted(value, move):
    wide, narrow = lax.axis_size("wide"), lax.axis_size("narrow")
    pairs = []
    for w in range(wide):
        for n in range(narrow):
            to_w, to_n = move(w, n)
            pairs.append((w * narrow + n, (to_w % wide) * narrow + to_n % narrow))
    return lax.ppermute(value, ("wide", "narrow"), pairs)


def by_chips(value, first, second):
    return permuted(value, lambda w, n: (w + 2 * (second if w % 2 else first), n))


def from_partner(value):
    return permuted(value, lambda w, n: (w ^ 1, n))


def gather_wide(unit, core, piece):
    four = by_chips(unit, -4, -12)
    across = by_chips(unit[:piece], -16, -16)
    eight = by_chips(four[:piece], -4, 4)
    got = from_partner(jnp.concatenate([four, eight, across], axis=0))
    sixteen = jnp.concatenate([across, got[3 * piece :]], axis=0)
    start = jnp.where(core == 0, unit, sixteen)
    stop = jnp.where(core == 0, sixteen, unit)
    bundle = jnp.concatenate([start, four, eight, got[2 * piece : 3 * piece], got[: 2 * piece]], axis=0)
    near = by_chips(bundle, -1, 1)
    two = by_chips(near[: 4 * piece], -1, 1)
    far = from_partner(near)
    two_far = from_partner(two)
    return bundle, stop, near, far, two, two_far


def products_kernel(piece, shards_x, rows_d, tile, width, env_count, *refs):
    gathered, points = refs[0], refs[1:7]
    own_ref, send_ref = refs[7:9]
    envs, rows, dots, columns, own, send, sems = refs[9:]
    count = len(UNITS) * 2 * piece
    block = 2 * shards_x * piece

    copies, at = [], 0
    for ref in points:
        size = ref.shape[0]
        copies.append(pltpu.make_async_copy(ref, rows.at[pl.ds(at, size)], sems.at[len(copies)]))
        at += size
    for i in range(shards_x):
        copies.append(
            pltpu.make_async_copy(
                gathered.at[i, pl.ds(rows_d, 4 * piece)],
                rows.at[pl.ds(at, 4 * piece)],
                sems.at[len(copies)],
            )
        )
        at += 4 * piece
    for i in range(shards_x):
        copies.append(
            pltpu.make_async_copy(
                gathered.at[i, pl.ds(0, rows_d)], envs.at[pl.ds(i * rows_d, rows_d)], sems.at[len(copies)]
            )
        )
    for copy in copies:
        copy.start()
    pick = (lax.broadcasted_iota(jnp.int32, (16, LANES), 1) == width) & (
        lax.broadcasted_iota(jnp.int32, (16, LANES), 0) == 0
    )
    rows[pl.ds(at, 16), :] = pick.astype(jnp.float32).astype(jnp.bfloat16)
    for copy in copies:
        copy.wait()

    total = rows.shape[0]
    step = total // 4
    for t in range(envs.shape[0] // tile):
        def some_dots(m, carry):
            part = pl.ds(pl.multiple_of(m * step, 16), step)
            dots[part, :] = lax.dot_general(
                rows[part, :],
                envs[pl.ds(t * tile, tile), :],
                (((1,), (1,)), ((), ())),
                preferred_element_type=jnp.float32,
            )
            return carry

        lax.fori_loop(0, 4, some_dots, 0)
        weights = dots[pl.ds(at, 8), :][:1] / env_count
        for i in range(shards_x):
            for which in range(2):
                for low in range(2):
                    source = count + i * 4 * piece + (2 * which + low) * piece
                    target = which * block + (low * shards_x + i) * piece
                    value = dots[pl.ds(source, piece), :]
                    columns[pl.ds(target, piece), :] = value * value / width * weights
        high, low_part = [], []
        for which in range(2):
            value = columns[pl.ds(which * block, block), :]
            top = value.astype(jnp.bfloat16)
            high.append(top)
            low_part.append((value - top.astype(jnp.float32)).astype(jnp.bfloat16))

        def some_products(m, carry):
            part = pl.ds(pl.multiple_of(m * (count // 3), 8), count // 3)
            value = dots[part, :]
            value = value * value / width
            top = value.astype(jnp.bfloat16)
            rest = (value - top.astype(jnp.float32)).astype(jnp.bfloat16)
            for which, target in ((0, own), (1, send)):
                result = 0
                for left, right in ((top, high[which]), (top, low_part[which]), (rest, high[which])):
                    result += lax.dot_general(
                        left, right, (((1,), (1,)), ((), ())), preferred_element_type=jnp.float32
                    )
                target[part, :] = result if t == 0 else target[part, :] + result
            return carry

        lax.fori_loop(0, 3, some_products, 0)

    for u, (distance, first_own) in enumerate(UNITS):
        for b in range(2):
            part = pl.ds((2 * u + b) * piece, piece)
            if first_own == (b == 0):
                own_ref[2 * distance] = own[part, :]
                if distance > 0:
                    send_ref[33 - 2 * distance] = send[part, :]
            else:
                if distance < 16:
                    own_ref[2 * distance + 1] = own[part, :]
                send_ref[32 - 2 * distance] = send[part, :]


def products(gathered, points, piece, rows_d, width, env_count):
    shards_x = gathered.shape[0]
    env_rows = shards_x * rows_d
    tile = 256 if env_rows % 256 == 0 else env_rows
    count = len(UNITS) * 2 * piece
    block = 2 * shards_x * piece
    total = count + 4 * shards_x * piece + 16
    shape = jax.ShapeDtypeStruct((33, piece, block), jnp.float32)
    anywhere = pl.BlockSpec(memory_space=pl.ANY)
    vmem = pl.BlockSpec(memory_space=pltpu.VMEM)
    flops = 2 * env_rows * (total * LANES + 6 * count * block)
    return pl.pallas_call(
        functools.partial(products_kernel, piece, shards_x, rows_d, tile, width, env_count),
        out_shape=(shape, shape),
        in_specs=[anywhere] * (1 + len(points)),
        out_specs=(vmem, vmem),
        scratch_shapes=[
            pltpu.VMEM((env_rows, LANES), jnp.bfloat16),
            pltpu.VMEM((total, LANES), jnp.bfloat16),
            pltpu.VMEM((total, tile), jnp.float32),
            pltpu.VMEM((2 * block, tile), jnp.float32),
            pltpu.VMEM((count, block), jnp.float32),
            pltpu.VMEM((count, block), jnp.float32),
            pltpu.SemaphoreType.DMA((len(points) + 2 * shards_x,)),
        ],
        compiler_params=pltpu.CompilerParams(vmem_limit_bytes=40 * 1024 * 1024),
        cost_estimate=pl.CostEstimate(flops=flops, bytes_accessed=10**7, transcendentals=0),
    )(gathered, *points)


def shards(descriptors, env_weights, sparse_points):
    core = lax.axis_index("wide") % 2
    narrow = lax.axis_size("narrow")
    wide = lax.axis_size("wide")
    shards_x = narrow // 2
    width = descriptors.shape[1]
    half = descriptors.shape[0] // 2
    env_count = descriptors.shape[0] * narrow
    piece = sparse_points.shape[0]

    mine = jnp.pad(sparse_points, ((0, 0), (0, LANES - width)))
    other = from_partner(mine)
    half_envs = lax.dynamic_slice_in_dim(
        jnp.concatenate(
            [descriptors, env_weights[:, None], jnp.zeros((2 * half, LANES - width - 1), descriptors.dtype)], axis=1
        ),
        core * half,
        half,
        0,
    )
    across_envs = permuted(
        half_envs, lambda w, n: (w + (wide // 2 if w % 2 else 0), n + shards_x)
    )
    unit = jnp.concatenate([mine, other], axis=0)
    across_unit = permuted(unit, lambda w, n: (w, n + shards_x))
    at_zero = lax.axis_index("narrow") < shards_x
    low = jnp.where(at_zero, unit, across_unit)
    high = jnp.where(at_zero, across_unit, unit)
    payload = jnp.concatenate(
        [half_envs, across_envs, low[:piece], high[:piece], low[piece:], high[piece:]], axis=0
    )
    payload, unit = lax.optimization_barrier((payload, unit))
    groups = [list(range(shards_x)), list(range(shards_x, narrow))]
    gathered = lax.all_gather(payload, "narrow", axis=0, tiled=False, axis_index_groups=groups)

    def none(_):
        return tuple(jnp.zeros((n * piece, LANES), unit.dtype) for n in (8, 2, 8, 8, 4, 4))

    points = lax.cond(
        1 + jnp.minimum(lax.axis_index("wide"), 0) > 0,
        lambda value: gather_wide(value, core, piece),
        none,
        unit,
    )
    gathered, points = lax.optimization_barrier((gathered, points))
    kept, sent = products(gathered, points, piece, 2 * half, width, env_count)
    total = kept + from_partner(sent)
    return jnp.where(core == 0, total, total[::-1])[None]


def solution(mesh):
    in_specs = (P("narrow", None), P("narrow"), P(("wide", "narrow"), None))
    out_specs = P("wide", None, "narrow", None)
    return jax.shard_map(shards, mesh=mesh, in_specs=in_specs, out_specs=out_specs, check_vma=False)
```

time: 171 us -> 135 us (0.79)
  waiting for transfers between devices: 56.6 us -> 39.1 us
  matrix products: 13.6 us -> 0 us
  Pallas kernels: 0 us -> 12.3 us
  local copies, waits for them, and re-layouts: 18.5 us -> 10.1 us
  starting transfers between devices: 64.1 us -> 56.9 us
    all_gather x1, waiting for transfers between devices: 34.3 us -> 0.01 us  [shards(): lax.all_gather(payload, 'narrow', axis=0, tiled=False, axis_index_groups=...]
    ppermute x14 -> x12, waiting for transfers between devices: 22.2 us -> 39.1 us  [permuted(): return lax.ppermute(value, ('wide', 'narrow'), pairs)]
    dot_general x6 -> x0, matrix products: 13.6 us -> none  [the longest x4 8.75 us: squared_dots(): lax.dot_general(left, right, (((1,), (1,)), ((), ())), preferred_element_...]
    pallas_call x0 -> x1, Pallas kernels: none -> 12.3 us  [products(): pl.pallas_call(functools.partial(products_kernel, piece, shards_x, rows_d...]
    unnamed x38 -> x9, local copies, waits for them, and re-layouts: 11.7 us -> 3.51 us
    ppermute x14 -> x12, starting transfers between devices: 64.1 us -> 56.9 us  [permuted(): return lax.ppermute(value, ('wide', 'narrow'), pairs)]
    slice x7 -> x4, local copies, waits for them, and re-layouts: 4.17 us -> 1.04 us  [the longest x1 1.02 us: gather_wide(): two = by_chips(near[:4 * piece], -1, 1)]
    concatenate x6 -> x2, other arithmetic: 2.05 us -> 0.04 us  [the longest x1 0.03 us: gather_wide(): got = from_partner(jnp.concatenate([four, eight, across], axis=0))]
  transfers between devices with their start and end apart: 15 -> 13, of which waited for: 6 -> 9; matrix products, arithmetic and copies ran while one was open for 11% -> 5% of each run, Pallas kernels for 0% -> 0%
where the time goes in v2:
time: 135 us; the launch traced here: 134 us
  starting transfers between devices  56.9 us (42%)
  waiting for transfers between devices  39.1 us (29%)
  between operations  13.6 us (10%)
  Pallas kernels  12.3 us (9%)
  local copies, waits for them, and re-layouts  10.1 us (7%)
  other arithmetic  1.92 us (1%)
    ppermute x12, starting transfers between devices, permuted(): return lax.ppermute(value, ('wide', 'narrow'), pairs)  56.9 us
    ppermute x12, waiting for transfers between devices, permuted(): return lax.ppermute(value, ('wide', 'narrow'), pairs)  39.1 us
    pallas_call x1, Pallas kernels, products(): pl.pallas_call(functools.partial(products_kernel, piece, shards_x, rows_d...  12.3 us
    unnamed x9, local copies, waits for them, and re-layouts  3.51 us
  transfers between devices with their start and end apart: 13, of which 9 were waited for; matrix products, arithmetic and copies ran while one was open for 5% of the time, Pallas kernels for 0%

profile of v2, /device:TPU:1, one launch (start us, length us, event | category | flops | bytes accessed | tf_op | source)
XLA Modules:
  0.0 134.0 jit_solution(110954202628677967)
XLA Ops:
  6.5 0.0 all-gather.3.cloned.1.call-start
  6.5 0.9 pad.4
  7.4 8.8 %collective-permute-start.9 = (bf16[24,2048]{1,0:T(8,128)(2,1)S(1)}, bf16[24,2048]{1,0:T(8,128)(2,1)S(1)}, u32[]{:S(2)}, u32[]{:S(2)}) collective-permute-start(bf16[24,2048]{1,0:T(8,128)(2,1)S(1)} %pad.4), channel_id=1, source_target_pairs={{0,8},{1,9},{2,10},{3,11},{4,12},{5,13},{6,14},{7,15},{8,0},{9,1},... | collective-permute-start | bytes 294920 | tf_op jit(solution)/shard_map/ppermute | solution.py:26
  16.3 0.7 broadcast_in_dim.12
  17.0 1.2 concatenate.18
  18.3 0.0 collective-permute-done.9
  18.3 1.9 %collective-permute-start.10 = (bf16[48,2048]{1,0:T(8,128)(2,1)S(1)}, bf16[48,2048]{1,0:T(8,128)(2,1)S(1)}, u32[]{:S(2)}, u32[]{:S(2)}) collective-permute-start(bf16[48,2048]{1,0:T(8,128)(2,1)S(1)} %pad_maximum_fusion.2), channel_id=1, source_target_pairs={{0,4},{1,5},{2,6},{3,7},{4,0},{5,1},{6,2},{7,3},{8,12},{9,13},{10,... | collective-permute-start | bytes 589832 | tf_op jit(solution)/shard_map/ppermute | solution.py:26
  20.2 0.1 constant_dynamic-update-slice_fusion.3
  20.3 1.9 %collective-permute-start.8 = (bf16[96,2048]{1,0:T(8,128)(2,1)S(1)}, bf16[96,2048]{1,0:T(8,128)(2,1)S(1)}, u32[]{:S(2)}, u32[]{:S(2)}) collective-permute-start(bf16[96,2048]{1,0:T(8,128)(2,1)S(1)} %get-tuple-element.46), channel_id=1, source_target_pairs={{0,4},{1,5},{2,6},{3,7},{4,0},{5,1},{6,2},{7,3},{8,268},{9,269},{1... | collective-permute-start | bytes 1179656 | tf_op jit(solution)/shard_map/ppermute | solution.py:26
  22.3 4.5 %collective-permute-done.10 = bf16[48,2048]{1,0:T(8,128)(2,1)S(1)} collective-permute-done((bf16[48,2048]{1,0:T(8,128)(2,1)S(1)}, bf16[48,2048]{1,0:T(8,128)(2,1)S(1)}, u32[]{:S(2)}, u32[]{:S(2)}) %collective-permute-start.10) | collective-permute-done | bytes 196640 | tf_op jit(solution)/shard_map/ppermute | solution.py:26
  26.7 0.1 broadcast_select_fusion.1
  26.8 3.3 %collective-permute-done.8 = bf16[96,2048]{1,0:T(8,128)(2,1)S(1)} collective-permute-done((bf16[96,2048]{1,0:T(8,128)(2,1)S(1)}, bf16[96,2048]{1,0:T(8,128)(2,1)S(1)}, u32[]{:S(2)}, u32[]{:S(2)}) %collective-permute-start.8) | collective-permute-done | bytes 393248 | tf_op jit(solution)/shard_map/ppermute | solution.py:26
  30.2 0.0 copy-start.1
  30.2 1.0 copy-done.1
  31.2 0.0 all-gather.3.cloned.1.call-update
  31.2 76.0 %conditional.1 = (bf16[192,2048]{1,0:T(8,128)(2,1)}, bf16[48,2048]{1,0:T(8,128)(2,1)S(1)}, bf16[192,2048]{1,0:T(8,128)(2,1)}, bf16[192,2048]{1,0:T(8,128)(2,1)},...) conditional(s32[]{:T(128)} %convert_element_type.5, () %tuple.16, (s32[]{:T(128)}, ...), branch_computations={%region_0.1_spmd, %region_1.2_spmd} | conditional | flops 1769472 | bytes 16712058 | solution.py:216
  31.2 6.1 %collective-permute-start.1 = (bf16[48,2048]{1,0:T(8,128)(2,1)S(1)}, bf16[48,2048]{1,0:T(8,128)(2,1)S(1)}, u32[]{:S(2)}, u32[]{:S(2)}) collective-permute-start(bf16[48,2048]{1,0:T(8,128)(2,1)S(1)} %get-tuple-element.10), channel_id=1, source_target_pairs={{0,448},{1,449},{2,450},{3,451},{4,452},{5,453},{6,454},{7,455},{8... | collective-permute-start | bytes 589832 | tf_op jit(solution)/shard_map/cond/branch_1_fun/ppermute | solution.py:26
  37.4 3.2 %collective-permute-start = (bf16[24,2048]{1,0:T(8,128)(2,1)S(1)}, bf16[24,2048]{1,0:T(8,128)(2,1)S(1)}, u32[]{:S(2)}, u32[]{:S(2)}) collective-permute-start(bf16[24,2048]{1,0:T(8,128)(2,1)S(1)} %slice.20), channel_id=1, source_target_pairs={{0,256},{1,257},{2,258},{3,259},{4,260},{5,261},{6,262},{7,263},{8... | collective-permute-start | bytes 294920 | tf_op jit(solution)/shard_map/cond/branch_1_fun/ppermute | solution.py:26
  40.6 2.5 %collective-permute-done.1 = bf16[48,2048]{1,0:T(8,128)(2,1)S(1)} collective-permute-done((bf16[48,2048]{1,0:T(8,128)(2,1)S(1)}, bf16[48,2048]{1,0:T(8,128)(2,1)S(1)}, u32[]{:S(2)}, u32[]{:S(2)}) %collective-permute-start.1) | collective-permute-done | bytes 196640 | tf_op jit(solution)/shard_map/cond/branch_1_fun/ppermute | solution.py:26
  43.1 11.5 %collective-permute-start.2 = (bf16[24,2048]{1,0:T(8,128)(2,1)S(1)}, bf16[24,2048]{1,0:T(8,128)(2,1)S(1)}, u32[]{:S(2)}, u32[]{:S(2)}) collective-permute-start(bf16[24,2048]{1,0:T(8,128)(2,1)S(1)} %slice.34), channel_id=1, source_target_pairs={{0,448},{1,449},{2,450},{3,451},{4,452},{5,453},{6,454},{7,455},{8... | collective-permute-start | bytes 294920 | tf_op jit(solution)/shard_map/cond/branch_1_fun/ppermute | solution.py:26
  54.6 0.0 collective-permute-done
  54.6 3.8 %collective-permute-done.2 = bf16[24,2048]{1,0:T(8,128)(2,1)S(1)} collective-permute-done((bf16[24,2048]{1,0:T(8,128)(2,1)S(1)}, bf16[24,2048]{1,0:T(8,128)(2,1)S(1)}, u32[]{:S(2)}, u32[]{:S(2)}) %collective-permute-start.2) | collective-permute-done | bytes 98336 | tf_op jit(solution)/shard_map/cond/branch_1_fun/ppermute | solution.py:26
  58.5 10.2 %collective-permute-start.3 = (bf16[96,2048]{1,0:T(8,128)(2,1)S(1)}, bf16[96,2048]{1,0:T(8,128)(2,1)S(1)}, u32[]{:S(2)}, u32[]{:S(2)}) collective-permute-start(bf16[96,2048]{1,0:T(8,128)(2,1)S(1)} %pad_maximum_fusion), channel_id=1, source_target_pairs={{0,8},{1,9},{2,10},{3,11},{4,12},{5,13},{6,14},{7,15},{8,0},{9,1},... | collective-permute-start | bytes 1179656 | tf_op jit(solution)/shard_map/cond/branch_1_fun/ppermute | solution.py:26
  68.6 1.3 collective-permute-done.3
  70.0 0.7 broadcast_select_fusion
  70.7 0.7 constant_dynamic-update-slice_fusion.1
  71.4 0.6 constant_dynamic-update-slice_fusion
  72.1 0.6 slice_dynamic-update-slice_fusion.1
  72.7 0.7 slice_dynamic-update-slice_fusion
  73.4 1.9 %collective-permute-start.4 = (bf16[192,2048]{1,0:T(8,128)(2,1)}, bf16[192,2048]{1,0:T(8,128)(2,1)}, u32[]{:S(2)}, u32[]{:S(2)}) collective-permute-start(bf16[192,2048]{1,0:T(8,128)(2,1)} %slice_dynamic-update-slice_fusion), channel_id=1, source_target_pairs={{0,496},{1,497},{2,498},{3,499},{4,500},{5,501},{6,502},{7,503},{8... | collective-permute-start | bytes 2359304 | tf_op jit(solution)/shard_map/cond/branch_1_fun/ppermute | solution.py:26
  75.3 14.7 %collective-permute-done.4 = bf16[192,2048]{1,0:T(8,128)(2,1)} collective-permute-done((bf16[192,2048]{1,0:T(8,128)(2,1)}, bf16[192,2048]{1,0:T(8,128)(2,1)}, u32[]{:S(2)}, u32[]{:S(2)}) %collective-permute-start.4) | collective-permute-done | bytes 786464 | tf_op jit(solution)/shard_map/cond/branch_1_fun/ppermute | solution.py:26
  90.1 1.0 slice.38
  91.1 1.9 %collective-permute-start.6 = (bf16[96,2048]{1,0:T(8,128)(2,1)S(1)}, bf16[96,2048]{1,0:T(8,128)(2,1)}, u32[]{:S(2)}, u32[]{:S(2)}) collective-permute-start(bf16[96,2048]{1,0:T(8,128)(2,1)S(1)} %slice.38), channel_id=1, source_target_pairs={{0,496},{1,497},{2,498},{3,499},{4,500},{5,501},{6,502},{7,503},{8... | collective-permute-start | bytes 1179656 | tf_op jit(solution)/shard_map/cond/branch_1_fun/ppermute | solution.py:26
  93.0 5.5 %collective-permute-start.5 = (bf16[192,2048]{1,0:T(8,128)(2,1)}, bf16[192,2048]{1,0:T(8,128)(2,1)}, u32[]{:S(2)}, u32[]{:S(2)}) collective-permute-start(bf16[192,2048]{1,0:T(8,128)(2,1)} %collective-permute-done.4), channel_id=1, source_target_pairs={{0,8},{1,9},{2,10},{3,11},{4,12},{5,13},{6,14},{7,15},{8,0},{9,1},... | collective-permute-start | bytes 2359304 | tf_op jit(solution)/shard_map/cond/branch_1_fun/ppermute | solution.py:26
  98.5 4.8 %collective-permute-done.6 = bf16[96,2048]{1,0:T(8,128)(2,1)} collective-permute-done((bf16[96,2048]{1,0:T(8,128)(2,1)S(1)}, bf16[96,2048]{1,0:T(8,128)(2,1)}, u32[]{:S(2)}, u32[]{:S(2)}) %collective-permute-start.6) | collective-permute-done | bytes 393248 | tf_op jit(solution)/shard_map/cond/branch_1_fun/ppermute | solution.py:26
  103.3 1.9 %collective-permute-start.7 = (bf16[96,2048]{1,0:T(8,128)(2,1)}, bf16[96,2048]{1,0:T(8,128)(2,1)}, u32[]{:S(2)}, u32[]{:S(2)}) collective-permute-start(bf16[96,2048]{1,0:T(8,128)(2,1)} %collective-permute-done.6), channel_id=1, source_target_pairs={{0,8},{1,9},{2,10},{3,11},{4,12},{5,13},{6,14},{7,15},{8,0},{9,1},... | collective-permute-start | bytes 1179656 | tf_op jit(solution)/shard_map/cond/branch_1_fun/ppermute | solution.py:26
  105.2 2.0 %collective-permute-done.7 = bf16[96,2048]{1,0:T(8,128)(2,1)} collective-permute-done((bf16[96,2048]{1,0:T(8,128)(2,1)}, bf16[96,2048]{1,0:T(8,128)(2,1)}, u32[]{:S(2)}, u32[]{:S(2)}) %collective-permute-start.7) | collective-permute-done | bytes 393248 | tf_op jit(solution)/shard_map/cond/branch_1_fun/ppermute | solution.py:26
  107.3 0.0 collective-permute-done.5
  107.3 0.0 all-gather.3.cloned.1.call-done
  107.3 0.0 copy-start
  107.3 2.3 %copy-done = bf16[1152,2048]{1,0:T(8,128)(2,1)S(1)} copy-done((bf16[1152,2048]{1,0:T(8,128)(2,1)S(1)}, bf16[1152,2048]{1,0:T(8,128)(2,1)}, u32[]{:S(2)}) %copy-start) | copy-done | bytes 4718616
  109.6 12.3 %shard_map.37 = (f32[33,24,192]{2,1,0:T(8,128)S(1)}, f32[33,24,192]{2,1,0:T(8,128)S(1)}) custom-call(bf16[4,288,2048]{2,1,0:T(8,128)(2,1)S(1)} %bitcast.3, bf16[192,2048]{1,0:T(8,128)(2,1)} %get-tuple-element.37.refs_1_, bf16[48,2048]{1,0:T(8,128)(2,1)S(1)} %get-tuple-element.38.refs_2_, bf16[192,2048]{1,0:T(8,128)(2,1)} %get-tuple-element.39.refs_3_, ...), custom_call_target="tpu_custom_call" | custom-call | flops 5269094400 | bytes 10000000 | tf_op jit(solution)/shard_map/pallas_call | solution.py:159
  121.9 2.0 %collective-permute-start.11 = (f32[33,24,192]{2,1,0:T(8,128)S(1)}, f32[33,24,192]{2,1,0:T(8,128)S(1)}, u32[]{:S(2)}, u32[]{:S(2)}) collective-permute-start(f32[33,24,192]{2,1,0:T(8,128)S(1)} %get-tuple-element.44), channel_id=1, source_target_pairs={{0,8},{1,9},{2,10},{3,11},{4,12},{5,13},{6,14},{7,15},{8,0},{9,1},... | collective-permute-start | bytes 1824776 | tf_op jit(solution)/shard_map/ppermute | solution.py:26
  123.9 2.2 %collective-permute-done.11 = f32[33,24,192]{2,1,0:T(8,128)S(1)} collective-permute-done((f32[33,24,192]{2,1,0:T(8,128)S(1)}, f32[33,24,192]{2,1,0:T(8,128)S(1)}, u32[]{:S(2)}, u32[]{:S(2)}) %collective-permute-start.11) | collective-permute-done | bytes 608288 | tf_op jit(solution)/shard_map/ppermute | solution.py:26
  126.1 0.1 add.14
  126.2 1.0 fusion
  (11 shorter events, 0.1 us)
Async XLA Ops:
  6.5 100.7 %all-gather.3.cloned.1.call-start = ((), (), s32[]{:S(2)}) async-start(), calls=%async_computation | async-start | bytes 5898240 | tf_op jit(solution)/shard_map/all_gather | solution.py:211
  7.4 10.8 %collective-permute-start.9 = (bf16[24,2048]{1,0:T(8,128)(2,1)S(1)}, bf16[24,2048]{1,0:T(8,128)(2,1)S(1)}, u32[]{:S(2)}, u32[]{:S(2)}) collective-permute-start(bf16[24,2048]{1,0:T(8,128)(2,1)S(1)} %pad.4), channel_id=1, source_target_pairs={{0,8},{1,9},{2,10},{3,11},{4,12},{5,13},{6,14},{7,15},{8,0},{9,1},... | collective-permute-start | bytes 294920 | tf_op jit(solution)/shard_map/ppermute | solution.py:26
  18.3 8.4 %collective-permute-start.10 = (bf16[48,2048]{1,0:T(8,128)(2,1)S(1)}, bf16[48,2048]{1,0:T(8,128)(2,1)S(1)}, u32[]{:S(2)}, u32[]{:S(2)}) collective-permute-start(bf16[48,2048]{1,0:T(8,128)(2,1)S(1)} %pad_maximum_fusion.2), channel_id=1, source_target_pairs={{0,4},{1,5},{2,6},{3,7},{4,0},{5,1},{6,2},{7,3},{8,12},{9,13},{10,... | collective-permute-start | bytes 589832 | tf_op jit(solution)/shard_map/ppermute | solution.py:26
  20.3 9.7 %collective-permute-start.8 = (bf16[96,2048]{1,0:T(8,128)(2,1)S(1)}, bf16[96,2048]{1,0:T(8,128)(2,1)S(1)}, u32[]{:S(2)}, u32[]{:S(2)}) collective-permute-start(bf16[96,2048]{1,0:T(8,128)(2,1)S(1)} %get-tuple-element.46), channel_id=1, source_target_pairs={{0,4},{1,5},{2,6},{3,7},{4,0},{5,1},{6,2},{7,3},{8,268},{9,269},{1... | collective-permute-start | bytes 1179656 | tf_op jit(solution)/shard_map/ppermute | solution.py:26
  30.2 1.0 copy-start.1
  31.2 11.8 %collective-permute-start.1 = (bf16[48,2048]{1,0:T(8,128)(2,1)S(1)}, bf16[48,2048]{1,0:T(8,128)(2,1)S(1)}, u32[]{:S(2)}, u32[]{:S(2)}) collective-permute-start(bf16[48,2048]{1,0:T(8,128)(2,1)S(1)} %get-tuple-element.10), channel_id=1, source_target_pairs={{0,448},{1,449},{2,450},{3,451},{4,452},{5,453},{6,454},{7,455},{8... | collective-permute-start | bytes 589832 | tf_op jit(solution)/shard_map/cond/branch_1_fun/ppermute | solution.py:26
  37.4 17.2 %collective-permute-start = (bf16[24,2048]{1,0:T(8,128)(2,1)S(1)}, bf16[24,2048]{1,0:T(8,128)(2,1)S(1)}, u32[]{:S(2)}, u32[]{:S(2)}) collective-permute-start(bf16[24,2048]{1,0:T(8,128)(2,1)S(1)} %slice.20), channel_id=1, source_target_pairs={{0,256},{1,257},{2,258},{3,259},{4,260},{5,261},{6,262},{7,263},{8... | collective-permute-start | bytes 294920 | tf_op jit(solution)/shard_map/cond/branch_1_fun/ppermute | solution.py:26
  43.1 15.3 %collective-permute-start.2 = (bf16[24,2048]{1,0:T(8,128)(2,1)S(1)}, bf16[24,2048]{1,0:T(8,128)(2,1)S(1)}, u32[]{:S(2)}, u32[]{:S(2)}) collective-permute-start(bf16[24,2048]{1,0:T(8,128)(2,1)S(1)} %slice.34), channel_id=1, source_target_pairs={{0,448},{1,449},{2,450},{3,451},{4,452},{5,453},{6,454},{7,455},{8... | collective-permute-start | bytes 294920 | tf_op jit(solution)/shard_map/cond/branch_1_fun/ppermute | solution.py:26
  58.5 11.5 %collective-permute-start.3 = (bf16[96,2048]{1,0:T(8,128)(2,1)S(1)}, bf16[96,2048]{1,0:T(8,128)(2,1)S(1)}, u32[]{:S(2)}, u32[]{:S(2)}) collective-permute-start(bf16[96,2048]{1,0:T(8,128)(2,1)S(1)} %pad_maximum_fusion), channel_id=1, source_target_pairs={{0,8},{1,9},{2,10},{3,11},{4,12},{5,13},{6,14},{7,15},{8,0},{9,1},... | collective-permute-start | bytes 1179656 | tf_op jit(solution)/shard_map/cond/branch_1_fun/ppermute | solution.py:26
  73.4 16.7 %collective-permute-start.4 = (bf16[192,2048]{1,0:T(8,128)(2,1)}, bf16[192,2048]{1,0:T(8,128)(2,1)}, u32[]{:S(2)}, u32[]{:S(2)}) collective-permute-start(bf16[192,2048]{1,0:T(8,128)(2,1)} %slice_dynamic-update-slice_fusion), channel_id=1, source_target_pairs={{0,496},{1,497},{2,498},{3,499},{4,500},{5,501},{6,502},{7,503},{8... | collective-permute-start | bytes 2359304 | tf_op jit(solution)/shard_map/cond/branch_1_fun/ppermute | solution.py:26
  91.1 12.2 %collective-permute-start.6 = (bf16[96,2048]{1,0:T(8,128)(2,1)S(1)}, bf16[96,2048]{1,0:T(8,128)(2,1)}, u32[]{:S(2)}, u32[]{:S(2)}) collective-permute-start(bf16[96,2048]{1,0:T(8,128)(2,1)S(1)} %slice.38), channel_id=1, source_target_pairs={{0,496},{1,497},{2,498},{3,499},{4,500},{5,501},{6,502},{7,503},{8... | collective-permute-start | bytes 1179656 | tf_op jit(solution)/shard_map/cond/branch_1_fun/ppermute | solution.py:26
  93.0 14.3 %collective-permute-start.5 = (bf16[192,2048]{1,0:T(8,128)(2,1)}, bf16[192,2048]{1,0:T(8,128)(2,1)}, u32[]{:S(2)}, u32[]{:S(2)}) collective-permute-start(bf16[192,2048]{1,0:T(8,128)(2,1)} %collective-permute-done.4), channel_id=1, source_target_pairs={{0,8},{1,9},{2,10},{3,11},{4,12},{5,13},{6,14},{7,15},{8,0},{9,1},... | collective-permute-start | bytes 2359304 | tf_op jit(solution)/shard_map/cond/branch_1_fun/ppermute | solution.py:26
  103.3 3.9 %collective-permute-start.7 = (bf16[96,2048]{1,0:T(8,128)(2,1)}, bf16[96,2048]{1,0:T(8,128)(2,1)}, u32[]{:S(2)}, u32[]{:S(2)}) collective-permute-start(bf16[96,2048]{1,0:T(8,128)(2,1)} %collective-permute-done.6), channel_id=1, source_target_pairs={{0,8},{1,9},{2,10},{3,11},{4,12},{5,13},{6,14},{7,15},{8,0},{9,1},... | collective-permute-start | bytes 1179656 | tf_op jit(solution)/shard_map/cond/branch_1_fun/ppermute | solution.py:26
  107.3 2.3 %copy-start = (bf16[1152,2048]{1,0:T(8,128)(2,1)S(1)}, bf16[1152,2048]{1,0:T(8,128)(2,1)}, u32[]{:S(2)}) copy-start(bf16[1152,2048]{1,0:T(8,128)(2,1)} %all-gather.3.cloned.1.call-done) | copy-start | bytes 14155780
  121.9 4.2 %collective-permute-start.11 = (f32[33,24,192]{2,1,0:T(8,128)S(1)}, f32[33,24,192]{2,1,0:T(8,128)S(1)}, u32[]{:S(2)}, u32[]{:S(2)}) collective-permute-start(f32[33,24,192]{2,1,0:T(8,128)S(1)} %get-tuple-element.44), channel_id=1, source_target_pairs={{0,8},{1,9},{2,10},{3,11},{4,12},{5,13},{6,14},{7,15},{8,0},{9,1},... | collective-permute-start | bytes 1824776 | tf_op jit(solution)/shard_map/ppermute | solution.py:26
Sparse Core Ops, SparseCore 0:
  31.3 60.3 all-gather.2

commit v3 on v2

--- a/solution.py
+++ b/solution.py
@@ -34,72 +34,93 @@
     return permuted(value, lambda w, n: (w ^ 1, n))
 
 
-def gather_wide(unit, core, piece):
+def gather_wide(unit, sixteen_mine, core, piece):
     four = by_chips(unit, -4, -12)
-    across = by_chips(unit[:piece], -16, -16)
-    eight = by_chips(four[:piece], -4, 4)
-    got = from_partner(jnp.concatenate([four, eight, across], axis=0))
-    sixteen = jnp.concatenate([across, got[3 * piece :]], axis=0)
+    sixteen = jnp.concatenate([sixteen_mine, from_partner(sixteen_mine)], axis=0)
     start = jnp.where(core == 0, unit, sixteen)
     stop = jnp.where(core == 0, sixteen, unit)
-    bundle = jnp.concatenate([start, four, eight, got[2 * piece : 3 * piece], got[: 2 * piece]], axis=0)
-    near = by_chips(bundle, -1, 1)
-    two = by_chips(near[: 4 * piece], -1, 1)
+    eight = by_chips(four[:piece], -4, 4)
+    near = by_chips(jnp.concatenate([start, four], axis=0), -1, 1)
+    got = from_partner(jnp.concatenate([four, eight], axis=0))
+    two = by_chips(near, -1, 1)
+    eights = jnp.concatenate([eight, got[2 * piece :]], axis=0)
+    twelve = got[: 2 * piece]
+    near_late = by_chips(jnp.concatenate([eights, twelve], axis=0), -1, 1)
     far = from_partner(near)
     two_far = from_partner(two)
-    return bundle, stop, near, far, two, two_far
+    far_late = from_partner(near_late)
+    return start, four, eights, twelve, stop, near, near_late, far, far_late, two, two_far
 
 
 def products_kernel(piece, shards_x, rows_d, tile, width, env_count, *refs):
-    gathered, points = refs[0], refs[1:7]
-    own_ref, send_ref = refs[7:9]
-    envs, rows, dots, columns, own, send, sems = refs[9:]
+    gathered, points = refs[0], refs[1:12]
+    own_ref, send_ref = refs[12:14]
+    envs, rows, dots, columns, own, send, sems = refs[14:]
     count = len(UNITS) * 2 * piece
     block = 2 * shards_x * piece
-
-    copies, at = [], 0
-    for ref in points:
-        size = ref.shape[0]
-        copies.append(pltpu.make_async_copy(ref, rows.at[pl.ds(at, size)], sems.at[len(copies)]))
-        at += size
+    at = count + 4 * shards_x * piece
+    tiles = envs.shape[0] // tile
+
+    def copied(source, target):
+        copies.append(pltpu.make_async_copy(source, target, sems.at[len(copies)]))
+        copies[-1].start()
+        return copies[-1]
+
+    def copied_envs(i):
+        return copied(gathered.at[i, pl.ds(0, rows_d)], envs.at[pl.ds(i * rows_d, rows_d)])
+
+    copies, row_copies, sizes = [], [], []
+    first = -(-tile // rows_d)
+    env_copies = [copied_envs(i) for i in range(first)]
+    place = 0
+    for group in ((0, 1, 2, 3, 4), (5, 6), (7, 8), (9, 10)):
+        row_copies.append([])
+        begin = place
+        for k in group:
+            size = points[k].shape[0]
+            row_copies[-1].append(copied(points[k], rows.at[pl.ds(place, size)]))
+            place += size
+        sizes.append(place - begin)
+    row_copies.append([])
     for i in range(shards_x):
-        copies.append(
-            pltpu.make_async_copy(
-                gathered.at[i, pl.ds(rows_d, 4 * piece)],
-                rows.at[pl.ds(at, 4 * piece)],
-                sems.at[len(copies)],
-            )
+        row_copies[-1].append(
+            copied(gathered.at[i, pl.ds(rows_d, 4 * piece)], rows.at[pl.ds(place, 4 * piece)])
         )
-        at += 4 * piece
-    for i in range(shards_x):
-        copies.append(
-            pltpu.make_async_copy(
-                gathered.at[i, pl.ds(0, rows_d)], envs.at[pl.ds(i * rows_d, rows_d)], sems.at[len(copies)]
-            )
-        )
-    for copy in copies:
-        copy.start()
+        place += 4 * piece
+    sizes.append(4 * shards_x * piece + 16)
+    late_copies = [copied_envs(i) for i in range(first, shards_x)]
     pick = (lax.broadcasted_iota(jnp.int32, (16, LANES), 1) == width) & (
         lax.broadcasted_iota(jnp.int32, (16, LANES), 0) == 0
     )
     rows[pl.ds(at, 16), :] = pick.astype(jnp.float32).astype(jnp.bfloat16)
-    for copy in copies:
-        copy.wait()
-
-    total = rows.shape[0]
-    step = total // 4
-    for t in range(envs.shape[0] // tile):
-        def some_dots(m, carry):
-            part = pl.ds(pl.multiple_of(m * step, 16), step)
-            dots[part, :] = lax.dot_general(
-                rows[part, :],
-                envs[pl.ds(t * tile, tile), :],
-                (((1,), (1,)), ((), ())),
-                preferred_element_type=jnp.float32,
-            )
-            return carry
-
-        lax.fori_loop(0, 4, some_dots, 0)
+
+    def dots_of(part, t):
+        dots[part, :] = lax.dot_general(
+            rows[part, :],
+            envs[pl.ds(t * tile, tile), :],
+            (((1,), (1,)), ((), ())),
+            preferred_element_type=jnp.float32,
+        )
+
+    step = rows.shape[0] // 4
+    for t in range(tiles):
+        if t == 0:
+            for copy in env_copies:
+                copy.wait()
+            place = 0
+            for waits, size in zip(row_copies, sizes):
+                for copy in waits:
+                    copy.wait()
+                dots_of(pl.ds(place, size), 0)
+                place += size
+            for copy in late_copies:
+                copy.wait()
+        else:
+            def some_dots(m, carry):
+                dots_of(pl.ds(pl.multiple_of(m * step, 16), step), t)
+                return carry
+
+            lax.fori_loop(0, 4, some_dots, 0)
         weights = dots[pl.ds(at, 8), :][:1] / env_count
         for i in range(shards_x):
             for which in range(2):
@@ -170,7 +191,7 @@
             pltpu.VMEM((count, block), jnp.float32),
             pltpu.SemaphoreType.DMA((len(points) + 2 * shards_x,)),
         ],
-        compiler_params=pltpu.CompilerParams(vmem_limit_bytes=40 * 1024 * 1024),
+        compiler_params=pltpu.CompilerParams(vmem_limit_bytes=60 * 1024 * 1024),
         cost_estimate=pl.CostEstimate(flops=flops, bytes_accessed=10**7, transcendentals=0),
     )(gathered, *points)
 
@@ -187,6 +208,8 @@
 
     mine = jnp.pad(sparse_points, ((0, 0), (0, LANES - width)))
     other = from_partner(mine)
+    across_mine = permuted(mine, lambda w, n: (w, n + shards_x))
+    unit = jnp.concatenate([mine, other], axis=0)
     half_envs = lax.dynamic_slice_in_dim(
         jnp.concatenate(
             [descriptors, env_weights[:, None], jnp.zeros((2 * half, LANES - width - 1), descriptors.dtype)], axis=1
@@ -198,26 +221,33 @@
     across_envs = permuted(
         half_envs, lambda w, n: (w + (wide // 2 if w % 2 else 0), n + shards_x)
     )
-    unit = jnp.concatenate([mine, other], axis=0)
-    across_unit = permuted(unit, lambda w, n: (w, n + shards_x))
+    across_other = from_partner(across_mine)
+    sixteen_mine = by_chips(mine, -16, -16)
     at_zero = lax.axis_index("narrow") < shards_x
-    low = jnp.where(at_zero, unit, across_unit)
-    high = jnp.where(at_zero, across_unit, unit)
     payload = jnp.concatenate(
-        [half_envs, across_envs, low[:piece], high[:piece], low[piece:], high[piece:]], axis=0
-    )
-    payload, unit = lax.optimization_barrier((payload, unit))
+        [
+            half_envs,
+            across_envs,
+            jnp.where(at_zero, mine, across_mine),
+            jnp.where(at_zero, across_mine, mine),
+            jnp.where(at_zero, other, across_other),
+            jnp.where(at_zero, across_other, other),
+        ],
+        axis=0,
+    )
+    payload, unit, sixteen_mine = lax.optimization_barrier((payload, unit, sixteen_mine))
     groups = [list(range(shards_x)), list(range(shards_x, narrow))]
     gathered = lax.all_gather(payload, "narrow", axis=0, tiled=False, axis_index_groups=groups)
 
-    def none(_):
-        return tuple(jnp.zeros((n * piece, LANES), unit.dtype) for n in (8, 2, 8, 8, 4, 4))
+    def none(*_):
+        return tuple(jnp.zeros((n * piece, LANES), unit.dtype) for n in (2, 2, 2, 2, 2, 4, 4, 4, 4, 4, 4))
 
     points = lax.cond(
         1 + jnp.minimum(lax.axis_index("wide"), 0) > 0,
-        lambda value: gather_wide(value, core, piece),
+        lambda *values: gather_wide(*values, core, piece),
         none,
         unit,
+        sixteen_mine,
     )
     gathered, points = lax.optimization_barrier((gathered, points))
     kept, sent = products(gathered, points, piece, 2 * half, width, env_count)

time: 135 us -> 125 us (0.926)
  waiting for transfers between devices: 39.1 us -> 14.9 us
  starting transfers between devices: 56.9 us -> 73.1 us
  local copies, waits for them, and re-layouts: 10.1 us -> 2.89 us
  other arithmetic: 1.92 us -> 4.98 us
  Pallas kernels: 12.3 us -> 14.6 us
    ppermute x12 -> x16, waiting for transfers between devices: 39.1 us -> 14.9 us  [permuted(): return lax.ppermute(value, ('wide', 'narrow'), pairs)]
    ppermute x12 -> x16, starting transfers between devices: 56.9 us -> 73.1 us  [permuted(): return lax.ppermute(value, ('wide', 'narrow'), pairs)]
    unnamed x9 -> x6, local copies, waits for them, and re-layouts: 3.51 us -> 0.12 us
    pallas_call x1, Pallas kernels: 12.3 us -> 14.6 us  [products(): pl.pallas_call(functools.partial(products_kernel, piece, shards_x, rows_d...]
    cond x3 -> x5, local copies, waits for them, and re-layouts: 1.98 us -> 0.02 us
    concatenate x1 -> x5, other arithmetic: 0.03 us -> 1.97 us  [the longest x1 0.95 us: gather_wide(): near = by_chips(jnp.concatenate([start, four], axis=0), -1, 1)]
  transfers between devices with their start and end apart: 13 -> 17, of which waited for: 9 -> 7; matrix products, arithmetic and copies ran while one was open for 5% -> 3% of each run, Pallas kernels for 0% -> 0%
where the time goes in v3:
time: 125 us; the launch traced here: 124 us
  starting transfers between devices  73.1 us (58%)
  waiting for transfers between devices  14.9 us (12%)
  Pallas kernels  14.6 us (12%)
  between operations  13.6 us (11%)
  other arithmetic  4.98 us (4%)
  local copies, waits for them, and re-layouts  2.89 us (2%)
    ppermute x16, starting transfers between devices, permuted(): return lax.ppermute(value, ('wide', 'narrow'), pairs)  73.1 us
    ppermute x16, waiting for transfers between devices, permuted(): return lax.ppermute(value, ('wide', 'narrow'), pairs)  14.9 us
    pallas_call x1, Pallas kernels, products(): pl.pallas_call(functools.partial(products_kernel, piece, shards_x, rows_d...  14.6 us
  transfers between devices with their start and end apart: 17, of which 7 were waited for; matrix products, arithmetic and copies ran while one was open for 3% of the time, Pallas kernels for 0%

profile of v3, /device:TPU:1, one launch (start us, length us, event | category | flops | bytes accessed | tf_op | source)
XLA Modules:
  0.0 124.2 jit_solution(4619928792100090769)
XLA Ops:
  6.5 0.7 broadcast_in_dim.12
  7.3 0.0 copy-start.3
  7.3 1.3 %concatenate.25 = bf16[192,2048]{1,0:T(8,128)(2,1)S(1)} concatenate(bf16[192,2000]{1,0:T(8,128)(2,1)} %param.5, bf16[192,1]{1,0:T(8,128)(2,1)S(1)} %broadcast_in_dim.12, bf16[192,47]{1,0:T(8,128)(2,1)S(1)} %broadcast_in_dim.10), dimensions={1} | concatenate | bytes 1572864 | tf_op jit(solution)/shard_map/concatenate | solution.py:214
  8.6 0.1 constant_dynamic-update-slice_fusion.3
  8.7 5.5 %collective-permute-start.10 = (bf16[96,2048]{1,0:T(8,128)(2,1)S(1)}, bf16[96,2048]{1,0:T(8,128)(2,1)S(1)}, u32[]{:S(2)}, u32[]{:S(2)}) collective-permute-start(bf16[96,2048]{1,0:T(8,128)(2,1)S(1)} %get-tuple-element.71), channel_id=1, source_target_pairs={{0,4},{1,5},{2,6},{3,7},{4,0},{5,1},{6,2},{7,3},{8,268},{9,269},{1... | collective-permute-start | bytes 1179656 | tf_op jit(solution)/shard_map/ppermute | solution.py:26
  14.2 1.9 %collective-permute-start.11 = (bf16[24,2048]{1,0:T(8,128)(2,1)S(1)}, bf16[24,2048]{1,0:T(8,128)(2,1)S(1)}, u32[]{:S(2)}, u32[]{:S(2)}) collective-permute-start(bf16[24,2048]{1,0:T(8,128)(2,1)S(1)} %pad.4), channel_id=1, source_target_pairs={{0,4},{1,5},{2,6},{3,7},{4,0},{5,1},{6,2},{7,3},{8,12},{9,13},{10,... | collective-permute-start | bytes 294920 | tf_op jit(solution)/shard_map/ppermute | solution.py:26
  16.1 7.2 %collective-permute-start.12 = (bf16[24,2048]{1,0:T(8,128)(2,1)S(1)}, bf16[24,2048]{1,0:T(8,128)(2,1)S(1)}, u32[]{:S(2)}, u32[]{:S(2)}) collective-permute-start(bf16[24,2048]{1,0:T(8,128)(2,1)S(1)} %pad.4), channel_id=1, source_target_pairs={{0,8},{1,9},{2,10},{3,11},{4,12},{5,13},{6,14},{7,15},{8,0},{9,1},... | collective-permute-start | bytes 294920 | tf_op jit(solution)/shard_map/ppermute | solution.py:26
  23.4 1.9 %collective-permute-start.14 = (bf16[24,2048]{1,0:T(8,128)(2,1)S(1)}, bf16[24,2048]{1,0:T(8,128)(2,1)S(1)}, u32[]{:S(2)}, u32[]{:S(2)}) collective-permute-start(bf16[24,2048]{1,0:T(8,128)(2,1)S(1)} %pad.4), channel_id=1, source_target_pairs={{0,256},{1,257},{2,258},{3,259},{4,260},{5,261},{6,262},{7,263},{8... | collective-permute-start | bytes 294920 | tf_op jit(solution)/shard_map/ppermute | solution.py:26
  25.3 0.0 collective-permute-done.11
  25.3 2.9 %collective-permute-start.13 = (bf16[24,2048]{1,0:T(8,128)(2,1)S(1)}, bf16[24,2048]{1,0:T(8,128)(2,1)S(1)}, u32[]{:S(2)}, u32[]{:S(2)}) collective-permute-start(bf16[24,2048]{1,0:T(8,128)(2,1)S(1)} %collective-permute-done.11), channel_id=1, source_target_pairs={{0,8},{1,9},{2,10},{3,11},{4,12},{5,13},{6,14},{7,15},{8,0},{9,1},... | collective-permute-start | bytes 294920 | tf_op jit(solution)/shard_map/ppermute | solution.py:26
  28.2 0.0 collective-permute-done.12
  28.2 0.0 collective-permute-done.10
  28.3 0.8 collective-permute-done.13
  29.2 2.0 %collective-permute-done.14 = bf16[24,2048]{1,0:T(8,128)(2,1)S(1)} collective-permute-done((bf16[24,2048]{1,0:T(8,128)(2,1)S(1)}, bf16[24,2048]{1,0:T(8,128)(2,1)S(1)}, u32[]{:S(2)}, u32[]{:S(2)}) %collective-permute-start.14) | collective-permute-done | bytes 98336 | tf_op jit(solution)/shard_map/ppermute | solution.py:26
  31.2 0.0 all-gather.3.cloned.1.call-update
  31.2 64.9 %conditional.1 = (bf16[48,2048]{1,0:T(8,128)(2,1)}, bf16[48,2048]{1,0:T(8,128)(2,1)S(1)}, bf16[48,2048]{1,0:T(8,128)(2,1)S(1)}, bf16[48,2048]{1,0:T(8,128)(2,1)}...) conditional(s32[]{:T(128)} %convert_element_type.5, () %tuple.16, ...), branch_computations={%region_0.1_spmd, %region_1.2_spmd} | conditional | flops 3145729 | bytes 18285098 | solution.py:245
  31.2 6.2 %collective-permute-start.1 = (bf16[48,2048]{1,0:T(8,128)(2,1)S(1)}, bf16[48,2048]{1,0:T(8,128)(2,1)S(1)}, u32[]{:S(2)}, u32[]{:S(2)}) collective-permute-start(bf16[48,2048]{1,0:T(8,128)(2,1)S(1)} %get-tuple-element.12), channel_id=1, source_target_pairs={{0,448},{1,449},{2,450},{3,451},{4,452},{5,453},{6,454},{7,455},{8... | collective-permute-start | bytes 589832 | tf_op jit(solution)/shard_map/cond/branch_1_fun/ppermute | solution.py:26
  37.4 6.5 %collective-permute-start = (bf16[24,2048]{1,0:T(8,128)(2,1)S(1)}, bf16[24,2048]{1,0:T(8,128)(2,1)S(1)}, u32[]{:S(2)}, u32[]{:S(2)}) collective-permute-start(bf16[24,2048]{1,0:T(8,128)(2,1)S(1)} %get-tuple-element.13), channel_id=1, source_target_pairs={{0,8},{1,9},{2,10},{3,11},{4,12},{5,13},{6,14},{7,15},{8,0},{9,1},... | collective-permute-start | bytes 294920 | tf_op jit(solution)/shard_map/cond/branch_1_fun/ppermute | solution.py:26
  43.9 0.9 collective-permute-done
  44.9 0.0 collective-permute-done.1
  44.9 0.0 copy-start
  44.9 9.7 %collective-permute-start.2 = (bf16[24,2048]{1,0:T(8,128)(2,1)S(1)}, bf16[24,2048]{1,0:T(8,128)(2,1)S(1)}, u32[]{:S(2)}, u32[]{:S(2)}) collective-permute-start(bf16[24,2048]{1,0:T(8,128)(2,1)S(1)} %slice.9), channel_id=1, source_target_pairs={{0,448},{1,449},{2,450},{3,451},{4,452},{5,453},{6,454},{7,455},{8... | collective-permute-start | bytes 294920 | tf_op jit(solution)/shard_map/cond/branch_1_fun/ppermute | solution.py:26
  54.6 0.7 broadcast_select_fusion
  55.3 3.2 %collective-permute-done.2 = bf16[24,2048]{1,0:T(8,128)(2,1)S(1)} collective-permute-done((bf16[24,2048]{1,0:T(8,128)(2,1)S(1)}, bf16[24,2048]{1,0:T(8,128)(2,1)S(1)}, u32[]{:S(2)}, u32[]{:S(2)}) %collective-permute-start.2) | collective-permute-done | bytes 98336 | tf_op jit(solution)/shard_map/cond/branch_1_fun/ppermute | solution.py:26
  58.5 3.3 %collective-permute-start.3 = (bf16[72,2048]{1,0:T(8,128)(2,1)S(1)}, bf16[72,2048]{1,0:T(8,128)(2,1)S(1)}, u32[]{:S(2)}, u32[]{:S(2)}) collective-permute-start(bf16[72,2048]{1,0:T(8,128)(2,1)S(1)} %pad_maximum_fusion.2), channel_id=1, source_target_pairs={{0,8},{1,9},{2,10},{3,11},{4,12},{5,13},{6,14},{7,15},{8,0},{9,1},... | collective-permute-start | bytes 884744 | tf_op jit(solution)/shard_map/cond/branch_1_fun/ppermute | solution.py:26
  61.9 1.0 pad_maximum_fusion
  62.8 0.0 copy-done
  62.8 7.5 %collective-permute-start.4 = (bf16[96,2048]{1,0:T(8,128)(2,1)S(1)}, bf16[96,2048]{1,0:T(8,128)(2,1)}, u32[]{:S(2)}, u32[]{:S(2)}) collective-permute-start(bf16[96,2048]{1,0:T(8,128)(2,1)S(1)} %pad_maximum_fusion), channel_id=1, source_target_pairs={{0,496},{1,497},{2,498},{3,499},{4,500},{5,501},{6,502},{7,503},{8... | collective-permute-start | bytes 1179656 | tf_op jit(solution)/shard_map/cond/branch_1_fun/ppermute | solution.py:26
  70.4 0.0 copy-start.1
  70.4 0.0 collective-permute-done.3
  70.4 0.7 slice.11
  71.1 1.0 pad_maximum_fusion.1
  72.1 1.9 %collective-permute-start.5 = (bf16[96,2048]{1,0:T(8,128)(2,1)S(1)}, bf16[96,2048]{1,0:T(8,128)(2,1)}, u32[]{:S(2)}, u32[]{:S(2)}) collective-permute-start(bf16[96,2048]{1,0:T(8,128)(2,1)S(1)} %pad_maximum_fusion.1), channel_id=1, source_target_pairs={{0,496},{1,497},{2,498},{3,499},{4,500},{5,501},{6,502},{7,503},{8... | collective-permute-start | bytes 1179656 | tf_op jit(solution)/shard_map/cond/branch_1_fun/ppermute | solution.py:26
  74.0 4.2 %collective-permute-done.4 = bf16[96,2048]{1,0:T(8,128)(2,1)} collective-permute-done((bf16[96,2048]{1,0:T(8,128)(2,1)S(1)}, bf16[96,2048]{1,0:T(8,128)(2,1)}, u32[]{:S(2)}, u32[]{:S(2)}) %collective-permute-start.4) | collective-permute-done | bytes 393248 | tf_op jit(solution)/shard_map/cond/branch_1_fun/ppermute | solution.py:26
  78.2 1.9 %collective-permute-start.8 = (bf16[96,2048]{1,0:T(8,128)(2,1)}, bf16[96,2048]{1,0:T(8,128)(2,1)}, u32[]{:S(2)}, u32[]{:S(2)}) collective-permute-start(bf16[96,2048]{1,0:T(8,128)(2,1)} %collective-permute-done.4), channel_id=1, source_target_pairs={{0,496},{1,497},{2,498},{3,499},{4,500},{5,501},{6,502},{7,503},{8... | collective-permute-start | bytes 1179656 | tf_op jit(solution)/shard_map/cond/branch_1_fun/ppermute | solution.py:26
  80.1 8.7 %collective-permute-start.6 = (bf16[96,2048]{1,0:T(8,128)(2,1)}, bf16[96,2048]{1,0:T(8,128)(2,1)}, u32[]{:S(2)}, u32[]{:S(2)}) collective-permute-start(bf16[96,2048]{1,0:T(8,128)(2,1)} %collective-permute-done.4), channel_id=1, source_target_pairs={{0,8},{1,9},{2,10},{3,11},{4,12},{5,13},{6,14},{7,15},{8,0},{9,1},... | collective-permute-start | bytes 1179656 | tf_op jit(solution)/shard_map/cond/branch_1_fun/ppermute | solution.py:26
  88.9 0.0 collective-permute-done.5
  88.9 1.9 %collective-permute-start.7 = (bf16[96,2048]{1,0:T(8,128)(2,1)}, bf16[96,2048]{1,0:T(8,128)(2,1)}, u32[]{:S(2)}, u32[]{:S(2)}) collective-permute-start(bf16[96,2048]{1,0:T(8,128)(2,1)} %collective-permute-done.5), channel_id=1, source_target_pairs={{0,8},{1,9},{2,10},{3,11},{4,12},{5,13},{6,14},{7,15},{8,0},{9,1},... | collective-permute-start | bytes 1179656 | tf_op jit(solution)/shard_map/cond/branch_1_fun/ppermute | solution.py:26
  90.8 0.0 collective-permute-done.8
  90.8 3.6 %collective-permute-start.9 = (bf16[96,2048]{1,0:T(8,128)(2,1)}, bf16[96,2048]{1,0:T(8,128)(2,1)}, u32[]{:S(2)}, u32[]{:S(2)}) collective-permute-start(bf16[96,2048]{1,0:T(8,128)(2,1)} %collective-permute-done.8), channel_id=1, source_target_pairs={{0,8},{1,9},{2,10},{3,11},{4,12},{5,13},{6,14},{7,15},{8,0},{9,1},... | collective-permute-start | bytes 1179656 | tf_op jit(solution)/shard_map/cond/branch_1_fun/ppermute | solution.py:26
  94.5 0.0 collective-permute-done.6
  94.5 0.0 collective-permute-done.7
  94.5 1.6 %collective-permute-done.9 = bf16[96,2048]{1,0:T(8,128)(2,1)} collective-permute-done((bf16[96,2048]{1,0:T(8,128)(2,1)}, bf16[96,2048]{1,0:T(8,128)(2,1)}, u32[]{:S(2)}, u32[]{:S(2)}) %collective-permute-start.9) | collective-permute-done | bytes 393248 | tf_op jit(solution)/shard_map/cond/branch_1_fun/ppermute | solution.py:26
  96.1 14.6 %shard_map.37 = (f32[33,24,192]{2,1,0:T(8,128)}, f32[33,24,192]{2,1,0:T(8,128)}) custom-call(bf16[4,288,2048]{2,1,0:T(8,128)(2,1)} %bitcast.3, bf16[48,2048]{1,0:T(8,128)(2,1)} %get-tuple-element.57.refs_1_, bf16[48,2048]{1,0:T(8,128)(2,1)S(1)} %get-tuple-element.58.refs_2_, bf16[48,2048]{1,0:T(8,128)(2,1)S(1)} %get-tuple-element.59.refs_3_, ...), custom_call_target="tpu_custom_call" | custom-call | flops 5269094400 | bytes 10000000 | tf_op jit(solution)/shard_map/pallas_call | solution.py:180
  110.8 2.3 %collective-permute-start.15 = (f32[33,24,192]{2,1,0:T(8,128)}, f32[33,24,192]{2,1,0:T(8,128)S(1)}, u32[]{:S(2)}, u32[]{:S(2)}) collective-permute-start(f32[33,24,192]{2,1,0:T(8,128)} %get-tuple-element.69), channel_id=1, source_target_pairs={{0,8},{1,9},{2,10},{3,11},{4,12},{5,13},{6,14},{7,15},{8,0},{9,1},... | collective-permute-start | bytes 1824776 | tf_op jit(solution)/shard_map/ppermute | solution.py:26
  113.1 2.1 %collective-permute-done.15 = f32[33,24,192]{2,1,0:T(8,128)S(1)} collective-permute-done((f32[33,24,192]{2,1,0:T(8,128)}, f32[33,24,192]{2,1,0:T(8,128)S(1)}, u32[]{:S(2)}, u32[]{:S(2)}) %collective-permute-start.15) | collective-permute-done | bytes 608288 | tf_op jit(solution)/shard_map/ppermute | solution.py:26
  115.2 1.2 %add.14 = f32[33,24,192]{2,1,0:T(8,128)S(1)} add(f32[33,24,192]{2,1,0:T(8,128)} %get-tuple-element.68, f32[33,24,192]{2,1,0:T(8,128)S(1)} %collective-permute-done.15) | non-fusion elementwise | flops 152064 | bytes 1824768 | tf_op jit(solution)/shard_map/add | solution.py:254
  116.4 1.0 fusion
  (20 shorter events, 0.3 us)
Async XLA Ops:
  6.5 89.6 %all-gather.3.cloned.1.call-start = ((), (), s32[]{:S(2)}) async-start(), calls=%async_computation | async-start | bytes 5898240 | tf_op jit(solution)/shard_map/all_gather | solution.py:240
  7.3 6.9 %copy-start.3 = (bf16[24,2000]{1,0:T(8,128)(2,1)S(1)}, bf16[24,2000]{1,0:T(8,128)(2,1)}, u32[]{:S(2)}) copy-start(bf16[24,2000]{1,0:T(8,128)(2,1)} %param.7) | copy-start | bytes 288004
  8.7 19.5 %collective-permute-start.10 = (bf16[96,2048]{1,0:T(8,128)(2,1)S(1)}, bf16[96,2048]{1,0:T(8,128)(2,1)S(1)}, u32[]{:S(2)}, u32[]{:S(2)}) collective-permute-start(bf16[96,2048]{1,0:T(8,128)(2,1)S(1)} %get-tuple-element.71), channel_id=1, source_target_pairs={{0,4},{1,5},{2,6},{3,7},{4,0},{5,1},{6,2},{7,3},{8,268},{9,269},{1... | collective-permute-start | bytes 1179656 | tf_op jit(solution)/shard_map/ppermute | solution.py:26
  14.2 11.1 %collective-permute-start.11 = (bf16[24,2048]{1,0:T(8,128)(2,1)S(1)}, bf16[24,2048]{1,0:T(8,128)(2,1)S(1)}, u32[]{:S(2)}, u32[]{:S(2)}) collective-permute-start(bf16[24,2048]{1,0:T(8,128)(2,1)S(1)} %pad.4), channel_id=1, source_target_pairs={{0,4},{1,5},{2,6},{3,7},{4,0},{5,1},{6,2},{7,3},{8,12},{9,13},{10,... | collective-permute-start | bytes 294920 | tf_op jit(solution)/shard_map/ppermute | solution.py:26
  16.1 12.1 %collective-permute-start.12 = (bf16[24,2048]{1,0:T(8,128)(2,1)S(1)}, bf16[24,2048]{1,0:T(8,128)(2,1)S(1)}, u32[]{:S(2)}, u32[]{:S(2)}) collective-permute-start(bf16[24,2048]{1,0:T(8,128)(2,1)S(1)} %pad.4), channel_id=1, source_target_pairs={{0,8},{1,9},{2,10},{3,11},{4,12},{5,13},{6,14},{7,15},{8,0},{9,1},... | collective-permute-start | bytes 294920 | tf_op jit(solution)/shard_map/ppermute | solution.py:26
  23.4 7.8 %collective-permute-start.14 = (bf16[24,2048]{1,0:T(8,128)(2,1)S(1)}, bf16[24,2048]{1,0:T(8,128)(2,1)S(1)}, u32[]{:S(2)}, u32[]{:S(2)}) collective-permute-start(bf16[24,2048]{1,0:T(8,128)(2,1)S(1)} %pad.4), channel_id=1, source_target_pairs={{0,256},{1,257},{2,258},{3,259},{4,260},{5,261},{6,262},{7,263},{8... | collective-permute-start | bytes 294920 | tf_op jit(solution)/shard_map/ppermute | solution.py:26
  25.3 3.8 %collective-permute-start.13 = (bf16[24,2048]{1,0:T(8,128)(2,1)S(1)}, bf16[24,2048]{1,0:T(8,128)(2,1)S(1)}, u32[]{:S(2)}, u32[]{:S(2)}) collective-permute-start(bf16[24,2048]{1,0:T(8,128)(2,1)S(1)} %collective-permute-done.11), channel_id=1, source_target_pairs={{0,8},{1,9},{2,10},{3,11},{4,12},{5,13},{6,14},{7,15},{8,0},{9,1},... | collective-permute-start | bytes 294920 | tf_op jit(solution)/shard_map/ppermute | solution.py:26
  29.2 2.0 %copy-start.2 = (bf16[288,2048]{1,0:T(8,128)(2,1)}, bf16[288,2048]{1,0:T(8,128)(2,1)S(1)}, u32[]{:S(2)}) copy-start(bf16[288,2048]{1,0:T(8,128)(2,1)S(1)} %select_dynamic-update-slice_fusion) | copy-start | bytes 3538948
  31.2 13.6 %collective-permute-start.1 = (bf16[48,2048]{1,0:T(8,128)(2,1)S(1)}, bf16[48,2048]{1,0:T(8,128)(2,1)S(1)}, u32[]{:S(2)}, u32[]{:S(2)}) collective-permute-start(bf16[48,2048]{1,0:T(8,128)(2,1)S(1)} %get-tuple-element.12), channel_id=1, source_target_pairs={{0,448},{1,449},{2,450},{3,451},{4,452},{5,453},{6,454},{7,455},{8... | collective-permute-start | bytes 589832 | tf_op jit(solution)/shard_map/cond/branch_1_fun/ppermute | solution.py:26
  37.4 7.5 %collective-permute-start = (bf16[24,2048]{1,0:T(8,128)(2,1)S(1)}, bf16[24,2048]{1,0:T(8,128)(2,1)S(1)}, u32[]{:S(2)}, u32[]{:S(2)}) collective-permute-start(bf16[24,2048]{1,0:T(8,128)(2,1)S(1)} %get-tuple-element.13), channel_id=1, source_target_pairs={{0,8},{1,9},{2,10},{3,11},{4,12},{5,13},{6,14},{7,15},{8,0},{9,1},... | collective-permute-start | bytes 294920 | tf_op jit(solution)/shard_map/cond/branch_1_fun/ppermute | solution.py:26
  44.9 18.0 %copy-start = (bf16[48,2048]{1,0:T(8,128)(2,1)}, bf16[48,2048]{1,0:T(8,128)(2,1)S(1)}, u32[]{:S(2)}) copy-start(bf16[48,2048]{1,0:T(8,128)(2,1)S(1)} %collective-permute-done.1) | copy-start | bytes 589828 | tf_op jit(solution)/shard_map/cond
  44.9 13.6 %collective-permute-start.2 = (bf16[24,2048]{1,0:T(8,128)(2,1)S(1)}, bf16[24,2048]{1,0:T(8,128)(2,1)S(1)}, u32[]{:S(2)}, u32[]{:S(2)}) collective-permute-start(bf16[24,2048]{1,0:T(8,128)(2,1)S(1)} %slice.9), channel_id=1, source_target_pairs={{0,448},{1,449},{2,450},{3,451},{4,452},{5,453},{6,454},{7,455},{8... | collective-permute-start | bytes 294920 | tf_op jit(solution)/shard_map/cond/branch_1_fun/ppermute | solution.py:26
  58.5 11.9 %collective-permute-start.3 = (bf16[72,2048]{1,0:T(8,128)(2,1)S(1)}, bf16[72,2048]{1,0:T(8,128)(2,1)S(1)}, u32[]{:S(2)}, u32[]{:S(2)}) collective-permute-start(bf16[72,2048]{1,0:T(8,128)(2,1)S(1)} %pad_maximum_fusion.2), channel_id=1, source_target_pairs={{0,8},{1,9},{2,10},{3,11},{4,12},{5,13},{6,14},{7,15},{8,0},{9,1},... | collective-permute-start | bytes 884744 | tf_op jit(solution)/shard_map/cond/branch_1_fun/ppermute | solution.py:26
  62.8 15.4 %collective-permute-start.4 = (bf16[96,2048]{1,0:T(8,128)(2,1)S(1)}, bf16[96,2048]{1,0:T(8,128)(2,1)}, u32[]{:S(2)}, u32[]{:S(2)}) collective-permute-start(bf16[96,2048]{1,0:T(8,128)(2,1)S(1)} %pad_maximum_fusion), channel_id=1, source_target_pairs={{0,496},{1,497},{2,498},{3,499},{4,500},{5,501},{6,502},{7,503},{8... | collective-permute-start | bytes 1179656 | tf_op jit(solution)/shard_map/cond/branch_1_fun/ppermute | solution.py:26
  70.4 25.8 %copy-start.1 = (bf16[48,2048]{1,0:T(8,128)(2,1)S(1)}, bf16[48,2048]{1,0:T(8,128)(2,1)}, u32[]{:S(2)}) copy-start(bf16[48,2048]{1,0:T(8,128)(2,1)} %copy-done) | copy-start | bytes 589828 | tf_op jit(solution)/shard_map/cond
  72.1 16.8 %collective-permute-start.5 = (bf16[96,2048]{1,0:T(8,128)(2,1)S(1)}, bf16[96,2048]{1,0:T(8,128)(2,1)}, u32[]{:S(2)}, u32[]{:S(2)}) collective-permute-start(bf16[96,2048]{1,0:T(8,128)(2,1)S(1)} %pad_maximum_fusion.1), channel_id=1, source_target_pairs={{0,496},{1,497},{2,498},{3,499},{4,500},{5,501},{6,502},{7,503},{8... | collective-permute-start | bytes 1179656 | tf_op jit(solution)/shard_map/cond/branch_1_fun/ppermute | solution.py:26
  78.2 12.6 %collective-permute-start.8 = (bf16[96,2048]{1,0:T(8,128)(2,1)}, bf16[96,2048]{1,0:T(8,128)(2,1)}, u32[]{:S(2)}, u32[]{:S(2)}) collective-permute-start(bf16[96,2048]{1,0:T(8,128)(2,1)} %collective-permute-done.4), channel_id=1, source_target_pairs={{0,496},{1,497},{2,498},{3,499},{4,500},{5,501},{6,502},{7,503},{8... | collective-permute-start | bytes 1179656 | tf_op jit(solution)/shard_map/cond/branch_1_fun/ppermute | solution.py:26
  80.1 14.3 %collective-permute-start.6 = (bf16[96,2048]{1,0:T(8,128)(2,1)}, bf16[96,2048]{1,0:T(8,128)(2,1)}, u32[]{:S(2)}, u32[]{:S(2)}) collective-permute-start(bf16[96,2048]{1,0:T(8,128)(2,1)} %collective-permute-done.4), channel_id=1, source_target_pairs={{0,8},{1,9},{2,10},{3,11},{4,12},{5,13},{6,14},{7,15},{8,0},{9,1},... | collective-permute-start | bytes 1179656 | tf_op jit(solution)/shard_map/cond/branch_1_fun/ppermute | solution.py:26
  88.9 5.6 %collective-permute-start.7 = (bf16[96,2048]{1,0:T(8,128)(2,1)}, bf16[96,2048]{1,0:T(8,128)(2,1)}, u32[]{:S(2)}, u32[]{:S(2)}) collective-permute-start(bf16[96,2048]{1,0:T(8,128)(2,1)} %collective-permute-done.5), channel_id=1, source_target_pairs={{0,8},{1,9},{2,10},{3,11},{4,12},{5,13},{6,14},{7,15},{8,0},{9,1},... | collective-permute-start | bytes 1179656 | tf_op jit(solution)/shard_map/cond/branch_1_fun/ppermute | solution.py:26
  90.8 5.3 %collective-permute-start.9 = (bf16[96,2048]{1,0:T(8,128)(2,1)}, bf16[96,2048]{1,0:T(8,128)(2,1)}, u32[]{:S(2)}, u32[]{:S(2)}) collective-permute-start(bf16[96,2048]{1,0:T(8,128)(2,1)} %collective-permute-done.8), channel_id=1, source_target_pairs={{0,8},{1,9},{2,10},{3,11},{4,12},{5,13},{6,14},{7,15},{8,0},{9,1},... | collective-permute-start | bytes 1179656 | tf_op jit(solution)/shard_map/cond/branch_1_fun/ppermute | solution.py:26
  110.8 4.4 %collective-permute-start.15 = (f32[33,24,192]{2,1,0:T(8,128)}, f32[33,24,192]{2,1,0:T(8,128)S(1)}, u32[]{:S(2)}, u32[]{:S(2)}) collective-permute-start(f32[33,24,192]{2,1,0:T(8,128)} %get-tuple-element.69), channel_id=1, source_target_pairs={{0,8},{1,9},{2,10},{3,11},{4,12},{5,13},{6,14},{7,15},{8,0},{9,1},... | collective-permute-start | bytes 1824776 | tf_op jit(solution)/shard_map/ppermute | solution.py:26
Sparse Core Ops, SparseCore 0:
  31.3 59.4 all-gather.2

commit v4 on v3

v4 whole, which is shorter than its diff:
```python
import functools

import jax
import jax.numpy as jnp
from jax import lax
from jax.experimental import pallas as pl
from jax.experimental.pallas import tpu as pltpu
from jax.sharding import PartitionSpec as P

LANES = 2048
UNITS = (
    (0, True), (4, True), (8, True), (12, False), (16, True),
    (1, True), (5, True), (9, True), (13, False),
    (15, False), (11, False), (7, False), (3, True),
    (2, True), (6, True), (14, False), (10, False),
)


def permuted(value, move):
    wide, narrow = lax.axis_size("wide"), lax.axis_size("narrow")
    pairs = []
    for w in range(wide):
        for n in range(narrow):
            to_w, to_n = move(w, n)
            pairs.append((w * narrow + n, (to_w % wide) * narrow + to_n % narrow))
    return lax.ppermute(value, ("wide", "narrow"), pairs)


def by_chips(value, first, second):
    return permuted(value, lambda w, n: (w + 2 * (second if w % 2 else first), n))


def from_partner(value):
    return permuted(value, lambda w, n: (w ^ 1, n))


def gather_wide(unit, four_mine, core, piece):
    eight = by_chips(four_mine, -4, 4)
    four = jnp.concatenate([four_mine, by_chips(unit[piece:], -4, -12)], axis=0)
    sixteen_mine = by_chips(unit[:piece], -16, -16)
    sixteen = jnp.concatenate([sixteen_mine, from_partner(sixteen_mine)], axis=0)
    start = jnp.where(core == 0, unit, sixteen)
    stop = jnp.where(core == 0, sixteen, unit)
    near = by_chips(jnp.concatenate([start, four], axis=0), -1, 1)
    got = from_partner(jnp.concatenate([four, eight], axis=0))
    two = by_chips(near, -1, 1)
    eights = jnp.concatenate([eight, got[2 * piece :]], axis=0)
    twelve = got[: 2 * piece]
    near_late = by_chips(jnp.concatenate([eights, twelve], axis=0), -1, 1)
    far = from_partner(near)
    two_far = from_partner(two)
    far_late = from_partner(near_late)
    return start, four, eights, twelve, stop, near, near_late, far, far_late, two, two_far


def dots_of(rows, envs):
    return lax.dot_general(rows, envs, (((1,), (1,)), ((), ())), preferred_element_type=jnp.float32)


def two_parts(value):
    top = value.astype(jnp.bfloat16)
    return top, (value - top.astype(jnp.float32)).astype(jnp.bfloat16)


def rows_kernel(shards_x, rows_d, tile, width, *refs):
    gathered, points = refs[0], refs[1:12]
    high_ref, low_ref = refs[12:14]
    envs, rows, sems = refs[14:]
    copies = []

    def copied(source, target):
        copies.append(pltpu.make_async_copy(source, target, sems.at[len(copies)]))
        copies[-1].start()
        return copies[-1]

    def copied_envs(i):
        return copied(gathered.at[i, pl.ds(0, rows_d)], envs.at[pl.ds(i * rows_d, rows_d)])

    first = -(-tile // rows_d)
    env_copies = [copied_envs(i) for i in range(first)]
    row_copies, sizes, place = [], [], 0
    for group in ((0, 1, 2, 3, 4), (5, 6), (7, 8), (9, 10)):
        row_copies.append([])
        begin = place
        for k in group:
            size = points[k].shape[0]
            row_copies[-1].append(copied(points[k], rows.at[pl.ds(place, size)]))
            place += size
        sizes.append(place - begin)
    late_copies = [copied_envs(i) for i in range(first, shards_x)]

    def some(part, t):
        value = dots_of(rows[part, :], envs[pl.ds(t * tile, tile), :])
        top, rest = two_parts(value * value / width)
        high_ref[part, pl.ds(t * tile, tile)] = top
        low_ref[part, pl.ds(t * tile, tile)] = rest

    for copy in env_copies:
        copy.wait()
    place = 0
    for waits, size in zip(row_copies, sizes):
        for copy in waits:
            copy.wait()
        some(pl.ds(place, size), 0)
        place += size
    for copy in late_copies:
        copy.wait()
    step = place // 3
    for t in range(1, envs.shape[0] // tile):
        def body(m, carry):
            some(pl.ds(pl.multiple_of(m * step, 16), step), t)
            return carry

        lax.fori_loop(0, 3, body, 0)


def products_kernel(piece, shards_x, rows_d, tile, width, env_count, core_ref, *refs):
    gathered, other, high_ref, low_ref = refs[:4]
    own_ref, send_ref = refs[4:6]
    envs, rows, dots, columns, own, send, sems = refs[6:]
    count = len(UNITS) * 2 * piece
    block = 2 * shards_x * piece
    at = 2 * block
    copies = []

    def copied(source, target):
        copies.append(pltpu.make_async_copy(source, target, sems.at[len(copies)]))
        copies[-1].start()
        return copies[-1]

    def copied_envs(i):
        return copied(gathered.at[i, pl.ds(0, rows_d)], envs.at[pl.ds(i * rows_d, rows_d)])

    first = -(-tile // rows_d)
    waits = [copied_envs(i) for i in range(first)]
    for i in range(shards_x):
        waits.append(copied(gathered.at[i, pl.ds(rows_d, 2 * piece)], rows.at[pl.ds(2 * i * piece, 2 * piece)]))
    waits.append(copied(other, rows.at[pl.ds(block, block)]))
    late = [copied_envs(i) for i in range(first, shards_x)]
    pick = (lax.broadcasted_iota(jnp.int32, (16, LANES), 1) == width) & (
        lax.broadcasted_iota(jnp.int32, (16, LANES), 0) == 0
    )
    rows[pl.ds(at, 16), :] = pick.astype(jnp.float32).astype(jnp.bfloat16)
    for copy in waits:
        copy.wait()

    for t in range(envs.shape[0] // tile):
        lanes = pl.ds(t * tile, tile)
        dots[...] = dots_of(rows[...], envs[lanes, :])
        if t == 0:
            for copy in late:
                copy.wait()
        weights = dots[pl.ds(at, 8), :][:1] / env_count
        for which in range(2):
            for i in range(shards_x):
                for low in range(2):
                    source = which * block + (2 * i + low) * piece
                    target = which * block + (low * shards_x + i) * piece
                    value = dots[pl.ds(source, piece), :]
                    columns[pl.ds(target, piece), :] = value * value / width * weights
        parts = [two_parts(columns[pl.ds(which * block, block), :]) for which in range(2)]

        def some_products(m, carry):
            part = pl.ds(pl.multiple_of(m * (count // 3), 16), count // 3)
            top, rest = high_ref[part, lanes], low_ref[part, lanes]
            for which, target in ((0, own), (1, send)):
                high, low_part = parts[which]
                result = dots_of(top, high) + dots_of(top, low_part) + dots_of(rest, high)
                target[part, :] = result if t == 0 else target[part, :] + result
            return carry

        lax.fori_loop(0, 3, some_products, 0)

    core = core_ref[0]
    for u, (distance, first_own) in enumerate(UNITS):
        for b in range(2):
            part = pl.ds((2 * u + b) * piece, piece)
            mine = first_own == (b == 0)
            near = 2 * distance + (0 if mine else 1)
            away = (33 if mine else 32) - 2 * distance
            if near < 33:
                own_ref[near + core * (32 - 2 * near)] = own[part, :]
            if away < 33:
                send_ref[away + (1 - core) * (32 - 2 * away)] = send[part, :]


def tile_of(env_rows):
    return 256 if env_rows % 256 == 0 else env_rows


def rows_call(gathered, points, rows_d, width):
    shards_x = gathered.shape[0]
    env_rows = shards_x * rows_d
    count = sum(p.shape[0] for p in points)
    shape = jax.ShapeDtypeStruct((count, env_rows), jnp.bfloat16)
    vmem = pl.BlockSpec(memory_space=pltpu.VMEM)
    return pl.pallas_call(
        functools.partial(rows_kernel, shards_x, rows_d, tile_of(env_rows), width),
        out_shape=(shape, shape),
        in_specs=[pl.BlockSpec(memory_space=pltpu.HBM)] + [pl.BlockSpec(memory_space=pl.ANY)] * len(points),
        out_specs=(vmem, vmem),
        scratch_shapes=[
            pltpu.VMEM((env_rows, LANES), jnp.bfloat16),
            pltpu.VMEM((count, LANES), jnp.bfloat16),
            pltpu.SemaphoreType.DMA((len(points) + shards_x,)),
        ],
        compiler_params=pltpu.CompilerParams(vmem_limit_bytes=24 * 1024 * 1024),
        cost_estimate=pl.CostEstimate(
            flops=2 * env_rows * count * LANES, bytes_accessed=9 * 10**6, transcendentals=0
        ),
    )(gathered, *points)


def products_call(core, gathered, other, high, low, piece, rows_d, width, env_count):
    shards_x = gathered.shape[0]
    env_rows = shards_x * rows_d
    tile = tile_of(env_rows)
    count = high.shape[0]
    block = 2 * shards_x * piece
    shape = jax.ShapeDtypeStruct((33, piece, block), jnp.float32)
    vmem = pl.BlockSpec(memory_space=pltpu.VMEM)
    return pl.pallas_call(
        functools.partial(products_kernel, piece, shards_x, rows_d, tile, width, env_count),
        out_shape=(shape, shape),
        in_specs=[
            pl.BlockSpec(memory_space=pltpu.SMEM),
            pl.BlockSpec(memory_space=pltpu.HBM),
            pl.BlockSpec(memory_space=pl.ANY),
            vmem,
            vmem,
        ],
        out_specs=(vmem, vmem),
        scratch_shapes=[
            pltpu.VMEM((env_rows, LANES), jnp.bfloat16),
            pltpu.VMEM((2 * block + 16, LANES), jnp.bfloat16),
            pltpu.VMEM((2 * block + 16, tile), jnp.float32),
            pltpu.VMEM((2 * block, tile), jnp.float32),
            pltpu.VMEM((count, block), jnp.float32),
            pltpu.VMEM((count, block), jnp.float32),
            pltpu.SemaphoreType.DMA((1 + 2 * shards_x,)),
        ],
        compiler_params=pltpu.CompilerParams(vmem_limit_bytes=24 * 1024 * 1024),
        cost_estimate=pl.CostEstimate(
            flops=2 * env_rows * (2 * block * LANES + 6 * count * block), bytes_accessed=9 * 10**6, transcendentals=0
        ),
    )(core, gathered, other, high, low)


def shards(descriptors, env_weights, sparse_points):
    core = lax.axis_index("wide") % 2
    narrow = lax.axis_size("narrow")
    wide = lax.axis_size("wide")
    shards_x = narrow // 2
    width = descriptors.shape[1]
    half = descriptors.shape[0] // 2
    env_count = descriptors.shape[0] * narrow
    piece = sparse_points.shape[0]

    mine = jnp.pad(sparse_points, ((0, 0), (0, LANES - width)))
    other = from_partner(mine)
    across_mine = permuted(mine, lambda w, n: (w, n + shards_x))
    unit = jnp.concatenate([mine, other], axis=0)
    half_envs = lax.dynamic_slice_in_dim(
        jnp.concatenate(
            [descriptors, env_weights[:, None], jnp.zeros((2 * half, LANES - width - 1), descriptors.dtype)], axis=1
        ),
        core * half,
        half,
        0,
    )
    across_envs = permuted(
        half_envs, lambda w, n: (w + (wide // 2 if w % 2 else 0), n + shards_x)
    )
    four_mine = by_chips(mine, -4, -12)
    at_zero = lax.axis_index("narrow") < shards_x
    payload = jnp.concatenate(
        [
            half_envs,
            across_envs,
            jnp.where(at_zero, mine, across_mine),
            jnp.where(at_zero, across_mine, mine),
        ],
        axis=0,
    )
    payload, unit, four_mine = lax.optimization_barrier((payload, unit, four_mine))
    groups = [list(range(shards_x)), list(range(shards_x, narrow))]
    gathered = lax.all_gather(payload, "narrow", axis=0, tiled=False, axis_index_groups=groups)

    def none(*_):
        return tuple(jnp.zeros((n * piece, LANES), unit.dtype) for n in (2, 2, 2, 2, 2, 4, 4, 4, 4, 4, 4))

    points = lax.cond(
        1 + jnp.minimum(lax.axis_index("wide"), 0) > 0,
        lambda *values: gather_wide(*values, core, piece),
        none,
        unit,
        four_mine,
    )
    gathered, points = lax.optimization_barrier((gathered, points))
    block_other = from_partner(gathered[:, 2 * half :].reshape(-1, LANES))
    high, low = rows_call(gathered, points, 2 * half, width)
    kept, sent = products_call(
        core.reshape(1), gathered, block_other, high, low, piece, 2 * half, width, env_count
    )
    return (kept + from_partner(sent))[None]


def solution(mesh):
    in_specs = (P("narrow", None), P("narrow"), P(("wide", "narrow"), None))
    out_specs = P("wide", None, "narrow", None)
    return jax.shard_map(shards, mesh=mesh, in_specs=in_specs, out_specs=out_specs, check_vma=False)
```

time: 125 us -> 129 us (1.032)
  starting transfers between devices: 73.1 us -> 68 us
  waiting for transfers between devices: 14.9 us -> 19.7 us
  local copies, waits for them, and re-layouts: 2.89 us -> 7.01 us
    ppermute x16 -> x17, starting transfers between devices: 73.1 us -> 68 us  [permuted(): return lax.ppermute(value, ('wide', 'narrow'), pairs)]
    ppermute x16 -> x17, waiting for transfers between devices: 14.9 us -> 19.7 us  [permuted(): return lax.ppermute(value, ('wide', 'narrow'), pairs)]
    unnamed x6, local copies, waits for them, and re-layouts: 0.12 us -> 2.11 us
    pallas_call x1 -> x2, Pallas kernels: 14.6 us -> 14.8 us  [the longest x1 7.63 us: rows_call(): pl.pallas_call(functools.partial(rows_kernel, shards_x, rows_d, tile_of(e...]
  transfers between devices with their start and end apart: 17 -> 18, of which waited for: 7 -> 7; matrix products, arithmetic and copies ran while one was open for 3% -> 5% of each run, Pallas kernels for 0% -> 6%
where the time goes in v4:
time: 129 us; the launch traced here: 128 us
  starting transfers between devices  68 us (53%)
  waiting for transfers between devices  19.7 us (15%)
  Pallas kernels  14.8 us (11%)
  between operations  13.6 us (11%)
  local copies, waits for them, and re-layouts  7.01 us (5%)
  other arithmetic  4.78 us (4%)
    ppermute x17, starting transfers between devices, permuted(): return lax.ppermute(value, ('wide', 'narrow'), pairs)  68 us
    ppermute x17, waiting for transfers between devices, permuted(): return lax.ppermute(value, ('wide', 'narrow'), pairs)  19.7 us
    pallas_call x1, Pallas kernels, rows_call(): pl.pallas_call(functools.partial(rows_kernel, shards_x, rows_d, tile_of(e...  7.63 us
    pallas_call x1, Pallas kernels, products_call(): pl.pallas_call(functools.partial(products_kernel, piece, shards_x, rows_d...  7.16 us
  transfers between devices with their start and end apart: 18, of which 7 were waited for; matrix products, arithmetic and copies ran while one was open for 5% of the time, Pallas kernels for 6%

profile of v4, /device:TPU:1, one launch (start us, length us, event | category | flops | bytes accessed | tf_op | source)
XLA Modules:
  0.0 128.0 jit_solution(12758615971990436635)
XLA Ops:
  6.5 1.0 pad.4
  7.5 4.0 %collective-permute-start.12 = (bf16[24,2048]{1,0:T(8,128)(2,1)S(1)}, bf16[24,2048]{1,0:T(8,128)(2,1)S(1)}, u32[]{:S(2)}, u32[]{:S(2)}) collective-permute-start(bf16[24,2048]{1,0:T(8,128)(2,1)S(1)} %pad.4), channel_id=1, source_target_pairs={{0,4},{1,5},{2,6},{3,7},{4,0},{5,1},{6,2},{7,3},{8,12},{9,13},{10,... | collective-permute-start | bytes 294920 | tf_op jit(solution)/shard_map/ppermute | solution.py:26
  11.6 6.7 %collective-permute-start.13 = (bf16[24,2048]{1,0:T(8,128)(2,1)S(1)}, bf16[24,2048]{1,0:T(8,128)(2,1)S(1)}, u32[]{:S(2)}, u32[]{:S(2)}) collective-permute-start(bf16[24,2048]{1,0:T(8,128)(2,1)S(1)} %pad.4), channel_id=1, source_target_pairs={{0,8},{1,9},{2,10},{3,11},{4,12},{5,13},{6,14},{7,15},{8,0},{9,1},... | collective-permute-start | bytes 294920 | tf_op jit(solution)/shard_map/ppermute | solution.py:26
  18.2 7.3 %collective-permute-start.14 = (bf16[24,2048]{1,0:T(8,128)(2,1)S(1)}, bf16[24,2048]{1,0:T(8,128)(2,1)S(1)}, u32[]{:S(2)}, u32[]{:S(2)}) collective-permute-start(bf16[24,2048]{1,0:T(8,128)(2,1)S(1)} %pad.4), channel_id=1, source_target_pairs={{0,448},{1,449},{2,450},{3,451},{4,452},{5,453},{6,454},{7,455},{8... | collective-permute-start | bytes 294920 | tf_op jit(solution)/shard_map/ppermute | solution.py:26
  25.6 0.7 broadcast_in_dim.12
  26.4 1.2 concatenate.30
  27.7 1.9 %collective-permute-start.11 = (bf16[96,2048]{1,0:T(8,128)(2,1)S(1)}, bf16[96,2048]{1,0:T(8,128)(2,1)S(1)}, u32[]{:S(2)}, u32[]{:S(2)}) collective-permute-start(bf16[96,2048]{1,0:T(8,128)(2,1)S(1)} %constant_dynamic-slice_fusion), channel_id=1, source_target_pairs={{0,4},{1,5},{2,6},{3,7},{4,0},{5,1},{6,2},{7,3},{8,268},{9,269},{1... | collective-permute-start | bytes 1179656 | tf_op jit(solution)/shard_map/ppermute | solution.py:26
  29.6 0.0 collective-permute-done.13
  29.6 0.0 collective-permute-done.12
  29.7 7.7 %collective-permute-done.11 = bf16[96,2048]{1,0:T(8,128)(2,1)S(1)} collective-permute-done((bf16[96,2048]{1,0:T(8,128)(2,1)S(1)}, bf16[96,2048]{1,0:T(8,128)(2,1)S(1)}, u32[]{:S(2)}, u32[]{:S(2)}) %collective-permute-start.11) | collective-permute-done | bytes 393248 | tf_op jit(solution)/shard_map/ppermute | solution.py:26
  37.4 1.0 pad_maximum_fusion.5
  38.4 0.0 collective-permute-done.14
  38.4 0.0 all-gather.3.cloned.1.call-update
  38.4 57.3 %conditional.1 = (bf16[48,2048]{1,0:T(8,128)(2,1)}, bf16[48,2048]{1,0:T(8,128)(2,1)S(1)}, bf16[48,2048]{1,0:T(8,128)(2,1)S(1)}, bf16[48,2048]{1,0:T(8,128)(2,1)}...) conditional(s32[]{:T(128)} %convert_element_type.5, () %tuple.16, ...), branch_computations={%region_0.1_spmd, %region_1.2_spmd} | conditional | flops 4227073 | bytes 17302042 | solution.py:292
  38.4 8.8 %collective-permute-start.3 = (bf16[24,2048]{1,0:T(8,128)(2,1)S(1)}, bf16[24,2048]{1,0:T(8,128)(2,1)S(1)}, u32[]{:S(2)}, u32[]{:S(2)}) collective-permute-start(bf16[24,2048]{1,0:T(8,128)(2,1)S(1)} %get-tuple-element.13), channel_id=1, source_target_pairs={{0,448},{1,449},{2,450},{3,451},{4,452},{5,453},{6,454},{7,455},{8... | collective-permute-start | bytes 294920 | tf_op jit(solution)/shard_map/cond/branch_1_fun/ppermute | solution.py:26
  47.3 3.9 %collective-permute-start.2 = (bf16[24,2048]{1,0:T(8,128)(2,1)S(1)}, bf16[24,2048]{1,0:T(8,128)(2,1)S(1)}, u32[]{:S(2)}, u32[]{:S(2)}) collective-permute-start(bf16[24,2048]{1,0:T(8,128)(2,1)S(1)} %get-tuple-element.76), channel_id=1, source_target_pairs={{0,448},{1,449},{2,450},{3,451},{4,452},{5,453},{6,454},{7,455},{8... | collective-permute-start | bytes 294920 | tf_op jit(solution)/shard_map/cond/branch_1_fun/ppermute | solution.py:26
  51.2 4.9 %collective-permute-start = (bf16[24,2048]{1,0:T(8,128)(2,1)S(1)}, bf16[24,2048]{1,0:T(8,128)(2,1)S(1)}, u32[]{:S(2)}, u32[]{:S(2)}) collective-permute-start(bf16[24,2048]{1,0:T(8,128)(2,1)S(1)} %get-tuple-element.77), channel_id=1, source_target_pairs={{0,256},{1,257},{2,258},{3,259},{4,260},{5,261},{6,262},{7,263},{8... | collective-permute-start | bytes 294920 | tf_op jit(solution)/shard_map/cond/branch_1_fun/ppermute | solution.py:26
  56.1 0.0 collective-permute-done.3
  56.1 0.7 collective-permute-done.2
  56.9 5.3 %collective-permute-start.4 = (bf16[72,2048]{1,0:T(8,128)(2,1)S(1)}, bf16[72,2048]{1,0:T(8,128)(2,1)S(1)}, u32[]{:S(2)}, u32[]{:S(2)}) collective-permute-start(bf16[72,2048]{1,0:T(8,128)(2,1)S(1)} %pad_maximum_fusion.2), channel_id=1, source_target_pairs={{0,8},{1,9},{2,10},{3,11},{4,12},{5,13},{6,14},{7,15},{8,0},{9,1},... | collective-permute-start | bytes 884744 | tf_op jit(solution)/shard_map/cond/branch_1_fun/ppermute | solution.py:26
  62.2 0.0 collective-permute-done
  62.2 1.9 %collective-permute-start.1 = (bf16[24,2048]{1,0:T(8,128)(2,1)S(1)}, bf16[24,2048]{1,0:T(8,128)(2,1)S(1)}, u32[]{:S(2)}, u32[]{:S(2)}) collective-permute-start(bf16[24,2048]{1,0:T(8,128)(2,1)S(1)} %collective-permute-done), channel_id=1, source_target_pairs={{0,8},{1,9},{2,10},{3,11},{4,12},{5,13},{6,14},{7,15},{8,0},{9,1},... | collective-permute-start | bytes 294920 | tf_op jit(solution)/shard_map/cond/branch_1_fun/ppermute | solution.py:26
  64.2 1.3 collective-permute-done.1
  65.4 0.7 broadcast_select_fusion
  66.2 1.0 pad_maximum_fusion
  67.1 4.0 %collective-permute-start.5 = (bf16[96,2048]{1,0:T(8,128)(2,1)S(1)}, bf16[96,2048]{1,0:T(8,128)(2,1)}, u32[]{:S(2)}, u32[]{:S(2)}) collective-permute-start(bf16[96,2048]{1,0:T(8,128)(2,1)S(1)} %pad_maximum_fusion), channel_id=1, source_target_pairs={{0,496},{1,497},{2,498},{3,499},{4,500},{5,501},{6,502},{7,503},{8... | collective-permute-start | bytes 1179656 | tf_op jit(solution)/shard_map/cond/branch_1_fun/ppermute | solution.py:26
  71.1 0.0 collective-permute-done.4
  71.1 0.7 slice.17
  71.8 1.0 pad_maximum_fusion.1
  72.8 1.9 %collective-permute-start.6 = (bf16[96,2048]{1,0:T(8,128)(2,1)S(1)}, bf16[96,2048]{1,0:T(8,128)(2,1)}, u32[]{:S(2)}, u32[]{:S(2)}) collective-permute-start(bf16[96,2048]{1,0:T(8,128)(2,1)S(1)} %pad_maximum_fusion.1), channel_id=1, source_target_pairs={{0,496},{1,497},{2,498},{3,499},{4,500},{5,501},{6,502},{7,503},{8... | collective-permute-start | bytes 1179656 | tf_op jit(solution)/shard_map/cond/branch_1_fun/ppermute | solution.py:26
  74.7 4.6 %collective-permute-done.5 = bf16[96,2048]{1,0:T(8,128)(2,1)} collective-permute-done((bf16[96,2048]{1,0:T(8,128)(2,1)S(1)}, bf16[96,2048]{1,0:T(8,128)(2,1)}, u32[]{:S(2)}, u32[]{:S(2)}) %collective-permute-start.5) | collective-permute-done | bytes 393248 | tf_op jit(solution)/shard_map/cond/branch_1_fun/ppermute | solution.py:26
  79.4 1.9 %collective-permute-start.9 = (bf16[96,2048]{1,0:T(8,128)(2,1)}, bf16[96,2048]{1,0:T(8,128)(2,1)}, u32[]{:S(2)}, u32[]{:S(2)}) collective-permute-start(bf16[96,2048]{1,0:T(8,128)(2,1)} %collective-permute-done.5), channel_id=1, source_target_pairs={{0,496},{1,497},{2,498},{3,499},{4,500},{5,501},{6,502},{7,503},{8... | collective-permute-start | bytes 1179656 | tf_op jit(solution)/shard_map/cond/branch_1_fun/ppermute | solution.py:26
  81.3 7.0 %collective-permute-start.7 = (bf16[96,2048]{1,0:T(8,128)(2,1)}, bf16[96,2048]{1,0:T(8,128)(2,1)}, u32[]{:S(2)}, u32[]{:S(2)}) collective-permute-start(bf16[96,2048]{1,0:T(8,128)(2,1)} %collective-permute-done.5), channel_id=1, source_target_pairs={{0,8},{1,9},{2,10},{3,11},{4,12},{5,13},{6,14},{7,15},{8,0},{9,1},... | collective-permute-start | bytes 1179656 | tf_op jit(solution)/shard_map/cond/branch_1_fun/ppermute | solution.py:26
  88.3 1.9 %collective-permute-start.8 = (bf16[96,2048]{1,0:T(8,128)(2,1)}, bf16[96,2048]{1,0:T(8,128)(2,1)}, u32[]{:S(2)}, u32[]{:S(2)}) collective-permute-start(bf16[96,2048]{1,0:T(8,128)(2,1)} %collective-permute-done.6), channel_id=1, source_target_pairs={{0,8},{1,9},{2,10},{3,11},{4,12},{5,13},{6,14},{7,15},{8,0},{9,1},... | collective-permute-start | bytes 1179656 | tf_op jit(solution)/shard_map/cond/branch_1_fun/ppermute | solution.py:26
  90.2 1.6 %collective-permute-done.9 = bf16[96,2048]{1,0:T(8,128)(2,1)} collective-permute-done((bf16[96,2048]{1,0:T(8,128)(2,1)}, bf16[96,2048]{1,0:T(8,128)(2,1)}, u32[]{:S(2)}, u32[]{:S(2)}) %collective-permute-start.9) | collective-permute-done | bytes 393248 | tf_op jit(solution)/shard_map/cond/branch_1_fun/ppermute | solution.py:26
  91.8 2.0 %collective-permute-start.10 = (bf16[96,2048]{1,0:T(8,128)(2,1)}, bf16[96,2048]{1,0:T(8,128)(2,1)}, u32[]{:S(2)}, u32[]{:S(2)}) collective-permute-start(bf16[96,2048]{1,0:T(8,128)(2,1)} %collective-permute-done.9), channel_id=1, source_target_pairs={{0,8},{1,9},{2,10},{3,11},{4,12},{5,13},{6,14},{7,15},{8,0},{9,1},... | collective-permute-start | bytes 1179656 | tf_op jit(solution)/shard_map/cond/branch_1_fun/ppermute | solution.py:26
  93.9 0.0 collective-permute-done.7
  93.9 0.0 collective-permute-done.8
  93.9 1.9 %collective-permute-done.10 = bf16[96,2048]{1,0:T(8,128)(2,1)} collective-permute-done((bf16[96,2048]{1,0:T(8,128)(2,1)}, bf16[96,2048]{1,0:T(8,128)(2,1)}, u32[]{:S(2)}, u32[]{:S(2)}) %collective-permute-start.10) | collective-permute-done | bytes 393248 | tf_op jit(solution)/shard_map/cond/branch_1_fun/ppermute | solution.py:26
  95.8 1.2 slice.15
  96.9 2.0 %collective-permute-start.15 = (bf16[192,2048]{1,0:T(8,128)(2,1)S(1)}, bf16[192,2048]{1,0:T(8,128)(2,1)S(1)}, u32[]{:S(2)}, u32[]{:S(2)}) collective-permute-start(bf16[192,2048]{1,0:T(8,128)(2,1)S(1)} %bitcast.8), channel_id=1, source_target_pairs={{0,8},{1,9},{2,10},{3,11},{4,12},{5,13},{6,14},{7,15},{8,0},{9,1},... | collective-permute-start | bytes 2359304 | tf_op jit(solution)/shard_map/ppermute | solution.py:26
  99.0 2.1 %copy-done = bf16[960,2048]{1,0:T(8,128)(2,1)S(1)} copy-done((bf16[960,2048]{1,0:T(8,128)(2,1)S(1)}, bf16[960,2048]{1,0:T(8,128)(2,1)}, u32[]{:S(2)}) %copy-start) | copy-done | bytes 3932184
  101.1 7.6 %shard_map.37 = (bf16[816,768]{1,0:T(8,128)(2,1)S(1)}, bf16[816,768]{1,0:T(8,128)(2,1)S(1)}) custom-call(bf16[4,240,2048]{2,1,0:T(8,128)(2,1)S(1)} %bitcast.6, bf16[48,2048]{1,0:T(8,128)(2,1)} %get-tuple-element.59.refs_1_, bf16[48,2048]{1,0:T(8,128)(2,1)S(1)} %get-tuple-element.60.refs_2_, bf16[48,2048]{1,0:T(8,128)(2,1)S(1)} %get-tuple-element.61.refs_3_, ...), custom_call_target="tpu_custom_call" | custom-call | flops 2566914048 | bytes 9000000 | tf_op jit(solution)/shard_map/pallas_call | solution.py:197
  108.7 0.0 collective-permute-done.15.refs_1_
  108.8 7.2 %shard_map.38 = (f32[33,24,192]{2,1,0:T(8,128)S(1)}, f32[33,24,192]{2,1,0:T(8,128)S(1)}) custom-call(s32[1]{0:T(128)} %bitcast.core_ref, bf16[4,240,2048]{2,1,0:T(8,128)(2,1)S(1)} %bitcast.7, bf16[192,2048]{1,0:T(8,128)(2,1)S(1)} %collective-permute-done.15.refs_1_, bf16[816,768]{1,0:T(8,128)(2,1)S(1)} %get-tuple-element.70.refs_2_, ...), custom_call_target="tpu_custom_call" | custom-call | flops 2651848704 | bytes 9000000 | tf_op jit(solution)/shard_map/pallas_call | solution.py:222
  115.9 2.3 %collective-permute-start.16 = (f32[33,24,192]{2,1,0:T(8,128)S(1)}, f32[33,24,192]{2,1,0:T(8,128)S(1)}, u32[]{:S(2)}, u32[]{:S(2)}) collective-permute-start(f32[33,24,192]{2,1,0:T(8,128)S(1)} %get-tuple-element.73), channel_id=1, source_target_pairs={{0,8},{1,9},{2,10},{3,11},{4,12},{5,13},{6,14},{7,15},{8,0},{9,1},... | collective-permute-start | bytes 1824776 | tf_op jit(solution)/shard_map/ppermute | solution.py:26
  118.2 1.9 %collective-permute-done.16 = f32[33,24,192]{2,1,0:T(8,128)S(1)} collective-permute-done((f32[33,24,192]{2,1,0:T(8,128)S(1)}, f32[33,24,192]{2,1,0:T(8,128)S(1)}, u32[]{:S(2)}, u32[]{:S(2)}) %collective-permute-start.16) | collective-permute-done | bytes 608288 | tf_op jit(solution)/shard_map/ppermute | solution.py:26
  120.2 1.0 add_bitcast_fusion
  (19 shorter events, 0.2 us)
Async XLA Ops:
  6.5 23.1 %copy-start.2 = (bf16[24,2000]{1,0:T(8,128)(2,1)S(1)}, bf16[24,2000]{1,0:T(8,128)(2,1)}, u32[]{:S(2)}) copy-start(bf16[24,2000]{1,0:T(8,128)(2,1)} %param.7) | copy-start | bytes 288004
  6.5 89.2 %all-gather.3.cloned.1.call-start = ((), (), s32[]{:S(2)}) async-start(), calls=%async_computation | async-start | bytes 4915200 | tf_op jit(solution)/shard_map/all_gather | solution.py:287
  7.5 22.1 %collective-permute-start.12 = (bf16[24,2048]{1,0:T(8,128)(2,1)S(1)}, bf16[24,2048]{1,0:T(8,128)(2,1)S(1)}, u32[]{:S(2)}, u32[]{:S(2)}) collective-permute-start(bf16[24,2048]{1,0:T(8,128)(2,1)S(1)} %pad.4), channel_id=1, source_target_pairs={{0,4},{1,5},{2,6},{3,7},{4,0},{5,1},{6,2},{7,3},{8,12},{9,13},{10,... | collective-permute-start | bytes 294920 | tf_op jit(solution)/shard_map/ppermute | solution.py:26
  11.6 18.0 %collective-permute-start.13 = (bf16[24,2048]{1,0:T(8,128)(2,1)S(1)}, bf16[24,2048]{1,0:T(8,128)(2,1)S(1)}, u32[]{:S(2)}, u32[]{:S(2)}) collective-permute-start(bf16[24,2048]{1,0:T(8,128)(2,1)S(1)} %pad.4), channel_id=1, source_target_pairs={{0,8},{1,9},{2,10},{3,11},{4,12},{5,13},{6,14},{7,15},{8,0},{9,1},... | collective-permute-start | bytes 294920 | tf_op jit(solution)/shard_map/ppermute | solution.py:26
  18.2 20.2 %collective-permute-start.14 = (bf16[24,2048]{1,0:T(8,128)(2,1)S(1)}, bf16[24,2048]{1,0:T(8,128)(2,1)S(1)}, u32[]{:S(2)}, u32[]{:S(2)}) collective-permute-start(bf16[24,2048]{1,0:T(8,128)(2,1)S(1)} %pad.4), channel_id=1, source_target_pairs={{0,448},{1,449},{2,450},{3,451},{4,452},{5,453},{6,454},{7,455},{8... | collective-permute-start | bytes 294920 | tf_op jit(solution)/shard_map/ppermute | solution.py:26
  27.7 9.7 %collective-permute-start.11 = (bf16[96,2048]{1,0:T(8,128)(2,1)S(1)}, bf16[96,2048]{1,0:T(8,128)(2,1)S(1)}, u32[]{:S(2)}, u32[]{:S(2)}) collective-permute-start(bf16[96,2048]{1,0:T(8,128)(2,1)S(1)} %constant_dynamic-slice_fusion), channel_id=1, source_target_pairs={{0,4},{1,5},{2,6},{3,7},{4,0},{5,1},{6,2},{7,3},{8,268},{9,269},{1... | collective-permute-start | bytes 1179656 | tf_op jit(solution)/shard_map/ppermute | solution.py:26
  38.4 17.7 %collective-permute-start.3 = (bf16[24,2048]{1,0:T(8,128)(2,1)S(1)}, bf16[24,2048]{1,0:T(8,128)(2,1)S(1)}, u32[]{:S(2)}, u32[]{:S(2)}) collective-permute-start(bf16[24,2048]{1,0:T(8,128)(2,1)S(1)} %get-tuple-element.13), channel_id=1, source_target_pairs={{0,448},{1,449},{2,450},{3,451},{4,452},{5,453},{6,454},{7,455},{8... | collective-permute-start | bytes 294920 | tf_op jit(solution)/shard_map/cond/branch_1_fun/ppermute | solution.py:26
  47.3 9.6 %collective-permute-start.2 = (bf16[24,2048]{1,0:T(8,128)(2,1)S(1)}, bf16[24,2048]{1,0:T(8,128)(2,1)S(1)}, u32[]{:S(2)}, u32[]{:S(2)}) collective-permute-start(bf16[24,2048]{1,0:T(8,128)(2,1)S(1)} %get-tuple-element.76), channel_id=1, source_target_pairs={{0,448},{1,449},{2,450},{3,451},{4,452},{5,453},{6,454},{7,455},{8... | collective-permute-start | bytes 294920 | tf_op jit(solution)/shard_map/cond/branch_1_fun/ppermute | solution.py:26
  51.2 11.0 %collective-permute-start = (bf16[24,2048]{1,0:T(8,128)(2,1)S(1)}, bf16[24,2048]{1,0:T(8,128)(2,1)S(1)}, u32[]{:S(2)}, u32[]{:S(2)}) collective-permute-start(bf16[24,2048]{1,0:T(8,128)(2,1)S(1)} %get-tuple-element.77), channel_id=1, source_target_pairs={{0,256},{1,257},{2,258},{3,259},{4,260},{5,261},{6,262},{7,263},{8... | collective-permute-start | bytes 294920 | tf_op jit(solution)/shard_map/cond/branch_1_fun/ppermute | solution.py:26
  56.9 14.3 %collective-permute-start.4 = (bf16[72,2048]{1,0:T(8,128)(2,1)S(1)}, bf16[72,2048]{1,0:T(8,128)(2,1)S(1)}, u32[]{:S(2)}, u32[]{:S(2)}) collective-permute-start(bf16[72,2048]{1,0:T(8,128)(2,1)S(1)} %pad_maximum_fusion.2), channel_id=1, source_target_pairs={{0,8},{1,9},{2,10},{3,11},{4,12},{5,13},{6,14},{7,15},{8,0},{9,1},... | collective-permute-start | bytes 884744 | tf_op jit(solution)/shard_map/cond/branch_1_fun/ppermute | solution.py:26
  62.2 3.2 %collective-permute-start.1 = (bf16[24,2048]{1,0:T(8,128)(2,1)S(1)}, bf16[24,2048]{1,0:T(8,128)(2,1)S(1)}, u32[]{:S(2)}, u32[]{:S(2)}) collective-permute-start(bf16[24,2048]{1,0:T(8,128)(2,1)S(1)} %collective-permute-done), channel_id=1, source_target_pairs={{0,8},{1,9},{2,10},{3,11},{4,12},{5,13},{6,14},{7,15},{8,0},{9,1},... | collective-permute-start | bytes 294920 | tf_op jit(solution)/shard_map/cond/branch_1_fun/ppermute | solution.py:26
  67.1 12.2 %collective-permute-start.5 = (bf16[96,2048]{1,0:T(8,128)(2,1)S(1)}, bf16[96,2048]{1,0:T(8,128)(2,1)}, u32[]{:S(2)}, u32[]{:S(2)}) collective-permute-start(bf16[96,2048]{1,0:T(8,128)(2,1)S(1)} %pad_maximum_fusion), channel_id=1, source_target_pairs={{0,496},{1,497},{2,498},{3,499},{4,500},{5,501},{6,502},{7,503},{8... | collective-permute-start | bytes 1179656 | tf_op jit(solution)/shard_map/cond/branch_1_fun/ppermute | solution.py:26
  72.8 15.5 %collective-permute-start.6 = (bf16[96,2048]{1,0:T(8,128)(2,1)S(1)}, bf16[96,2048]{1,0:T(8,128)(2,1)}, u32[]{:S(2)}, u32[]{:S(2)}) collective-permute-start(bf16[96,2048]{1,0:T(8,128)(2,1)S(1)} %pad_maximum_fusion.1), channel_id=1, source_target_pairs={{0,496},{1,497},{2,498},{3,499},{4,500},{5,501},{6,502},{7,503},{8... | collective-permute-start | bytes 1179656 | tf_op jit(solution)/shard_map/cond/branch_1_fun/ppermute | solution.py:26
  79.4 12.4 %collective-permute-start.9 = (bf16[96,2048]{1,0:T(8,128)(2,1)}, bf16[96,2048]{1,0:T(8,128)(2,1)}, u32[]{:S(2)}, u32[]{:S(2)}) collective-permute-start(bf16[96,2048]{1,0:T(8,128)(2,1)} %collective-permute-done.5), channel_id=1, source_target_pairs={{0,496},{1,497},{2,498},{3,499},{4,500},{5,501},{6,502},{7,503},{8... | collective-permute-start | bytes 1179656 | tf_op jit(solution)/shard_map/cond/branch_1_fun/ppermute | solution.py:26
  81.3 12.6 %collective-permute-start.7 = (bf16[96,2048]{1,0:T(8,128)(2,1)}, bf16[96,2048]{1,0:T(8,128)(2,1)}, u32[]{:S(2)}, u32[]{:S(2)}) collective-permute-start(bf16[96,2048]{1,0:T(8,128)(2,1)} %collective-permute-done.5), channel_id=1, source_target_pairs={{0,8},{1,9},{2,10},{3,11},{4,12},{5,13},{6,14},{7,15},{8,0},{9,1},... | collective-permute-start | bytes 1179656 | tf_op jit(solution)/shard_map/cond/branch_1_fun/ppermute | solution.py:26
  88.3 5.6 %collective-permute-start.8 = (bf16[96,2048]{1,0:T(8,128)(2,1)}, bf16[96,2048]{1,0:T(8,128)(2,1)}, u32[]{:S(2)}, u32[]{:S(2)}) collective-permute-start(bf16[96,2048]{1,0:T(8,128)(2,1)} %collective-permute-done.6), channel_id=1, source_target_pairs={{0,8},{1,9},{2,10},{3,11},{4,12},{5,13},{6,14},{7,15},{8,0},{9,1},... | collective-permute-start | bytes 1179656 | tf_op jit(solution)/shard_map/cond/branch_1_fun/ppermute | solution.py:26
  91.8 3.9 %collective-permute-start.10 = (bf16[96,2048]{1,0:T(8,128)(2,1)}, bf16[96,2048]{1,0:T(8,128)(2,1)}, u32[]{:S(2)}, u32[]{:S(2)}) collective-permute-start(bf16[96,2048]{1,0:T(8,128)(2,1)} %collective-permute-done.9), channel_id=1, source_target_pairs={{0,8},{1,9},{2,10},{3,11},{4,12},{5,13},{6,14},{7,15},{8,0},{9,1},... | collective-permute-start | bytes 1179656 | tf_op jit(solution)/shard_map/cond/branch_1_fun/ppermute | solution.py:26
  96.9 11.8 %collective-permute-start.15 = (bf16[192,2048]{1,0:T(8,128)(2,1)S(1)}, bf16[192,2048]{1,0:T(8,128)(2,1)S(1)}, u32[]{:S(2)}, u32[]{:S(2)}) collective-permute-start(bf16[192,2048]{1,0:T(8,128)(2,1)S(1)} %bitcast.8), channel_id=1, source_target_pairs={{0,8},{1,9},{2,10},{3,11},{4,12},{5,13},{6,14},{7,15},{8,0},{9,1},... | collective-permute-start | bytes 2359304 | tf_op jit(solution)/shard_map/ppermute | solution.py:26
  99.0 2.1 %copy-start = (bf16[960,2048]{1,0:T(8,128)(2,1)S(1)}, bf16[960,2048]{1,0:T(8,128)(2,1)}, u32[]{:S(2)}) copy-start(bf16[960,2048]{1,0:T(8,128)(2,1)} %all-gather.3.cloned.1.call-done) | copy-start | bytes 11796484
  101.1 7.6 %copy-start.1 = (bf16[960,2048]{1,0:T(8,128)(2,1)S(1)}, bf16[960,2048]{1,0:T(8,128)(2,1)}, u32[]{:S(2)}) copy-start(bf16[960,2048]{1,0:T(8,128)(2,1)} %all-gather.3.cloned.1.call-done) | copy-start | bytes 11796484
  115.9 4.2 %collective-permute-start.16 = (f32[33,24,192]{2,1,0:T(8,128)S(1)}, f32[33,24,192]{2,1,0:T(8,128)S(1)}, u32[]{:S(2)}, u32[]{:S(2)}) collective-permute-start(f32[33,24,192]{2,1,0:T(8,128)S(1)} %get-tuple-element.73), channel_id=1, source_target_pairs={{0,8},{1,9},{2,10},{3,11},{4,12},{5,13},{6,14},{7,15},{8,0},{9,1},... | collective-permute-start | bytes 1824776 | tf_op jit(solution)/shard_map/ppermute | solution.py:26
Sparse Core Ops, SparseCore 0:
  38.6 50.4 all-gather.2

commit v5 on v4

v5 whole, which is shorter than its diff:
```python
import functools

import jax
import jax.numpy as jnp
from jax import lax
from jax.experimental import pallas as pl
from jax.experimental.pallas import tpu as pltpu
from jax.sharding import PartitionSpec as P

LANES = 2048
UNITS = (
    (0, True), (4, True), (8, True), (12, False), (16, True),
    (1, True), (5, True), (9, True), (13, False),
    (15, False), (11, False), (7, False), (3, True),
    (2, True), (6, True), (14, False), (10, False),
)


def permuted(value, move):
    wide, narrow = lax.axis_size("wide"), lax.axis_size("narrow")
    pairs = []
    for w in range(wide):
        for n in range(narrow):
            to_w, to_n = move(w, n)
            pairs.append((w * narrow + n, (to_w % wide) * narrow + to_n % narrow))
    return lax.ppermute(value, ("wide", "narrow"), pairs)


def by_chips(value, first, second):
    return permuted(value, lambda w, n: (w + 2 * (second if w % 2 else first), n))


def from_partner(value):
    return permuted(value, lambda w, n: (w ^ 1, n))


def gather_wide(unit, four_mine, core, piece):
    eight = by_chips(four_mine, -4, 4)
    four = jnp.concatenate([four_mine, by_chips(unit[piece:], -4, -12)], axis=0)
    sixteen_mine = by_chips(unit[:piece], -16, -16)
    sixteen = jnp.concatenate([sixteen_mine, from_partner(sixteen_mine)], axis=0)
    start = jnp.where(core == 0, unit, sixteen)
    stop = jnp.where(core == 0, sixteen, unit)
    near = by_chips(jnp.concatenate([start, four], axis=0), -1, 1)
    got = from_partner(jnp.concatenate([four, eight], axis=0))
    two = by_chips(near, -1, 1)
    eights = jnp.concatenate([eight, got[2 * piece :]], axis=0)
    twelve = got[: 2 * piece]
    near_late = by_chips(jnp.concatenate([eights, twelve], axis=0), -1, 1)
    far = from_partner(near)
    two_far = from_partner(two)
    far_late = from_partner(near_late)
    return start, four, eights, twelve, stop, near, near_late, far, far_late, two, two_far


def dots_of(rows, envs):
    return lax.dot_general(rows, envs, (((1,), (1,)), ((), ())), preferred_element_type=jnp.float32)


def two_parts(value):
    top = value.astype(jnp.bfloat16)
    return top, (value - top.astype(jnp.float32)).astype(jnp.bfloat16)


class Copies:
    def __init__(self, sems):
        self.sems, self.count = sems, 0

    def __call__(self, source, target):
        copy = pltpu.make_async_copy(source, target, self.sems.at[self.count])
        self.count += 1
        copy.start()
        return copy


def copied_envs(copied, gathered, envs, shards_x, rows_d):
    return [
        copied(gathered.at[i, pl.ds(0, rows_d)], envs.at[pl.ds(i * rows_d, rows_d)]) for i in range(shards_x)
    ]


def rows_kernel(shards_x, rows_d, width, *refs):
    gathered, points = refs[0], refs[1:12]
    high_out, low_out = refs[12:14]
    envs, rows, high, low, sems = refs[14:]
    copied = Copies(sems)
    waits = copied_envs(copied, gathered, envs, shards_x, rows_d)
    place, ends = 0, []
    for point in points:
        size = point.shape[0]
        ends.append((place + size, copied(point, rows.at[pl.ds(place, size)])))
        place += size
    step = place // 3
    for copy in waits:
        copy.wait()
    waits, done = [], 0
    for m in range(3):
        while done < len(ends) and (done == 0 or ends[done - 1][0] < (m + 1) * step):
            ends[done][1].wait()
            done += 1
        part = pl.ds(m * step, step)
        value = dots_of(rows[part, :], envs[...])
        top, rest = two_parts(value * value / width)
        high[part, :] = top
        low[part, :] = rest
        waits += [copied(high.at[part], high_out.at[part]), copied(low.at[part], low_out.at[part])]
    for copy in waits:
        copy.wait()


def products_kernel(piece, shards_x, rows_d, width, env_count, core_ref, *refs):
    gathered, other, high_in, low_in = refs[:4]
    own_ref, send_ref = refs[4:6]
    envs, rows, high, low, dots, columns, both, sems = refs[6:]
    count = len(UNITS) * 2 * piece
    block = 2 * shards_x * piece
    at = 2 * block
    away = columns.shape[1] // 2
    copied = Copies(sems)
    waits = copied_envs(copied, gathered, envs, shards_x, rows_d)
    for i in range(shards_x):
        waits.append(copied(gathered.at[i, pl.ds(rows_d, 2 * piece)], rows.at[pl.ds(2 * i * piece, 2 * piece)]))
    waits.append(copied(other, rows.at[pl.ds(block, block)]))
    late = [copied(high_in, high), copied(low_in, low)]
    pick = (lax.broadcasted_iota(jnp.int32, (16, LANES), 1) == width) & (
        lax.broadcasted_iota(jnp.int32, (16, LANES), 0) == 0
    )
    rows[pl.ds(at, 16), :] = pick.astype(jnp.float32).astype(jnp.bfloat16)
    for copy in waits:
        copy.wait()

    dots[...] = dots_of(rows[...], envs[...])
    weights = dots[pl.ds(at, 8), :][:1] / env_count
    columns[...] = jnp.zeros_like(columns)
    for which in range(2):
        parts = []
        for low_y in range(2):
            for i in range(shards_x):
                value = dots[pl.ds(which * block + (2 * i + low_y) * piece, piece), :]
                parts.append(value * value / width * weights)
        top, rest = two_parts(jnp.concatenate(parts, axis=0))
        columns[0, pl.ds(which * away, block), :] = top
        columns[1, pl.ds(which * away, block), :] = rest
    for copy in late:
        copy.wait()

    step = count // 3

    def some_products(m, carry):
        part = pl.ds(pl.multiple_of(m * step, 16), step)
        both[part, :] = (
            dots_of(high[part, :], columns[0]) + dots_of(high[part, :], columns[1]) + dots_of(low[part, :], columns[0])
        )
        return carry

    lax.fori_loop(0, 3, some_products, 0)

    core = core_ref[0]
    for u, (distance, first_own) in enumerate(UNITS):
        for b in range(2):
            part = pl.ds((2 * u + b) * piece, piece)
            mine = first_own == (b == 0)
            ahead = 2 * distance + (0 if mine else 1)
            behind = (33 if mine else 32) - 2 * distance
            if ahead < 33:
                own_ref[ahead + core * (32 - 2 * ahead)] = both[part, pl.ds(0, block)]
            if behind < 33:
                send_ref[behind + (1 - core) * (32 - 2 * behind)] = both[part, pl.ds(away, block)]


def rows_call(gathered, points, rows_d, width):
    shards_x = gathered.shape[0]
    env_rows = shards_x * rows_d
    count = sum(p.shape[0] for p in points)
    shape = jax.ShapeDtypeStruct((count, env_rows), jnp.bfloat16)
    anywhere = pl.BlockSpec(memory_space=pl.ANY)
    return pl.pallas_call(
        functools.partial(rows_kernel, shards_x, rows_d, width),
        out_shape=(shape, shape),
        in_specs=[anywhere] * (1 + len(points)),
        out_specs=(anywhere, anywhere),
        scratch_shapes=[
            pltpu.VMEM((env_rows, LANES), jnp.bfloat16),
            pltpu.VMEM((count, LANES), jnp.bfloat16),
            pltpu.VMEM((count, env_rows), jnp.bfloat16),
            pltpu.VMEM((count, env_rows), jnp.bfloat16),
            pltpu.SemaphoreType.DMA((len(points) + shards_x + 6,)),
        ],
        compiler_params=pltpu.CompilerParams(vmem_limit_bytes=58 * 1024 * 1024),
        cost_estimate=pl.CostEstimate(
            flops=2 * env_rows * count * LANES, bytes_accessed=9 * 10**6, transcendentals=0
        ),
    )(gathered, *points)


def products_call(core, gathered, other, high, low, piece, rows_d, width, env_count):
    shards_x = gathered.shape[0]
    env_rows = shards_x * rows_d
    count = high.shape[0]
    block = 2 * shards_x * piece
    lanes = 2 * (-(-block // 128) * 128)
    shape = jax.ShapeDtypeStruct((33, piece, block), jnp.float32)
    anywhere = pl.BlockSpec(memory_space=pl.ANY)
    vmem = pl.BlockSpec(memory_space=pltpu.VMEM)
    return pl.pallas_call(
        functools.partial(products_kernel, piece, shards_x, rows_d, width, env_count),
        out_shape=(shape, shape),
        in_specs=[pl.BlockSpec(memory_space=pltpu.SMEM)] + [anywhere] * 4,
        out_specs=(vmem, vmem),
        scratch_shapes=[
            pltpu.VMEM((env_rows, LANES), jnp.bfloat16),
            pltpu.VMEM((2 * block + 16, LANES), jnp.bfloat16),
            pltpu.VMEM((count, env_rows), jnp.bfloat16),
            pltpu.VMEM((count, env_rows), jnp.bfloat16),
            pltpu.VMEM((2 * block + 16, env_rows), jnp.float32),
            pltpu.VMEM((2, lanes, env_rows), jnp.bfloat16),
            pltpu.VMEM((count, lanes), jnp.float32),
            pltpu.SemaphoreType.DMA((3 + 2 * shards_x,)),
        ],
        compiler_params=pltpu.CompilerParams(vmem_limit_bytes=58 * 1024 * 1024),
        cost_estimate=pl.CostEstimate(
            flops=2 * env_rows * (2 * block * LANES + 6 * count * block), bytes_accessed=9 * 10**6, transcendentals=0
        ),
    )(core, gathered, other, high, low)


def shards(descriptors, env_weights, sparse_points):
    core = lax.axis_index("wide") % 2
    narrow = lax.axis_size("narrow")
    wide = lax.axis_size("wide")
    shards_x = narrow // 2
    width = descriptors.shape[1]
    half = descriptors.shape[0] // 2
    env_count = descriptors.shape[0] * narrow
    piece = sparse_points.shape[0]

    mine = jnp.pad(sparse_points, ((0, 0), (0, LANES - width)))
    half_envs = lax.dynamic_slice_in_dim(
        jnp.concatenate(
            [descriptors, env_weights[:, None], jnp.zeros((2 * half, LANES - width - 1), descriptors.dtype)], axis=1
        ),
        core * half,
        half,
        0,
    )
    half_envs, mine = lax.optimization_barrier((half_envs, mine))
    across_envs = permuted(
        half_envs, lambda w, n: (w + (wide // 2 if w % 2 else 0), n + shards_x)
    )
    other = from_partner(mine)
    mine, other = lax.optimization_barrier((mine, other))
    four_mine = by_chips(mine, -4, -12)
    across_mine = permuted(mine, lambda w, n: (w, n + shards_x))
    unit = jnp.concatenate([mine, other], axis=0)
    at_zero = lax.axis_index("narrow") < shards_x
    payload = jnp.concatenate(
        [
            half_envs,
            across_envs,
            jnp.where(at_zero, mine, across_mine),
            jnp.where(at_zero, across_mine, mine),
        ],
        axis=0,
    )
    payload, unit, four_mine = lax.optimization_barrier((payload, unit, four_mine))
    groups = [list(range(shards_x)), list(range(shards_x, narrow))]
    gathered = lax.all_gather(payload, "narrow", axis=0, tiled=False, axis_index_groups=groups)

    def none(*_):
        return tuple(jnp.zeros((n * piece, LANES), unit.dtype) for n in (2, 2, 2, 2, 2, 4, 4, 4, 4, 4, 4))

    points = lax.cond(
        1 + jnp.minimum(lax.axis_index("wide"), 0) > 0,
        lambda *values: gather_wide(*values, core, piece),
        none,
        unit,
        four_mine,
    )
    gathered, points = lax.optimization_barrier((gathered, points))
    block_other = from_partner(gathered[:, 2 * half :].reshape(-1, LANES))
    high, low = rows_call(gathered, points, 2 * half, width)
    kept, sent = products_call(
        core.reshape(1), gathered, block_other, high, low, piece, 2 * half, width, env_count
    )
    return (kept + from_partner(sent))[None]


def solution(mesh):
    in_specs = (P("narrow", None), P("narrow"), P(("wide", "narrow"), None))
    out_specs = P("wide", None, "narrow", None)
    return jax.shard_map(shards, mesh=mesh, in_specs=in_specs, out_specs=out_specs, check_vma=False)
```

time: 129 us -> 132 us (1.023)
  waiting for transfers between devices: 19.7 us -> 21.4 us
  starting transfers between devices: 68 us -> 69.6 us
    ppermute x17, waiting for transfers between devices: 19.7 us -> 21.4 us  [permuted(): return lax.ppermute(value, ('wide', 'narrow'), pairs)]
    ppermute x17, starting transfers between devices: 68 us -> 69.6 us  [permuted(): return lax.ppermute(value, ('wide', 'narrow'), pairs)]
  transfers between devices with their start and end apart: 18 -> 18, of which waited for: 7 -> 6; matrix products, arithmetic and copies ran while one was open for 5% -> 3% of each run, Pallas kernels for 6% -> 5%
where the time goes in v5:
time: 132 us
  starting transfers between devices  69.6 us (53%)
  waiting for transfers between devices  21.4 us (16%)
  Pallas kernels  15.1 us (11%)
  between operations  13.6 us (10%)
  other arithmetic  5.87 us (4%)
  local copies, waits for them, and re-layouts  5.78 us (4%)
    ppermute x17, starting transfers between devices, permuted(): return lax.ppermute(value, ('wide', 'narrow'), pairs)  69.6 us
    ppermute x17, waiting for transfers between devices, permuted(): return lax.ppermute(value, ('wide', 'narrow'), pairs)  21.4 us
    pallas_call x1, Pallas kernels, products_call(): pl.pallas_call(functools.partial(products_kernel, piece, shards_x, rows_d...  7.92 us
    pallas_call x1, Pallas kernels, rows_call(): pl.pallas_call(functools.partial(rows_kernel, shards_x, rows_d, width), o...  7.17 us
  transfers between devices with their start and end apart: 18, of which 6 were waited for; matrix products, arithmetic and copies ran while one was open for 3% of the time, Pallas kernels for 5%

profile of v5, /device:TPU:1, one launch (start us, length us, event | category | flops | bytes accessed | tf_op | source)
XLA Modules:
  0.0 131.6 jit_solution(9835819088552664070)
XLA Ops:
  6.5 0.7 broadcast_in_dim.12
  7.3 0.9 pad.4
  8.2 1.2 concatenate.30
  9.5 8.8 %collective-permute-start.12 = (bf16[24,2048]{1,0:T(8,128)(2,1)S(1)}, bf16[24,2048]{1,0:T(8,128)(2,1)S(1)}, u32[]{:S(2)}, u32[]{:S(2)}) collective-permute-start(bf16[24,2048]{1,0:T(8,128)(2,1)S(1)} %pad.4), channel_id=1, source_target_pairs={{0,8},{1,9},{2,10},{3,11},{4,12},{5,13},{6,14},{7,15},{8,0},{9,1},... | collective-permute-start | bytes 294920 | tf_op jit(solution)/shard_map/ppermute | solution.py:26
  18.3 1.9 %collective-permute-start.11 = (bf16[96,2048]{1,0:T(8,128)(2,1)S(1)}, bf16[96,2048]{1,0:T(8,128)(2,1)S(1)}, u32[]{:S(2)}, u32[]{:S(2)}) collective-permute-start(bf16[96,2048]{1,0:T(8,128)(2,1)S(1)} %constant_dynamic-slice_fusion), channel_id=1, source_target_pairs={{0,4},{1,5},{2,6},{3,7},{4,0},{5,1},{6,2},{7,3},{8,268},{9,269},{1... | collective-permute-start | bytes 1179656 | tf_op jit(solution)/shard_map/ppermute | solution.py:26
  20.2 0.0 collective-permute-done.12
  20.2 1.9 %collective-permute-start.13 = (bf16[24,2048]{1,0:T(8,128)(2,1)S(1)}, bf16[24,2048]{1,0:T(8,128)(2,1)S(1)}, u32[]{:S(2)}, u32[]{:S(2)}) collective-permute-start(bf16[24,2048]{1,0:T(8,128)(2,1)S(1)} %pad.4), channel_id=1, source_target_pairs={{0,4},{1,5},{2,6},{3,7},{4,0},{5,1},{6,2},{7,3},{8,12},{9,13},{10,... | collective-permute-start | bytes 294920 | tf_op jit(solution)/shard_map/ppermute | solution.py:26
  22.2 7.1 %collective-permute-start.14 = (bf16[24,2048]{1,0:T(8,128)(2,1)S(1)}, bf16[24,2048]{1,0:T(8,128)(2,1)S(1)}, u32[]{:S(2)}, u32[]{:S(2)}) collective-permute-start(bf16[24,2048]{1,0:T(8,128)(2,1)S(1)} %pad.4), channel_id=1, source_target_pairs={{0,448},{1,449},{2,450},{3,451},{4,452},{5,453},{6,454},{7,455},{8... | collective-permute-start | bytes 294920 | tf_op jit(solution)/shard_map/ppermute | solution.py:26
  29.3 0.0 collective-permute-done.13
  29.3 0.0 collective-permute-done.11
  29.3 1.0 pad_maximum_fusion.5
  30.3 4.0 %collective-permute-done.14 = bf16[24,2048]{1,0:T(8,128)(2,1)S(1)} collective-permute-done((bf16[24,2048]{1,0:T(8,128)(2,1)S(1)}, bf16[24,2048]{1,0:T(8,128)(2,1)S(1)}, u32[]{:S(2)}, u32[]{:S(2)}) %collective-permute-start.14) | collective-permute-done | bytes 98336 | tf_op jit(solution)/shard_map/ppermute | solution.py:26
  34.3 0.0 all-gather.3.cloned.1.call-update
  34.3 64.5 %conditional.1 = (bf16[48,2048]{1,0:T(8,128)(2,1)}, bf16[48,2048]{1,0:T(8,128)(2,1)S(1)}, bf16[48,2048]{1,0:T(8,128)(2,1)S(1)}, bf16[48,2048]{1,0:T(8,128)(2,1)}...) conditional(s32[]{:T(128)} %convert_element_type.5, () %tuple.20, ...), branch_computations={%region_0.1_spmd, %region_1.2_spmd} | conditional | flops 4227073 | bytes 17302042 | solution.py:272
  34.3 7.9 %collective-permute-start.3 = (bf16[24,2048]{1,0:T(8,128)(2,1)S(1)}, bf16[24,2048]{1,0:T(8,128)(2,1)S(1)}, u32[]{:S(2)}, u32[]{:S(2)}) collective-permute-start(bf16[24,2048]{1,0:T(8,128)(2,1)S(1)} %get-tuple-element.13), channel_id=1, source_target_pairs={{0,448},{1,449},{2,450},{3,451},{4,452},{5,453},{6,454},{7,455},{8... | collective-permute-start | bytes 294920 | tf_op jit(solution)/shard_map/cond/branch_1_fun/ppermute | solution.py:26
  42.3 10.2 %collective-permute-start.2 = (bf16[24,2048]{1,0:T(8,128)(2,1)S(1)}, bf16[24,2048]{1,0:T(8,128)(2,1)S(1)}, u32[]{:S(2)}, u32[]{:S(2)}) collective-permute-start(bf16[24,2048]{1,0:T(8,128)(2,1)S(1)} %get-tuple-element.84), channel_id=1, source_target_pairs={{0,448},{1,449},{2,450},{3,451},{4,452},{5,453},{6,454},{7,455},{8... | collective-permute-start | bytes 294920 | tf_op jit(solution)/shard_map/cond/branch_1_fun/ppermute | solution.py:26
  52.5 3.5 %collective-permute-start = (bf16[24,2048]{1,0:T(8,128)(2,1)S(1)}, bf16[24,2048]{1,0:T(8,128)(2,1)S(1)}, u32[]{:S(2)}, u32[]{:S(2)}) collective-permute-start(bf16[24,2048]{1,0:T(8,128)(2,1)S(1)} %get-tuple-element.85), channel_id=1, source_target_pairs={{0,256},{1,257},{2,258},{3,259},{4,260},{5,261},{6,262},{7,263},{8... | collective-permute-start | bytes 294920 | tf_op jit(solution)/shard_map/cond/branch_1_fun/ppermute | solution.py:26
  56.0 0.0 collective-permute-done.3
  56.0 0.0 collective-permute-done.2
  56.1 9.3 %collective-permute-start.4 = (bf16[72,2048]{1,0:T(8,128)(2,1)S(1)}, bf16[72,2048]{1,0:T(8,128)(2,1)S(1)}, u32[]{:S(2)}, u32[]{:S(2)}) collective-permute-start(bf16[72,2048]{1,0:T(8,128)(2,1)S(1)} %pad_maximum_fusion.2), channel_id=1, source_target_pairs={{0,8},{1,9},{2,10},{3,11},{4,12},{5,13},{6,14},{7,15},{8,0},{9,1},... | collective-permute-start | bytes 884744 | tf_op jit(solution)/shard_map/cond/branch_1_fun/ppermute | solution.py:26
  65.4 0.0 collective-permute-done
  65.4 1.9 %collective-permute-start.1 = (bf16[24,2048]{1,0:T(8,128)(2,1)S(1)}, bf16[24,2048]{1,0:T(8,128)(2,1)S(1)}, u32[]{:S(2)}, u32[]{:S(2)}) collective-permute-start(bf16[24,2048]{1,0:T(8,128)(2,1)S(1)} %collective-permute-done), channel_id=1, source_target_pairs={{0,8},{1,9},{2,10},{3,11},{4,12},{5,13},{6,14},{7,15},{8,0},{9,1},... | collective-permute-start | bytes 294920 | tf_op jit(solution)/shard_map/cond/branch_1_fun/ppermute | solution.py:26
  67.3 1.3 collective-permute-done.1
  68.6 0.7 broadcast_select_fusion
  69.3 1.0 pad_maximum_fusion
  70.3 1.9 %collective-permute-start.5 = (bf16[96,2048]{1,0:T(8,128)(2,1)S(1)}, bf16[96,2048]{1,0:T(8,128)(2,1)}, u32[]{:S(2)}, u32[]{:S(2)}) collective-permute-start(bf16[96,2048]{1,0:T(8,128)(2,1)S(1)} %pad_maximum_fusion), channel_id=1, source_target_pairs={{0,496},{1,497},{2,498},{3,499},{4,500},{5,501},{6,502},{7,503},{8... | collective-permute-start | bytes 1179656 | tf_op jit(solution)/shard_map/cond/branch_1_fun/ppermute | solution.py:26
  72.2 0.0 collective-permute-done.4
  72.2 0.7 slice.17
  72.9 1.0 pad_maximum_fusion.1
  73.9 1.9 %collective-permute-start.6 = (bf16[96,2048]{1,0:T(8,128)(2,1)S(1)}, bf16[96,2048]{1,0:T(8,128)(2,1)}, u32[]{:S(2)}, u32[]{:S(2)}) collective-permute-start(bf16[96,2048]{1,0:T(8,128)(2,1)S(1)} %pad_maximum_fusion.1), channel_id=1, source_target_pairs={{0,496},{1,497},{2,498},{3,499},{4,500},{5,501},{6,502},{7,503},{8... | collective-permute-start | bytes 1179656 | tf_op jit(solution)/shard_map/cond/branch_1_fun/ppermute | solution.py:26
  75.8 6.7 %collective-permute-done.5 = bf16[96,2048]{1,0:T(8,128)(2,1)} collective-permute-done((bf16[96,2048]{1,0:T(8,128)(2,1)S(1)}, bf16[96,2048]{1,0:T(8,128)(2,1)}, u32[]{:S(2)}, u32[]{:S(2)}) %collective-permute-start.5) | collective-permute-done | bytes 393248 | tf_op jit(solution)/shard_map/cond/branch_1_fun/ppermute | solution.py:26
  82.5 1.9 %collective-permute-start.9 = (bf16[96,2048]{1,0:T(8,128)(2,1)}, bf16[96,2048]{1,0:T(8,128)(2,1)}, u32[]{:S(2)}, u32[]{:S(2)}) collective-permute-start(bf16[96,2048]{1,0:T(8,128)(2,1)} %collective-permute-done.5), channel_id=1, source_target_pairs={{0,496},{1,497},{2,498},{3,499},{4,500},{5,501},{6,502},{7,503},{8... | collective-permute-start | bytes 1179656 | tf_op jit(solution)/shard_map/cond/branch_1_fun/ppermute | solution.py:26
  84.4 3.2 %collective-permute-start.7 = (bf16[96,2048]{1,0:T(8,128)(2,1)}, bf16[96,2048]{1,0:T(8,128)(2,1)}, u32[]{:S(2)}, u32[]{:S(2)}) collective-permute-start(bf16[96,2048]{1,0:T(8,128)(2,1)} %collective-permute-done.5), channel_id=1, source_target_pairs={{0,8},{1,9},{2,10},{3,11},{4,12},{5,13},{6,14},{7,15},{8,0},{9,1},... | collective-permute-start | bytes 1179656 | tf_op jit(solution)/shard_map/cond/branch_1_fun/ppermute | solution.py:26
  87.6 0.0 collective-permute-done.6
  87.6 1.9 %collective-permute-start.8 = (bf16[96,2048]{1,0:T(8,128)(2,1)}, bf16[96,2048]{1,0:T(8,128)(2,1)}, u32[]{:S(2)}, u32[]{:S(2)}) collective-permute-start(bf16[96,2048]{1,0:T(8,128)(2,1)} %collective-permute-done.6), channel_id=1, source_target_pairs={{0,8},{1,9},{2,10},{3,11},{4,12},{5,13},{6,14},{7,15},{8,0},{9,1},... | collective-permute-start | bytes 1179656 | tf_op jit(solution)/shard_map/cond/branch_1_fun/ppermute | solution.py:26
  89.6 5.4 %collective-permute-done.9 = bf16[96,2048]{1,0:T(8,128)(2,1)} collective-permute-done((bf16[96,2048]{1,0:T(8,128)(2,1)}, bf16[96,2048]{1,0:T(8,128)(2,1)}, u32[]{:S(2)}, u32[]{:S(2)}) %collective-permute-start.9) | collective-permute-done | bytes 393248 | tf_op jit(solution)/shard_map/cond/branch_1_fun/ppermute | solution.py:26
  94.9 1.9 %collective-permute-start.10 = (bf16[96,2048]{1,0:T(8,128)(2,1)}, bf16[96,2048]{1,0:T(8,128)(2,1)}, u32[]{:S(2)}, u32[]{:S(2)}) collective-permute-start(bf16[96,2048]{1,0:T(8,128)(2,1)} %collective-permute-done.9), channel_id=1, source_target_pairs={{0,8},{1,9},{2,10},{3,11},{4,12},{5,13},{6,14},{7,15},{8,0},{9,1},... | collective-permute-start | bytes 1179656 | tf_op jit(solution)/shard_map/cond/branch_1_fun/ppermute | solution.py:26
  96.9 0.0 collective-permute-done.7
  96.9 0.0 collective-permute-done.8
  96.9 2.0 %collective-permute-done.10 = bf16[96,2048]{1,0:T(8,128)(2,1)} collective-permute-done((bf16[96,2048]{1,0:T(8,128)(2,1)}, bf16[96,2048]{1,0:T(8,128)(2,1)}, u32[]{:S(2)}, u32[]{:S(2)}) %collective-permute-start.10) | collective-permute-done | bytes 393248 | tf_op jit(solution)/shard_map/cond/branch_1_fun/ppermute | solution.py:26
  98.9 1.2 slice.15
  100.1 2.0 %collective-permute-start.15 = (bf16[192,2048]{1,0:T(8,128)(2,1)S(1)}, bf16[192,2048]{1,0:T(8,128)(2,1)S(1)}, u32[]{:S(2)}, u32[]{:S(2)}) collective-permute-start(bf16[192,2048]{1,0:T(8,128)(2,1)S(1)} %bitcast.5), channel_id=1, source_target_pairs={{0,8},{1,9},{2,10},{3,11},{4,12},{5,13},{6,14},{7,15},{8,0},{9,1},... | collective-permute-start | bytes 2359304 | tf_op jit(solution)/shard_map/ppermute | solution.py:26
  102.1 7.2 %shard_map.37 = (bf16[816,768]{1,0:T(8,128)(2,1)}, bf16[816,768]{1,0:T(8,128)(2,1)}) custom-call(bf16[4,240,2048]{2,1,0:T(8,128)(2,1)} %bitcast.7, bf16[48,2048]{1,0:T(8,128)(2,1)} %get-tuple-element.67.refs_1_, bf16[48,2048]{1,0:T(8,128)(2,1)S(1)} %get-tuple-element.68.refs_2_, bf16[48,2048]{1,0:T(8,128)(2,1)S(1)} %get-tuple-element.69.refs_3_, ...), custom_call_target="tpu_custom_call" | custom-call | flops 2566914048 | bytes 9000000 | tf_op jit(solution)/shard_map/pallas_call | solution.py:177
  109.3 0.9 copy-done
  110.3 7.9 %shard_map.38 = (f32[33,24,192]{2,1,0:T(8,128)}, f32[33,24,192]{2,1,0:T(8,128)}) custom-call(s32[1]{0:T(128)} %bitcast.core_ref, bf16[4,240,2048]{2,1,0:T(8,128)(2,1)} %bitcast.8, bf16[192,2048]{1,0:T(8,128)(2,1)} %copy-done, bf16[816,768]{1,0:T(8,128)(2,1)} %get-tuple-element.78.refs_2_, bf16[816,768]{1,0:T(8,128)(2,1)} %get-tuple-element.79.refs_3_), custom_call_target="tpu_custom_call" | custom-call | flops 2651848704 | bytes 9000000 | tf_op jit(solution)/shard_map/pallas_call | solution.py:205
  118.2 2.3 %collective-permute-start.16 = (f32[33,24,192]{2,1,0:T(8,128)}, f32[33,24,192]{2,1,0:T(8,128)S(1)}, u32[]{:S(2)}, u32[]{:S(2)}) collective-permute-start(f32[33,24,192]{2,1,0:T(8,128)} %get-tuple-element.81), channel_id=1, source_target_pairs={{0,8},{1,9},{2,10},{3,11},{4,12},{5,13},{6,14},{7,15},{8,0},{9,1},... | collective-permute-start | bytes 1824776 | tf_op jit(solution)/shard_map/ppermute | solution.py:26
  120.5 2.1 %collective-permute-done.16 = f32[33,24,192]{2,1,0:T(8,128)S(1)} collective-permute-done((f32[33,24,192]{2,1,0:T(8,128)}, f32[33,24,192]{2,1,0:T(8,128)S(1)}, u32[]{:S(2)}, u32[]{:S(2)}) %collective-permute-start.16) | collective-permute-done | bytes 608288 | tf_op jit(solution)/shard_map/ppermute | solution.py:26
  122.6 2.1 %add_bitcast_fusion = f32[1,33,24,192]{3,2,1,0:T(8,128)} fusion(f32[33,24,192]{2,1,0:T(8,128)} %get-tuple-element.80, f32[33,24,192]{2,1,0:T(8,128)S(1)} %collective-permute-done.16), kind=kLoop, calls=%fused_computation.10 | loop fusion | flops 152064 | bytes 1824768 | tf_op jit(solution)/shard_map/broadcast_in_dim | solution.py:285
  (15 shorter events, 0.2 us)
Async XLA Ops:
  6.5 92.4 %all-gather.3.cloned.1.call-start = ((), (), s32[]{:S(2)}) async-start(), calls=%async_computation | async-start | bytes 4915200 | tf_op jit(solution)/shard_map/all_gather | solution.py:267
  9.5 10.7 %collective-permute-start.12 = (bf16[24,2048]{1,0:T(8,128)(2,1)S(1)}, bf16[24,2048]{1,0:T(8,128)(2,1)S(1)}, u32[]{:S(2)}, u32[]{:S(2)}) collective-permute-start(bf16[24,2048]{1,0:T(8,128)(2,1)S(1)} %pad.4), channel_id=1, source_target_pairs={{0,8},{1,9},{2,10},{3,11},{4,12},{5,13},{6,14},{7,15},{8,0},{9,1},... | collective-permute-start | bytes 294920 | tf_op jit(solution)/shard_map/ppermute | solution.py:26
  18.3 11.0 %collective-permute-start.11 = (bf16[96,2048]{1,0:T(8,128)(2,1)S(1)}, bf16[96,2048]{1,0:T(8,128)(2,1)S(1)}, u32[]{:S(2)}, u32[]{:S(2)}) collective-permute-start(bf16[96,2048]{1,0:T(8,128)(2,1)S(1)} %constant_dynamic-slice_fusion), channel_id=1, source_target_pairs={{0,4},{1,5},{2,6},{3,7},{4,0},{5,1},{6,2},{7,3},{8,268},{9,269},{1... | collective-permute-start | bytes 1179656 | tf_op jit(solution)/shard_map/ppermute | solution.py:26
  20.2 9.0 %collective-permute-start.13 = (bf16[24,2048]{1,0:T(8,128)(2,1)S(1)}, bf16[24,2048]{1,0:T(8,128)(2,1)S(1)}, u32[]{:S(2)}, u32[]{:S(2)}) collective-permute-start(bf16[24,2048]{1,0:T(8,128)(2,1)S(1)} %pad.4), channel_id=1, source_target_pairs={{0,4},{1,5},{2,6},{3,7},{4,0},{5,1},{6,2},{7,3},{8,12},{9,13},{10,... | collective-permute-start | bytes 294920 | tf_op jit(solution)/shard_map/ppermute | solution.py:26
  22.2 12.1 %collective-permute-start.14 = (bf16[24,2048]{1,0:T(8,128)(2,1)S(1)}, bf16[24,2048]{1,0:T(8,128)(2,1)S(1)}, u32[]{:S(2)}, u32[]{:S(2)}) collective-permute-start(bf16[24,2048]{1,0:T(8,128)(2,1)S(1)} %pad.4), channel_id=1, source_target_pairs={{0,448},{1,449},{2,450},{3,451},{4,452},{5,453},{6,454},{7,455},{8... | collective-permute-start | bytes 294920 | tf_op jit(solution)/shard_map/ppermute | solution.py:26
  34.3 21.7 %collective-permute-start.3 = (bf16[24,2048]{1,0:T(8,128)(2,1)S(1)}, bf16[24,2048]{1,0:T(8,128)(2,1)S(1)}, u32[]{:S(2)}, u32[]{:S(2)}) collective-permute-start(bf16[24,2048]{1,0:T(8,128)(2,1)S(1)} %get-tuple-element.13), channel_id=1, source_target_pairs={{0,448},{1,449},{2,450},{3,451},{4,452},{5,453},{6,454},{7,455},{8... | collective-permute-start | bytes 294920 | tf_op jit(solution)/shard_map/cond/branch_1_fun/ppermute | solution.py:26
  42.3 13.8 %collective-permute-start.2 = (bf16[24,2048]{1,0:T(8,128)(2,1)S(1)}, bf16[24,2048]{1,0:T(8,128)(2,1)S(1)}, u32[]{:S(2)}, u32[]{:S(2)}) collective-permute-start(bf16[24,2048]{1,0:T(8,128)(2,1)S(1)} %get-tuple-element.84), channel_id=1, source_target_pairs={{0,448},{1,449},{2,450},{3,451},{4,452},{5,453},{6,454},{7,455},{8... | collective-permute-start | bytes 294920 | tf_op jit(solution)/shard_map/cond/branch_1_fun/ppermute | solution.py:26
  52.5 12.9 %collective-permute-start = (bf16[24,2048]{1,0:T(8,128)(2,1)S(1)}, bf16[24,2048]{1,0:T(8,128)(2,1)S(1)}, u32[]{:S(2)}, u32[]{:S(2)}) collective-permute-start(bf16[24,2048]{1,0:T(8,128)(2,1)S(1)} %get-tuple-element.85), channel_id=1, source_target_pairs={{0,256},{1,257},{2,258},{3,259},{4,260},{5,261},{6,262},{7,263},{8... | collective-permute-start | bytes 294920 | tf_op jit(solution)/shard_map/cond/branch_1_fun/ppermute | solution.py:26
  56.1 16.1 %collective-permute-start.4 = (bf16[72,2048]{1,0:T(8,128)(2,1)S(1)}, bf16[72,2048]{1,0:T(8,128)(2,1)S(1)}, u32[]{:S(2)}, u32[]{:S(2)}) collective-permute-start(bf16[72,2048]{1,0:T(8,128)(2,1)S(1)} %pad_maximum_fusion.2), channel_id=1, source_target_pairs={{0,8},{1,9},{2,10},{3,11},{4,12},{5,13},{6,14},{7,15},{8,0},{9,1},... | collective-permute-start | bytes 884744 | tf_op jit(solution)/shard_map/cond/branch_1_fun/ppermute | solution.py:26
  65.4 3.2 %collective-permute-start.1 = (bf16[24,2048]{1,0:T(8,128)(2,1)S(1)}, bf16[24,2048]{1,0:T(8,128)(2,1)S(1)}, u32[]{:S(2)}, u32[]{:S(2)}) collective-permute-start(bf16[24,2048]{1,0:T(8,128)(2,1)S(1)} %collective-permute-done), channel_id=1, source_target_pairs={{0,8},{1,9},{2,10},{3,11},{4,12},{5,13},{6,14},{7,15},{8,0},{9,1},... | collective-permute-start | bytes 294920 | tf_op jit(solution)/shard_map/cond/branch_1_fun/ppermute | solution.py:26
  70.3 12.2 %collective-permute-start.5 = (bf16[96,2048]{1,0:T(8,128)(2,1)S(1)}, bf16[96,2048]{1,0:T(8,128)(2,1)}, u32[]{:S(2)}, u32[]{:S(2)}) collective-permute-start(bf16[96,2048]{1,0:T(8,128)(2,1)S(1)} %pad_maximum_fusion), channel_id=1, source_target_pairs={{0,496},{1,497},{2,498},{3,499},{4,500},{5,501},{6,502},{7,503},{8... | collective-permute-start | bytes 1179656 | tf_op jit(solution)/shard_map/cond/branch_1_fun/ppermute | solution.py:26
  73.9 13.8 %collective-permute-start.6 = (bf16[96,2048]{1,0:T(8,128)(2,1)S(1)}, bf16[96,2048]{1,0:T(8,128)(2,1)}, u32[]{:S(2)}, u32[]{:S(2)}) collective-permute-start(bf16[96,2048]{1,0:T(8,128)(2,1)S(1)} %pad_maximum_fusion.1), channel_id=1, source_target_pairs={{0,496},{1,497},{2,498},{3,499},{4,500},{5,501},{6,502},{7,503},{8... | collective-permute-start | bytes 1179656 | tf_op jit(solution)/shard_map/cond/branch_1_fun/ppermute | solution.py:26
  82.5 12.4 %collective-permute-start.9 = (bf16[96,2048]{1,0:T(8,128)(2,1)}, bf16[96,2048]{1,0:T(8,128)(2,1)}, u32[]{:S(2)}, u32[]{:S(2)}) collective-permute-start(bf16[96,2048]{1,0:T(8,128)(2,1)} %collective-permute-done.5), channel_id=1, source_target_pairs={{0,496},{1,497},{2,498},{3,499},{4,500},{5,501},{6,502},{7,503},{8... | collective-permute-start | bytes 1179656 | tf_op jit(solution)/shard_map/cond/branch_1_fun/ppermute | solution.py:26
  84.4 12.5 %collective-permute-start.7 = (bf16[96,2048]{1,0:T(8,128)(2,1)}, bf16[96,2048]{1,0:T(8,128)(2,1)}, u32[]{:S(2)}, u32[]{:S(2)}) collective-permute-start(bf16[96,2048]{1,0:T(8,128)(2,1)} %collective-permute-done.5), channel_id=1, source_target_pairs={{0,8},{1,9},{2,10},{3,11},{4,12},{5,13},{6,14},{7,15},{8,0},{9,1},... | collective-permute-start | bytes 1179656 | tf_op jit(solution)/shard_map/cond/branch_1_fun/ppermute | solution.py:26
  87.6 9.3 %collective-permute-start.8 = (bf16[96,2048]{1,0:T(8,128)(2,1)}, bf16[96,2048]{1,0:T(8,128)(2,1)}, u32[]{:S(2)}, u32[]{:S(2)}) collective-permute-start(bf16[96,2048]{1,0:T(8,128)(2,1)} %collective-permute-done.6), channel_id=1, source_target_pairs={{0,8},{1,9},{2,10},{3,11},{4,12},{5,13},{6,14},{7,15},{8,0},{9,1},... | collective-permute-start | bytes 1179656 | tf_op jit(solution)/shard_map/cond/branch_1_fun/ppermute | solution.py:26
  94.9 3.9 %collective-permute-start.10 = (bf16[96,2048]{1,0:T(8,128)(2,1)}, bf16[96,2048]{1,0:T(8,128)(2,1)}, u32[]{:S(2)}, u32[]{:S(2)}) collective-permute-start(bf16[96,2048]{1,0:T(8,128)(2,1)} %collective-permute-done.9), channel_id=1, source_target_pairs={{0,8},{1,9},{2,10},{3,11},{4,12},{5,13},{6,14},{7,15},{8,0},{9,1},... | collective-permute-start | bytes 1179656 | tf_op jit(solution)/shard_map/cond/branch_1_fun/ppermute | solution.py:26
  100.1 9.2 %collective-permute-start.15 = (bf16[192,2048]{1,0:T(8,128)(2,1)S(1)}, bf16[192,2048]{1,0:T(8,128)(2,1)S(1)}, u32[]{:S(2)}, u32[]{:S(2)}) collective-permute-start(bf16[192,2048]{1,0:T(8,128)(2,1)S(1)} %bitcast.5), channel_id=1, source_target_pairs={{0,8},{1,9},{2,10},{3,11},{4,12},{5,13},{6,14},{7,15},{8,0},{9,1},... | collective-permute-start | bytes 2359304 | tf_op jit(solution)/shard_map/ppermute | solution.py:26
  109.3 0.9 copy-start
  118.2 4.4 %collective-permute-start.16 = (f32[33,24,192]{2,1,0:T(8,128)}, f32[33,24,192]{2,1,0:T(8,128)S(1)}, u32[]{:S(2)}, u32[]{:S(2)}) collective-permute-start(f32[33,24,192]{2,1,0:T(8,128)} %get-tuple-element.81), channel_id=1, source_target_pairs={{0,8},{1,9},{2,10},{3,11},{4,12},{5,13},{6,14},{7,15},{8,0},{9,1},... | collective-permute-start | bytes 1824776 | tf_op jit(solution)/shard_map/ppermute | solution.py:26
Sparse Core Ops, SparseCore 0:
  34.5 55.7 all-gather.2

commit v6 on v3

--- a/solution.py
+++ b/solution.py
@@ -10,8 +10,9 @@
 LANES = 2048
 UNITS = (
     (0, True), (4, True), (8, True), (12, False), (16, True),
-    (1, True), (5, True), (9, True), (13, False),
-    (15, False), (11, False), (7, False), (3, True),
+    (1, True), (5, True),
+    (9, True), (7, True), (3, True), (13, False),
+    (15, False), (11, False),
     (2, True), (6, True), (14, False), (10, False),
 )
 
@@ -34,28 +35,35 @@
     return permuted(value, lambda w, n: (w ^ 1, n))
 
 
-def gather_wide(unit, sixteen_mine, core, piece):
+def gather_wide(unit, core, piece):
     four = by_chips(unit, -4, -12)
+    sixteen_mine = by_chips(unit[:piece], -16, -16)
     sixteen = jnp.concatenate([sixteen_mine, from_partner(sixteen_mine)], axis=0)
     start = jnp.where(core == 0, unit, sixteen)
     stop = jnp.where(core == 0, sixteen, unit)
+    near = by_chips(jnp.concatenate([start, four], axis=0), -1, 1)
     eight = by_chips(four[:piece], -4, 4)
-    near = by_chips(jnp.concatenate([start, four], axis=0), -1, 1)
-    got = from_partner(jnp.concatenate([four, eight], axis=0))
+    near, eight = lax.optimization_barrier((near, eight))
     two = by_chips(near, -1, 1)
+    held = jnp.concatenate([four, eight], axis=0)
+    back = by_chips(held, 1, -1)
+    late = by_chips(eight, -1, 1)
+    got = from_partner(held)
+    far = from_partner(near)
+    got_late = from_partner(jnp.concatenate([late, back], axis=0))
+    two_far = from_partner(two)
     eights = jnp.concatenate([eight, got[2 * piece :]], axis=0)
     twelve = got[: 2 * piece]
-    near_late = by_chips(jnp.concatenate([eights, twelve], axis=0), -1, 1)
-    far = from_partner(near)
-    two_far = from_partner(two)
-    far_late = from_partner(near_late)
-    return start, four, eights, twelve, stop, near, near_late, far, far_late, two, two_far
-
-
-def products_kernel(piece, shards_x, rows_d, tile, width, env_count, *refs):
-    gathered, points = refs[0], refs[1:12]
-    own_ref, send_ref = refs[12:14]
-    envs, rows, dots, columns, own, send, sems = refs[14:]
+    nines = jnp.concatenate([late, got_late[3 * piece :]], axis=0)
+    sevens = jnp.concatenate([back[2 * piece :], got_late[:piece]], axis=0)
+    threes, thirteens = back[: 2 * piece], got_late[piece : 3 * piece]
+    return start, four, eights, twelve, stop, near, nines, sevens, threes, thirteens, far, two, two_far
+
+
+def products_kernel(piece, shards_x, rows_d, tile, width, env_count, core_ref, *refs):
+    gathered, points = refs[0], refs[1:14]
+    own_ref, send_ref = refs[14:16]
+    envs, rows, dots, columns, own, send, sems = refs[16:]
     count = len(UNITS) * 2 * piece
     block = 2 * shards_x * piece
     at = count + 4 * shards_x * piece
@@ -73,7 +81,7 @@
     first = -(-tile // rows_d)
     env_copies = [copied_envs(i) for i in range(first)]
     place = 0
-    for group in ((0, 1, 2, 3, 4), (5, 6), (7, 8), (9, 10)):
+    for group in ((0, 1, 2, 3, 4), (5,), (6, 7, 8, 9), (10, 11, 12)):
         row_copies.append([])
         begin = place
         for k in group:
@@ -153,20 +161,20 @@
 
         lax.fori_loop(0, 3, some_products, 0)
 
+    core = core_ref[0]
     for u, (distance, first_own) in enumerate(UNITS):
         for b in range(2):
             part = pl.ds((2 * u + b) * piece, piece)
-            if first_own == (b == 0):
-                own_ref[2 * distance] = own[part, :]
-                if distance > 0:
-                    send_ref[33 - 2 * distance] = send[part, :]
-            else:
-                if distance < 16:
-                    own_ref[2 * distance + 1] = own[part, :]
-                send_ref[32 - 2 * distance] = send[part, :]
-
-
-def products(gathered, points, piece, rows_d, width, env_count):
+            mine = first_own == (b == 0)
+            ahead = 2 * distance + (0 if mine else 1)
+            behind = (33 if mine else 32) - 2 * distance
+            if ahead < 33:
+                own_ref[ahead + core * (32 - 2 * ahead)] = own[part, :]
+            if behind < 33:
+                send_ref[behind + (1 - core) * (32 - 2 * behind)] = send[part, :]
+
+
+def products(core, gathered, points, piece, rows_d, width, env_count):
     shards_x = gathered.shape[0]
     env_rows = shards_x * rows_d
     tile = 256 if env_rows % 256 == 0 else env_rows
@@ -180,7 +188,7 @@
     return pl.pallas_call(
         functools.partial(products_kernel, piece, shards_x, rows_d, tile, width, env_count),
         out_shape=(shape, shape),
-        in_specs=[anywhere] * (1 + len(points)),
+        in_specs=[pl.BlockSpec(memory_space=pltpu.SMEM)] + [anywhere] * (1 + len(points)),
         out_specs=(vmem, vmem),
         scratch_shapes=[
             pltpu.VMEM((env_rows, LANES), jnp.bfloat16),
@@ -191,9 +199,9 @@
             pltpu.VMEM((count, block), jnp.float32),
             pltpu.SemaphoreType.DMA((len(points) + 2 * shards_x,)),
         ],
-        compiler_params=pltpu.CompilerParams(vmem_limit_bytes=60 * 1024 * 1024),
+        compiler_params=pltpu.CompilerParams(vmem_limit_bytes=40 * 1024 * 1024),
         cost_estimate=pl.CostEstimate(flops=flops, bytes_accessed=10**7, transcendentals=0),
-    )(gathered, *points)
+    )(core, gathered, *points)
 
 
 def shards(descriptors, env_weights, sparse_points):
@@ -222,7 +230,6 @@
         half_envs, lambda w, n: (w + (wide // 2 if w % 2 else 0), n + shards_x)
     )
     across_other = from_partner(across_mine)
-    sixteen_mine = by_chips(mine, -16, -16)
     at_zero = lax.axis_index("narrow") < shards_x
     payload = jnp.concatenate(
         [
@@ -235,24 +242,22 @@
         ],
         axis=0,
     )
-    payload, unit, sixteen_mine = lax.optimization_barrier((payload, unit, sixteen_mine))
+    payload, unit = lax.optimization_barrier((payload, unit))
     groups = [list(range(shards_x)), list(range(shards_x, narrow))]
     gathered = lax.all_gather(payload, "narrow", axis=0, tiled=False, axis_index_groups=groups)
 
     def none(*_):
-        return tuple(jnp.zeros((n * piece, LANES), unit.dtype) for n in (2, 2, 2, 2, 2, 4, 4, 4, 4, 4, 4))
+        return tuple(jnp.zeros((n * piece, LANES), unit.dtype) for n in (2, 2, 2, 2, 2, 4, 2, 2, 2, 2, 4, 4, 4))
 
     points = lax.cond(
         1 + jnp.minimum(lax.axis_index("wide"), 0) > 0,
         lambda *values: gather_wide(*values, core, piece),
         none,
         unit,
-        sixteen_mine,
     )
     gathered, points = lax.optimization_barrier((gathered, points))
-    kept, sent = products(gathered, points, piece, 2 * half, width, env_count)
-    total = kept + from_partner(sent)
-    return jnp.where(core == 0, total, total[::-1])[None]
+    kept, sent = products(core.reshape(1), gathered, points, piece, 2 * half, width, env_count)
+    return (kept + from_partner(sent))[None]
 
 
 def solution(mesh):

time: 125 us -> 129 us (1.032)
  other arithmetic: 4.98 us -> 1.25 us
  waiting for transfers between devices: 14.9 us -> 18.4 us
  local copies, waits for them, and re-layouts: 2.89 us -> 5.66 us
    ppermute x16 -> x17, waiting for transfers between devices: 14.9 us -> 18.4 us  [permuted(): return lax.ppermute(value, ('wide', 'narrow'), pairs)]
    unnamed x6 -> x8, local copies, waits for them, and re-layouts: 0.12 us -> 3.48 us
    ppermute x16 -> x17, starting transfers between devices: 73.1 us -> 73.7 us  [permuted(): return lax.ppermute(value, ('wide', 'narrow'), pairs)]
  transfers between devices with their start and end apart: 17 -> 18, of which waited for: 7 -> 6; matrix products, arithmetic and copies ran while one was open for 3% -> 0% of each run, Pallas kernels for 0% -> 0%
where the time goes in v6:
time: 129 us; the launch traced here: 128 us
  starting transfers between devices  73.7 us (57%)
  waiting for transfers between devices  18.4 us (14%)
  Pallas kernels  15.2 us (12%)
  between operations  13.6 us (11%)
  local copies, waits for them, and re-layouts  5.66 us (4%)
    ppermute x17, starting transfers between devices, permuted(): return lax.ppermute(value, ('wide', 'narrow'), pairs)  73.7 us
    ppermute x17, waiting for transfers between devices, permuted(): return lax.ppermute(value, ('wide', 'narrow'), pairs)  18.4 us
    pallas_call x1, Pallas kernels, products(): pl.pallas_call(functools.partial(products_kernel, piece, shards_x, rows_d...  15.2 us
    unnamed x8, local copies, waits for them, and re-layouts  3.48 us
  transfers between devices with their start and end apart: 18, of which 6 were waited for; matrix products, arithmetic and copies ran while one was open for 0% of the time, Pallas kernels for 0%

profile of v6, /device:TPU:1, one launch (start us, length us, event | category | flops | bytes accessed | tf_op | source)
XLA Modules:
  0.0 128.1 jit_solution(7747249848741853745)
XLA Ops:
  6.5 0.0 all-gather.3.cloned.1.call-start
  6.5 0.7 broadcast_in_dim.12
  7.3 0.0 copy-start.4
  7.3 1.3 concatenate.30
  8.6 0.1 constant_dynamic-update-slice_fusion.5
  8.7 5.5 %collective-permute-start.12 = (bf16[96,2048]{1,0:T(8,128)(2,1)S(1)}, bf16[96,2048]{1,0:T(8,128)(2,1)S(1)}, u32[]{:S(2)}, u32[]{:S(2)}) collective-permute-start(bf16[96,2048]{1,0:T(8,128)(2,1)S(1)} %get-tuple-element.76), channel_id=1, source_target_pairs={{0,4},{1,5},{2,6},{3,7},{4,0},{5,1},{6,2},{7,3},{8,268},{9,269},{1... | collective-permute-start | bytes 1179656 | tf_op jit(solution)/shard_map/ppermute | solution.py:27
  14.2 1.9 %collective-permute-start.13 = (bf16[24,2048]{1,0:T(8,128)(2,1)S(1)}, bf16[24,2048]{1,0:T(8,128)(2,1)S(1)}, u32[]{:S(2)}, u32[]{:S(2)}) collective-permute-start(bf16[24,2048]{1,0:T(8,128)(2,1)S(1)} %pad.4), channel_id=1, source_target_pairs={{0,4},{1,5},{2,6},{3,7},{4,0},{5,1},{6,2},{7,3},{8,12},{9,13},{10,... | collective-permute-start | bytes 294920 | tf_op jit(solution)/shard_map/ppermute | solution.py:27
  16.1 7.2 %collective-permute-start.14 = (bf16[24,2048]{1,0:T(8,128)(2,1)S(1)}, bf16[24,2048]{1,0:T(8,128)(2,1)S(1)}, u32[]{:S(2)}, u32[]{:S(2)}) collective-permute-start(bf16[24,2048]{1,0:T(8,128)(2,1)S(1)} %pad.4), channel_id=1, source_target_pairs={{0,8},{1,9},{2,10},{3,11},{4,12},{5,13},{6,14},{7,15},{8,0},{9,1},... | collective-permute-start | bytes 294920 | tf_op jit(solution)/shard_map/ppermute | solution.py:27
  23.4 0.0 collective-permute-done.13
  23.4 4.8 %collective-permute-start.15 = (bf16[24,2048]{1,0:T(8,128)(2,1)S(1)}, bf16[24,2048]{1,0:T(8,128)(2,1)S(1)}, u32[]{:S(2)}, u32[]{:S(2)}) collective-permute-start(bf16[24,2048]{1,0:T(8,128)(2,1)S(1)} %collective-permute-done.13), channel_id=1, source_target_pairs={{0,8},{1,9},{2,10},{3,11},{4,12},{5,13},{6,14},{7,15},{8,0},{9,1},... | collective-permute-start | bytes 294920 | tf_op jit(solution)/shard_map/ppermute | solution.py:27
  28.2 0.0 collective-permute-done.14
  28.2 0.0 collective-permute-done.12
  28.3 0.8 collective-permute-done.15
  29.2 0.0 copy-start.3
  29.2 1.0 copy-done.3
  30.2 0.0 all-gather.3.cloned.1.call-update
  30.2 68.3 %conditional.1 = (bf16[48,2048]{1,0:T(8,128)(2,1)S(1)}, bf16[48,2048]{1,0:T(8,128)(2,1)S(1)}, bf16[48,2048]{1,0:T(8,128)(2,1)S(1)}, bf16[48,2048]{1,0:T(8,128)(2...) conditional(s32[]{:T(128)} %convert_element_type.5, () %tuple.17, ...), branch_computations={%region_0.1_spmd, %region_1.2_spmd} | conditional | flops 2949121 | bytes 22610626 | solution.py:252
  30.3 1.9 %collective-permute-start = (bf16[24,2048]{1,0:T(8,128)(2,1)S(1)}, bf16[24,2048]{1,0:T(8,128)(2,1)S(1)}, u32[]{:S(2)}, u32[]{:S(2)}) collective-permute-start(bf16[24,2048]{1,0:T(8,128)(2,1)S(1)} %slice.18), channel_id=1, source_target_pairs={{0,256},{1,257},{2,258},{3,259},{4,260},{5,261},{6,262},{7,263},{8... | collective-permute-start | bytes 294920 | tf_op jit(solution)/shard_map/cond/branch_1_fun/ppermute | solution.py:27
  32.2 7.2 %collective-permute-start.2 = (bf16[48,2048]{1,0:T(8,128)(2,1)S(1)}, bf16[48,2048]{1,0:T(8,128)(2,1)S(1)}, u32[]{:S(2)}, u32[]{:S(2)}) collective-permute-start(bf16[48,2048]{1,0:T(8,128)(2,1)S(1)} %get-tuple-element.10), channel_id=1, source_target_pairs={{0,448},{1,449},{2,450},{3,451},{4,452},{5,453},{6,454},{7,455},{8... | collective-permute-start | bytes 589832 | tf_op jit(solution)/shard_map/cond/branch_1_fun/ppermute | solution.py:27
  39.4 0.0 collective-permute-done
  39.4 6.5 %collective-permute-start.1 = (bf16[24,2048]{1,0:T(8,128)(2,1)S(1)}, bf16[24,2048]{1,0:T(8,128)(2,1)S(1)}, u32[]{:S(2)}, u32[]{:S(2)}) collective-permute-start(bf16[24,2048]{1,0:T(8,128)(2,1)S(1)} %collective-permute-done), channel_id=1, source_target_pairs={{0,8},{1,9},{2,10},{3,11},{4,12},{5,13},{6,14},{7,15},{8,0},{9,1},... | collective-permute-start | bytes 294920 | tf_op jit(solution)/shard_map/cond/branch_1_fun/ppermute | solution.py:27
  45.9 0.9 collective-permute-done.1
  46.8 0.0 copy-start.5
  46.8 0.0 collective-permute-done.2
  46.9 5.5 %collective-permute-start.3 = (bf16[96,2048]{1,0:T(8,128)(2,1)S(1)}, bf16[96,2048]{1,0:T(8,128)(2,1)}, u32[]{:S(2)}, u32[]{:S(2)}) collective-permute-start(bf16[96,2048]{1,0:T(8,128)(2,1)S(1)} %pad_maximum_fusion), channel_id=1, source_target_pairs={{0,496},{1,497},{2,498},{3,499},{4,500},{5,501},{6,502},{7,503},{8... | collective-permute-start | bytes 1179656 | tf_op jit(solution)/shard_map/cond/branch_1_fun/ppermute | solution.py:27
  52.4 6.5 %collective-permute-start.4 = (bf16[24,2048]{1,0:T(8,128)(2,1)S(1)}, bf16[24,2048]{1,0:T(8,128)(2,1)S(1)}, u32[]{:S(2)}, u32[]{:S(2)}) collective-permute-start(bf16[24,2048]{1,0:T(8,128)(2,1)S(1)} %slice.27), channel_id=1, source_target_pairs={{0,448},{1,449},{2,450},{3,451},{4,452},{5,453},{6,454},{7,455},{8... | collective-permute-start | bytes 294920 | tf_op jit(solution)/shard_map/cond/branch_1_fun/ppermute | solution.py:27
  58.9 8.5 %collective-permute-done.4 = bf16[24,2048]{1,0:T(8,128)(2,1)S(1)} collective-permute-done((bf16[24,2048]{1,0:T(8,128)(2,1)S(1)}, bf16[24,2048]{1,0:T(8,128)(2,1)S(1)}, u32[]{:S(2)}, u32[]{:S(2)}) %collective-permute-start.4) | collective-permute-done | bytes 98336 | tf_op jit(solution)/shard_map/cond/branch_1_fun/ppermute | solution.py:27
  67.4 0.0 collective-permute-done.3
  67.4 7.3 %collective-permute-start.7 = (bf16[72,2048]{1,0:T(8,128)(2,1)S(1)}, bf16[72,2048]{1,0:T(8,128)(2,1)S(1)}, u32[]{:S(2)}, u32[]{:S(2)}) collective-permute-start(bf16[72,2048]{1,0:T(8,128)(2,1)S(1)} %constant_dynamic-update-slice_fusion.2), channel_id=1, source_target_pairs={{0,16},{1,17},{2,18},{3,19},{4,20},{5,21},{6,22},{7,23},{8,504},{9... | collective-permute-start | bytes 884744 | tf_op jit(solution)/shard_map/cond/branch_1_fun/ppermute | solution.py:27
  74.8 1.9 %collective-permute-start.6 = (bf16[24,2048]{1,0:T(8,128)(2,1)S(1)}, bf16[24,2048]{1,0:T(8,128)(2,1)S(1)}, u32[]{:S(2)}, u32[]{:S(2)}) collective-permute-start(bf16[24,2048]{1,0:T(8,128)(2,1)S(1)} %collective-permute-done.4), channel_id=1, source_target_pairs={{0,496},{1,497},{2,498},{3,499},{4,500},{5,501},{6,502},{7,503},{8... | collective-permute-start | bytes 294920 | tf_op jit(solution)/shard_map/cond/branch_1_fun/ppermute | solution.py:27
  76.7 5.4 %collective-permute-start.5 = (bf16[72,2048]{1,0:T(8,128)(2,1)S(1)}, bf16[72,2048]{1,0:T(8,128)(2,1)S(1)}, u32[]{:S(2)}, u32[]{:S(2)}) collective-permute-start(bf16[72,2048]{1,0:T(8,128)(2,1)S(1)} %constant_dynamic-update-slice_fusion.2), channel_id=1, source_target_pairs={{0,8},{1,9},{2,10},{3,11},{4,12},{5,13},{6,14},{7,15},{8,0},{9,1},... | collective-permute-start | bytes 884744 | tf_op jit(solution)/shard_map/cond/branch_1_fun/ppermute | solution.py:27
  82.1 1.9 %collective-permute-start.10 = (bf16[96,2048]{1,0:T(8,128)(2,1)}, bf16[96,2048]{1,0:T(8,128)(2,1)}, u32[]{:S(2)}, u32[]{:S(2)}) collective-permute-start(bf16[96,2048]{1,0:T(8,128)(2,1)} %collective-permute-done.3), channel_id=1, source_target_pairs={{0,496},{1,497},{2,498},{3,499},{4,500},{5,501},{6,502},{7,503},{8... | collective-permute-start | bytes 1179656 | tf_op jit(solution)/shard_map/cond/branch_1_fun/ppermute | solution.py:27
  84.0 0.0 collective-permute-done.6
  84.0 0.0 collective-permute-done.7
  84.1 4.3 %collective-permute-start.8 = (bf16[96,2048]{1,0:T(8,128)(2,1)S(1)}, bf16[96,2048]{1,0:T(8,128)(2,1)S(1)}, u32[]{:S(2)}, u32[]{:S(2)}) collective-permute-start(bf16[96,2048]{1,0:T(8,128)(2,1)S(1)} %pad_maximum_fusion.1), channel_id=1, source_target_pairs={{0,8},{1,9},{2,10},{3,11},{4,12},{5,13},{6,14},{7,15},{8,0},{9,1},... | collective-permute-start | bytes 1179656 | tf_op jit(solution)/shard_map/cond/branch_1_fun/ppermute | solution.py:27
  88.4 1.9 %collective-permute-start.9 = (bf16[96,2048]{1,0:T(8,128)(2,1)}, bf16[96,2048]{1,0:T(8,128)(2,1)}, u32[]{:S(2)}, u32[]{:S(2)}) collective-permute-start(bf16[96,2048]{1,0:T(8,128)(2,1)} %collective-permute-done.3), channel_id=1, source_target_pairs={{0,8},{1,9},{2,10},{3,11},{4,12},{5,13},{6,14},{7,15},{8,0},{9,1},... | collective-permute-start | bytes 1179656 | tf_op jit(solution)/shard_map/cond/branch_1_fun/ppermute | solution.py:27
  90.4 0.0 collective-permute-done.5
  90.4 0.0 copy-start.6
  90.5 4.0 %collective-permute-done.10 = bf16[96,2048]{1,0:T(8,128)(2,1)} collective-permute-done((bf16[96,2048]{1,0:T(8,128)(2,1)}, bf16[96,2048]{1,0:T(8,128)(2,1)}, u32[]{:S(2)}, u32[]{:S(2)}) %collective-permute-start.10) | collective-permute-done | bytes 393248 | tf_op jit(solution)/shard_map/cond/branch_1_fun/ppermute | solution.py:27
  94.6 1.9 %collective-permute-start.11 = (bf16[96,2048]{1,0:T(8,128)(2,1)}, bf16[96,2048]{1,0:T(8,128)(2,1)}, u32[]{:S(2)}, u32[]{:S(2)}) collective-permute-start(bf16[96,2048]{1,0:T(8,128)(2,1)} %collective-permute-done.10), channel_id=1, source_target_pairs={{0,8},{1,9},{2,10},{3,11},{4,12},{5,13},{6,14},{7,15},{8,0},{9,1},... | collective-permute-start | bytes 1179656 | tf_op jit(solution)/shard_map/cond/branch_1_fun/ppermute | solution.py:27
  96.5 0.0 collective-permute-done.8
  96.6 0.0 collective-permute-done.9
  96.6 1.9 %collective-permute-done.11 = bf16[96,2048]{1,0:T(8,128)(2,1)} collective-permute-done((bf16[96,2048]{1,0:T(8,128)(2,1)}, bf16[96,2048]{1,0:T(8,128)(2,1)}, u32[]{:S(2)}, u32[]{:S(2)}) %collective-permute-start.11) | collective-permute-done | bytes 393248 | tf_op jit(solution)/shard_map/cond/branch_1_fun/ppermute | solution.py:27
  98.5 2.3 %copy-done = bf16[1152,2048]{1,0:T(8,128)(2,1)S(1)} copy-done((bf16[1152,2048]{1,0:T(8,128)(2,1)S(1)}, bf16[1152,2048]{1,0:T(8,128)(2,1)}, u32[]{:S(2)}) %copy-start) | copy-done | bytes 4718616
  100.9 15.2 %shard_map.37 = (f32[33,24,192]{2,1,0:T(8,128)S(1)}, f32[33,24,192]{2,1,0:T(8,128)S(1)}) custom-call(s32[1]{0:T(128)} %bitcast.core_ref, bf16[4,288,2048]{2,1,0:T(8,128)(2,1)S(1)} %bitcast.4, bf16[48,2048]{1,0:T(8,128)(2,1)S(1)} %get-tuple-element.60.refs_1_, bf16[48,2048]{1,0:T(8,128)(2,1)S(1)} %get-tuple-element.61.refs_2_, ...), custom_call_target="tpu_custom_call" | custom-call | flops 5269094400 | bytes 10000000 | tf_op jit(solution)/shard_map/pallas_call | solution.py:188
  116.1 2.0 %collective-permute-start.16 = (f32[33,24,192]{2,1,0:T(8,128)S(1)}, f32[33,24,192]{2,1,0:T(8,128)S(1)}, u32[]{:S(2)}, u32[]{:S(2)}) collective-permute-start(f32[33,24,192]{2,1,0:T(8,128)S(1)} %get-tuple-element.74), channel_id=1, source_target_pairs={{0,8},{1,9},{2,10},{3,11},{4,12},{5,13},{6,14},{7,15},{8,0},{9,1},... | collective-permute-start | bytes 1824776 | tf_op jit(solution)/shard_map/ppermute | solution.py:27
  118.1 2.2 %collective-permute-done.16 = f32[33,24,192]{2,1,0:T(8,128)S(1)} collective-permute-done((f32[33,24,192]{2,1,0:T(8,128)S(1)}, f32[33,24,192]{2,1,0:T(8,128)S(1)}, u32[]{:S(2)}, u32[]{:S(2)}) %collective-permute-start.16) | collective-permute-done | bytes 608288 | tf_op jit(solution)/shard_map/ppermute | solution.py:27
  120.3 1.0 add_bitcast_fusion
  (34 shorter events, 0.5 us)
Async XLA Ops:
  6.5 92.0 %all-gather.3.cloned.1.call-start = ((), (), s32[]{:S(2)}) async-start(), calls=%async_computation | async-start | bytes 5898240 | tf_op jit(solution)/shard_map/all_gather | solution.py:247
  7.3 6.9 %copy-start.4 = (bf16[24,2000]{1,0:T(8,128)(2,1)S(1)}, bf16[24,2000]{1,0:T(8,128)(2,1)}, u32[]{:S(2)}) copy-start(bf16[24,2000]{1,0:T(8,128)(2,1)} %param.7) | copy-start | bytes 288004
  8.7 19.5 %collective-permute-start.12 = (bf16[96,2048]{1,0:T(8,128)(2,1)S(1)}, bf16[96,2048]{1,0:T(8,128)(2,1)S(1)}, u32[]{:S(2)}, u32[]{:S(2)}) collective-permute-start(bf16[96,2048]{1,0:T(8,128)(2,1)S(1)} %get-tuple-element.76), channel_id=1, source_target_pairs={{0,4},{1,5},{2,6},{3,7},{4,0},{5,1},{6,2},{7,3},{8,268},{9,269},{1... | collective-permute-start | bytes 1179656 | tf_op jit(solution)/shard_map/ppermute | solution.py:27
  14.2 9.2 %collective-permute-start.13 = (bf16[24,2048]{1,0:T(8,128)(2,1)S(1)}, bf16[24,2048]{1,0:T(8,128)(2,1)S(1)}, u32[]{:S(2)}, u32[]{:S(2)}) collective-permute-start(bf16[24,2048]{1,0:T(8,128)(2,1)S(1)} %pad.4), channel_id=1, source_target_pairs={{0,4},{1,5},{2,6},{3,7},{4,0},{5,1},{6,2},{7,3},{8,12},{9,13},{10,... | collective-permute-start | bytes 294920 | tf_op jit(solution)/shard_map/ppermute | solution.py:27
  16.1 12.1 %collective-permute-start.14 = (bf16[24,2048]{1,0:T(8,128)(2,1)S(1)}, bf16[24,2048]{1,0:T(8,128)(2,1)S(1)}, u32[]{:S(2)}, u32[]{:S(2)}) collective-permute-start(bf16[24,2048]{1,0:T(8,128)(2,1)S(1)} %pad.4), channel_id=1, source_target_pairs={{0,8},{1,9},{2,10},{3,11},{4,12},{5,13},{6,14},{7,15},{8,0},{9,1},... | collective-permute-start | bytes 294920 | tf_op jit(solution)/shard_map/ppermute | solution.py:27
  23.4 5.7 %collective-permute-start.15 = (bf16[24,2048]{1,0:T(8,128)(2,1)S(1)}, bf16[24,2048]{1,0:T(8,128)(2,1)S(1)}, u32[]{:S(2)}, u32[]{:S(2)}) collective-permute-start(bf16[24,2048]{1,0:T(8,128)(2,1)S(1)} %collective-permute-done.13), channel_id=1, source_target_pairs={{0,8},{1,9},{2,10},{3,11},{4,12},{5,13},{6,14},{7,15},{8,0},{9,1},... | collective-permute-start | bytes 294920 | tf_op jit(solution)/shard_map/ppermute | solution.py:27
  29.2 1.0 copy-start.3
  30.3 9.1 %collective-permute-start = (bf16[24,2048]{1,0:T(8,128)(2,1)S(1)}, bf16[24,2048]{1,0:T(8,128)(2,1)S(1)}, u32[]{:S(2)}, u32[]{:S(2)}) collective-permute-start(bf16[24,2048]{1,0:T(8,128)(2,1)S(1)} %slice.18), channel_id=1, source_target_pairs={{0,256},{1,257},{2,258},{3,259},{4,260},{5,261},{6,262},{7,263},{8... | collective-permute-start | bytes 294920 | tf_op jit(solution)/shard_map/cond/branch_1_fun/ppermute | solution.py:27
  32.2 14.6 %collective-permute-start.2 = (bf16[48,2048]{1,0:T(8,128)(2,1)S(1)}, bf16[48,2048]{1,0:T(8,128)(2,1)S(1)}, u32[]{:S(2)}, u32[]{:S(2)}) collective-permute-start(bf16[48,2048]{1,0:T(8,128)(2,1)S(1)} %get-tuple-element.10), channel_id=1, source_target_pairs={{0,448},{1,449},{2,450},{3,451},{4,452},{5,453},{6,454},{7,455},{8... | collective-permute-start | bytes 589832 | tf_op jit(solution)/shard_map/cond/branch_1_fun/ppermute | solution.py:27
  39.4 7.4 %collective-permute-start.1 = (bf16[24,2048]{1,0:T(8,128)(2,1)S(1)}, bf16[24,2048]{1,0:T(8,128)(2,1)S(1)}, u32[]{:S(2)}, u32[]{:S(2)}) collective-permute-start(bf16[24,2048]{1,0:T(8,128)(2,1)S(1)} %collective-permute-done), channel_id=1, source_target_pairs={{0,8},{1,9},{2,10},{3,11},{4,12},{5,13},{6,14},{7,15},{8,0},{9,1},... | collective-permute-start | bytes 294920 | tf_op jit(solution)/shard_map/cond/branch_1_fun/ppermute | solution.py:27
  46.8 37.3 %copy-start.5 = (bf16[48,2048]{1,0:T(8,128)(2,1)}, bf16[48,2048]{1,0:T(8,128)(2,1)S(1)}, u32[]{:S(2)}) copy-start(bf16[48,2048]{1,0:T(8,128)(2,1)S(1)} %get-tuple-element.96) | copy-start | bytes 589828 | tf_op jit(solution)/shard_map/cond
  46.9 37.2 %copy-start.1 = (bf16[48,2048]{1,0:T(8,128)(2,1)}, bf16[48,2048]{1,0:T(8,128)(2,1)S(1)}, u32[]{:S(2)}) copy-start(bf16[48,2048]{1,0:T(8,128)(2,1)S(1)} %collective-permute-done.2) | copy-start | bytes 589828 | tf_op jit(solution)/shard_map/cond
  46.9 20.5 %collective-permute-start.3 = (bf16[96,2048]{1,0:T(8,128)(2,1)S(1)}, bf16[96,2048]{1,0:T(8,128)(2,1)}, u32[]{:S(2)}, u32[]{:S(2)}) collective-permute-start(bf16[96,2048]{1,0:T(8,128)(2,1)S(1)} %pad_maximum_fusion), channel_id=1, source_target_pairs={{0,496},{1,497},{2,498},{3,499},{4,500},{5,501},{6,502},{7,503},{8... | collective-permute-start | bytes 1179656 | tf_op jit(solution)/shard_map/cond/branch_1_fun/ppermute | solution.py:27
  52.4 15.0 %collective-permute-start.4 = (bf16[24,2048]{1,0:T(8,128)(2,1)S(1)}, bf16[24,2048]{1,0:T(8,128)(2,1)S(1)}, u32[]{:S(2)}, u32[]{:S(2)}) collective-permute-start(bf16[24,2048]{1,0:T(8,128)(2,1)S(1)} %slice.27), channel_id=1, source_target_pairs={{0,448},{1,449},{2,450},{3,451},{4,452},{5,453},{6,454},{7,455},{8... | collective-permute-start | bytes 294920 | tf_op jit(solution)/shard_map/cond/branch_1_fun/ppermute | solution.py:27
  67.4 16.6 %collective-permute-start.7 = (bf16[72,2048]{1,0:T(8,128)(2,1)S(1)}, bf16[72,2048]{1,0:T(8,128)(2,1)S(1)}, u32[]{:S(2)}, u32[]{:S(2)}) collective-permute-start(bf16[72,2048]{1,0:T(8,128)(2,1)S(1)} %constant_dynamic-update-slice_fusion.2), channel_id=1, source_target_pairs={{0,16},{1,17},{2,18},{3,19},{4,20},{5,21},{6,22},{7,23},{8,504},{9... | collective-permute-start | bytes 884744 | tf_op jit(solution)/shard_map/cond/branch_1_fun/ppermute | solution.py:27
  74.8 9.3 %collective-permute-start.6 = (bf16[24,2048]{1,0:T(8,128)(2,1)S(1)}, bf16[24,2048]{1,0:T(8,128)(2,1)S(1)}, u32[]{:S(2)}, u32[]{:S(2)}) collective-permute-start(bf16[24,2048]{1,0:T(8,128)(2,1)S(1)} %collective-permute-done.4), channel_id=1, source_target_pairs={{0,496},{1,497},{2,498},{3,499},{4,500},{5,501},{6,502},{7,503},{8... | collective-permute-start | bytes 294920 | tf_op jit(solution)/shard_map/cond/branch_1_fun/ppermute | solution.py:27
  76.7 13.7 %collective-permute-start.5 = (bf16[72,2048]{1,0:T(8,128)(2,1)S(1)}, bf16[72,2048]{1,0:T(8,128)(2,1)S(1)}, u32[]{:S(2)}, u32[]{:S(2)}) collective-permute-start(bf16[72,2048]{1,0:T(8,128)(2,1)S(1)} %constant_dynamic-update-slice_fusion.2), channel_id=1, source_target_pairs={{0,8},{1,9},{2,10},{3,11},{4,12},{5,13},{6,14},{7,15},{8,0},{9,1},... | collective-permute-start | bytes 884744 | tf_op jit(solution)/shard_map/cond/branch_1_fun/ppermute | solution.py:27
  82.1 12.5 %collective-permute-start.10 = (bf16[96,2048]{1,0:T(8,128)(2,1)}, bf16[96,2048]{1,0:T(8,128)(2,1)}, u32[]{:S(2)}, u32[]{:S(2)}) collective-permute-start(bf16[96,2048]{1,0:T(8,128)(2,1)} %collective-permute-done.3), channel_id=1, source_target_pairs={{0,496},{1,497},{2,498},{3,499},{4,500},{5,501},{6,502},{7,503},{8... | collective-permute-start | bytes 1179656 | tf_op jit(solution)/shard_map/cond/branch_1_fun/ppermute | solution.py:27
  84.1 12.4 %collective-permute-start.8 = (bf16[96,2048]{1,0:T(8,128)(2,1)S(1)}, bf16[96,2048]{1,0:T(8,128)(2,1)S(1)}, u32[]{:S(2)}, u32[]{:S(2)}) collective-permute-start(bf16[96,2048]{1,0:T(8,128)(2,1)S(1)} %pad_maximum_fusion.1), channel_id=1, source_target_pairs={{0,8},{1,9},{2,10},{3,11},{4,12},{5,13},{6,14},{7,15},{8,0},{9,1},... | collective-permute-start | bytes 1179656 | tf_op jit(solution)/shard_map/cond/branch_1_fun/ppermute | solution.py:27
  88.4 8.1 %collective-permute-start.9 = (bf16[96,2048]{1,0:T(8,128)(2,1)}, bf16[96,2048]{1,0:T(8,128)(2,1)}, u32[]{:S(2)}, u32[]{:S(2)}) collective-permute-start(bf16[96,2048]{1,0:T(8,128)(2,1)} %collective-permute-done.3), channel_id=1, source_target_pairs={{0,8},{1,9},{2,10},{3,11},{4,12},{5,13},{6,14},{7,15},{8,0},{9,1},... | collective-permute-start | bytes 1179656 | tf_op jit(solution)/shard_map/cond/branch_1_fun/ppermute | solution.py:27
  90.4 8.1 %copy-start.2 = (bf16[48,2048]{1,0:T(8,128)(2,1)S(1)}, bf16[48,2048]{1,0:T(8,128)(2,1)}, u32[]{:S(2)}) copy-start(bf16[48,2048]{1,0:T(8,128)(2,1)} %copy-done.1) | copy-start | bytes 589828 | tf_op jit(solution)/shard_map/cond
  90.4 8.1 %copy-start.6 = (bf16[48,2048]{1,0:T(8,128)(2,1)S(1)}, bf16[48,2048]{1,0:T(8,128)(2,1)}, u32[]{:S(2)}) copy-start(bf16[48,2048]{1,0:T(8,128)(2,1)} %copy-done.5) | copy-start | bytes 589828 | tf_op jit(solution)/shard_map/cond
  94.6 3.9 %collective-permute-start.11 = (bf16[96,2048]{1,0:T(8,128)(2,1)}, bf16[96,2048]{1,0:T(8,128)(2,1)}, u32[]{:S(2)}, u32[]{:S(2)}) collective-permute-start(bf16[96,2048]{1,0:T(8,128)(2,1)} %collective-permute-done.10), channel_id=1, source_target_pairs={{0,8},{1,9},{2,10},{3,11},{4,12},{5,13},{6,14},{7,15},{8,0},{9,1},... | collective-permute-start | bytes 1179656 | tf_op jit(solution)/shard_map/cond/branch_1_fun/ppermute | solution.py:27
  98.5 2.3 %copy-start = (bf16[1152,2048]{1,0:T(8,128)(2,1)S(1)}, bf16[1152,2048]{1,0:T(8,128)(2,1)}, u32[]{:S(2)}) copy-start(bf16[1152,2048]{1,0:T(8,128)(2,1)} %all-gather.3.cloned.1.call-done) | copy-start | bytes 14155780
  116.1 4.2 %collective-permute-start.16 = (f32[33,24,192]{2,1,0:T(8,128)S(1)}, f32[33,24,192]{2,1,0:T(8,128)S(1)}, u32[]{:S(2)}, u32[]{:S(2)}) collective-permute-start(f32[33,24,192]{2,1,0:T(8,128)S(1)} %get-tuple-element.74), channel_id=1, source_target_pairs={{0,8},{1,9},{2,10},{3,11},{4,12},{5,13},{6,14},{7,15},{8,0},{9,1},... | collective-permute-start | bytes 1824776 | tf_op jit(solution)/shard_map/ppermute | solution.py:27
Sparse Core Ops, SparseCore 0:
  30.4 60.0 all-gather.2
